TPU v7x, 512 devices: a whole 4x4x16 slice. The times are simulated.
512 devices in a mesh: leaf: 512 (over x, y, z, core).
Axes of the slice: x: 4, y: 4, z: 16, core: 2. Of those that a mesh axis runs over, the one named last changes fastest.
Arguments:
- right_sides: float32 [16, 1048576], P(None, 'leaf'), may hold values from -6 to 6
- coordinates: bfloat16 [3, 1048576], P(None, 'leaf'), may hold values from 0 to 4
- tree_order: int32 [1048576], P('leaf'), may hold values from 0 to 2047, as said below
- leaf_basis: bfloat16 [8192, 64, 128], P('leaf'), may hold values from -0.5 to 0.5
- far_pairs: int32 [2, 65536], P(None, 'leaf'), may hold values from 0 to 15, as said below
- far_coupling: bfloat16 [65536, 64, 64], P('leaf'), may hold values from -0.25 to 0.25
- near_pairs: int32 [2, 24576], P(None, 'leaf'), may hold values from 0 to 17, as said below
- leaf_transfer: bfloat16 [8192, 64, 64], P('leaf'), may hold values from -0.25 to 0.25
- top_transfer: bfloat16 [9, 2, 64, 64], replicated, may hold values from -0.625 to 0.625
- top_coupling: bfloat16 [9, 2, 64, 64], replicated, may hold values from -0.75 to 0.75
Outputs:
- product: float32 [16, 1048576], P(None, 'leaf')
Inputs may be any that keep to these rules, and one draw needn't show every extreme that they name: `tree_order`: each subtree's block of 2048 entries is a permutation of 0 to 2047. `near_pairs`: in each subtree's block of 48 columns, row 0 names every local leaf exactly three times (values up to 15), once with itself as source (source = target + 1); row 1 values 0 and 17 each appear exactly once per block. `far_pairs`: in each subtree's block of 128 columns, every local leaf is target exactly 8 times with distinct sources, none of which is a near-field source of that target.
All inputs are finite; a program needn't handle non-finite values.
Results may differ from a plain program's by a relative error of at most 0.0031.
Values may be sent and summed in bfloat16 or wider, within the bound.
No kernel may reach another device: no remote copies, remote signals or barrier semaphores. Data moves between devices by JAX's collectives and lax.ppermute only.
A program may use at most 64 MiB of HBM per device.

v0:
```python
import jax
import jax.numpy as jnp
from jax import lax
from jax.sharding import PartitionSpec as P

HIGH = lax.Precision.HIGHEST
SQRT_THREE = 3.0**0.5
KERNEL_SCALE = 0.125


def extended(cells, sides, width):
    for axis, dim in sides:
        count = lax.axis_size(axis)
        ends = count - 1
        head = lax.slice_in_dim(cells, 0, width, axis=dim)
        tail = lax.slice_in_dim(cells, cells.shape[dim] - width, cells.shape[dim], axis=dim)
        cells = jnp.concatenate(
            [
                lax.ppermute(tail, axis, [(i, (i + 1) % count) for i in range(ends)]),
                cells,
                lax.ppermute(head, axis, [((i + 1) % count, i) for i in range(ends)]),
            ],
            axis=dim,
        )
    return cells


def matern_block(targets, sources):
    squared = jnp.zeros((targets.shape[1], targets.shape[2], sources.shape[2]), jnp.float32)
    for dimension in range(3):
        difference = targets[dimension][:, :, None] - sources[dimension][:, None, :]
        squared = squared + difference * difference
    scaled = SQRT_THREE * jnp.sqrt(squared)
    return (KERNEL_SCALE * (1.0 + scaled) * jnp.exp(-scaled)).astype(jnp.bfloat16)


def per_device(
    right_sides,
    coordinates,
    tree_order,
    leaf_basis,
    far_pairs,
    far_coupling,
    near_pairs,
    leaf_transfer,
    top_transfer,
    top_coupling,
):
    columns = right_sides.shape[0]
    leaf_count, basis_rank, leaf_size = leaf_basis.shape
    sorted_rhs = jnp.take(right_sides, tree_order, axis=1).astype(jnp.bfloat16)
    sorted_pts = jnp.take(coordinates, tree_order, axis=1)
    stacked = jnp.concatenate([sorted_rhs, sorted_pts], axis=0)
    padded = extended(stacked, (("leaf", 1),), leaf_size)
    padded = padded.reshape(columns + 3, leaf_count + 2, leaf_size)
    rhs_leaves = sorted_rhs.reshape(columns, leaf_count, leaf_size)
    leaf_coef = jnp.einsum(
        "trp,ktp->tkr", leaf_basis, rhs_leaves, preferred_element_type=jnp.float32
    )
    root_coef = jnp.einsum(
        "tcp,tkc->kp", leaf_transfer.astype(jnp.float32), leaf_coef, precision=HIGH
    )
    device = lax.axis_index("leaf")
    levels = lax.axis_size("leaf").bit_length() - 1
    siblings = []
    gathered = lax.all_gather(root_coef[None], "leaf", axis=0, tiled=True)
    coefficients = [gathered]
    for height in range(levels - 1):
        paired = coefficients[height].reshape(-1, 2, columns, basis_rank)
        left_part = jnp.einsum(
            "cp,nkc->nkp", top_transfer[height, 0].astype(jnp.float32), paired[:, 0], precision=HIGH
        )
        right_part = jnp.einsum(
            "cp,nkc->nkp", top_transfer[height, 1].astype(jnp.float32), paired[:, 1], precision=HIGH
        )
        coefficients.append(left_part + right_part)
    for height in range(levels):
        node_index = jnp.right_shift(device, height)
        siblings.append(
            lax.dynamic_index_in_dim(
                coefficients[height], jnp.bitwise_xor(node_index, 1), 0, keepdims=False
            )
        )
    field = jnp.zeros((columns, basis_rank), jnp.float32)
    for height in reversed(range(levels)):
        parity = jnp.bitwise_and(jnp.right_shift(device, height), 1)
        coupling_mat = lax.dynamic_index_in_dim(top_coupling[height], parity, 0, keepdims=False)
        transfer_mat = lax.dynamic_index_in_dim(top_transfer[height], parity, 0, keepdims=False)
        coupled = jnp.einsum(
            "ab,kb->ka", coupling_mat.astype(jnp.float32), siblings[height], precision=HIGH
        )
        inherited = jnp.einsum("cp,kp->kc", transfer_mat.astype(jnp.float32), field, precision=HIGH)
        field = coupled + inherited
    targets = jnp.take(padded[columns:], near_pairs[0] + 1, axis=1).astype(jnp.float32)
    sources = jnp.take(padded[columns:], near_pairs[1], axis=1).astype(jnp.float32)
    source_rhs = jnp.take(padded[:columns], near_pairs[1], axis=1)
    kernel = matern_block(targets, sources)
    contrib = jnp.einsum("nts,kns->knt", kernel, source_rhs, preferred_element_type=jnp.float32)
    leaf_ids = jnp.arange(leaf_count, dtype=jnp.int32)
    near_onehot = (near_pairs[0][None, :] == leaf_ids[:, None]).astype(jnp.float32)
    near_sum = jnp.einsum("ln,knt->klt", near_onehot, contrib, precision=HIGH)
    gathered_coef = jnp.take(leaf_coef, far_pairs[1], axis=0)
    far_terms = jnp.einsum(
        "nab,nkb->nka", far_coupling.astype(jnp.float32), gathered_coef, precision=HIGH
    )
    far_onehot = (far_pairs[0][None, :] == leaf_ids[:, None]).astype(jnp.float32)
    far_sum = jnp.einsum("ln,nka->lka", far_onehot, far_terms, precision=HIGH)
    leaf_field = far_sum + jnp.einsum(
        "tcp,kp->tkc", leaf_transfer.astype(jnp.float32), field, precision=HIGH
    )
    values = near_sum + jnp.einsum(
        "trp,tkr->ktp", leaf_basis.astype(jnp.float32), leaf_field, precision=HIGH
    )
    flattened = values.reshape(columns, leaf_count * leaf_size)
    return (
        jnp.zeros((columns, leaf_count * leaf_size), jnp.float32).at[:, tree_order].set(flattened)
    )


def solution(mesh):
    return jax.shard_map(
        per_device,
        mesh=mesh,
        in_specs=(
            P(None, "leaf"),
            P(None, "leaf"),
            P("leaf"),
            P("leaf", None, None),
            P(None, "leaf"),
            P("leaf", None, None),
            P(None, "leaf"),
            P("leaf", None, None),
            P(),
            P(),
        ),
        out_specs=P(None, "leaf"),
        check_vma=False,
    )
```

profile of v0, /device:TPU:1, one launch (start us, length us, event | category | flops | bytes accessed | tf_op | source)
XLA Modules:
  0.0 266.6 jit_solution(9708970037539739198)
XLA Ops:
  6.5 1.3 broadcast_clamp_fusion
  8.6 1.2 copy.171
  9.8 6.2 %gather_fusion = bf16[2048,16]{1,0:T(8,128)(2,1)S(1)} fusion(bf16[16,2048]{0,1:T(8,128)(2,1)S(1)} %copy.171, s32[2048]{0:T(1024)S(1)} %get-tuple-element.46), kind=kCustom, calls=%fused_computation.2 | custom fusion | bytes 139264 | tf_op jit(solution)/shard_map/jit(_take)/gather | solution.py:51
  16.4 1.8 convolution_bitcast_fusion.1
  19.8 6.2 %gather_fusion.1 = bf16[2048,3]{1,0:T(8,128)(2,1)S(1)} fusion(bf16[3,2048]{0,1:T(8,128)(2,1)S(1)} %copy.173, s32[2048]{0:T(1024)S(1)} %get-tuple-element.46), kind=kCustom, calls=%fused_computation.3 | custom fusion | bytes 32768 | tf_op jit(solution)/shard_map/jit(_take)/gather | solution.py:52
  27.2 4.9 %collective-permute-start = (bf16[19,128]{1,0:T(8,128)(2,1)}, bf16[19,128]{1,0:T(8,128)(2,1)}, u32[]{:S(2)}, u32[]{:S(2)}) collective-permute-start(bf16[19,128]{1,0:T(8,128)(2,1)} %get-tuple-element.44), channel_id=1, source_target_pairs={{0,1},{1,2},{2,3},{3,4},{4,5},{5,6},{6,7},{7,8},{8,9},{9,10},{10,1... | collective-permute-start | bytes 14600 | tf_op jit(solution)/shard_map/ppermute | solution.py:19
  32.1 5.7 %collective-permute-start.1 = (bf16[19,128]{1,0:T(8,128)(2,1)}, bf16[19,128]{1,0:T(8,128)(2,1)}, u32[]{:S(2)}, u32[]{:S(2)}) collective-permute-start(bf16[19,128]{1,0:T(8,128)(2,1)} %get-tuple-element.45), channel_id=1, source_target_pairs={{1,0},{2,1},{3,2},{4,3},{5,4},{6,5},{7,6},{8,7},{9,8},{10,9},{11,1... | collective-permute-start | bytes 14600 | tf_op jit(solution)/shard_map/ppermute | solution.py:21
  37.9 0.8 gather_fusion.3
  38.7 3.9 %copy.178 = bf16[128,64,64]{2,1,0:T(8,128)(2,1)S(1)} copy(bf16[128,64,64]{0,2,1:T(8,128)(2,1)} %param.17) | data formatting | bytes 2097152 | tf_op args[5]
  42.6 1.3 compare_and_fusion.1
  45.9 1.2 slice_bitcast_fusion.13
  47.1 1.2 slice_bitcast_fusion.14
  48.3 1.6 fusion.161
  50.0 1.6 fusion.160
  51.6 4.4 %fusion.8 = f32[128,16,64]{2,1,0:T(8,128)} fusion(bf16[128,64,64]{2,1,0:T(8,128)(2,1)S(1)} %copy.178, f32[128,16,64]{2,1,0:T(8,128)S(1)} %gather_fusion.3, pred[128]{0:T(512)(128)(4,1)S(1)} %compare_and_fusion.2), kind=kOutput, calls=%fused_computation.36 | convolution fusion | flops 100794368 | bytes 2097280 | tf_op jit(solution)/shard_map/nab,nkb->nka/dot_general | solution.py:103
  59.4 0.8 bitcast_convert_fusion
  60.3 5.7 %fusion.1 = f32[16,48,128]{2,0,1:T(8,128)} fusion(f32[48,128]{1,0:T(8,128)S(1)} %bitcast.335, f32[48,128]{1,0:T(8,128)S(1)} %bitcast.338, f32[48,128]{1,0:T(8,128)S(1)} %bitcast.336, f32[48,128]{1,0:T(8,128)S(1)} %bitcast.339, f32[48,128]{1,0:T(8,128)S(1)} %bitcast.334, f32[48,128]{1,0:T(8,128)S(1)} %bitcast.337, ...), kind=kOutput, calls=%fused_computation.12 | convolution fusion | flops 36274176 | bytes 737328 | tf_op jit(solution)/shard_map/nts,kns->knt/dot_general | solution.py:98
  66.0 155.9 %all-gather.3.cloned.1.call-done = f32[8192,64]{1,0:T(8,128)} async-done(((f32[16,64]{1,0:T(8,128)}), f32[8192,64]{1,0:T(8,128)}) %all-gather.3.cloned.1.call-update) | async-done | bytes 2097168 | tf_op jit(solution)/shard_map/all_gather | solution.py:66
  221.9 3.9 %fusion.156 = (f32[256,1,16,64]{3,2,1,0:T(8,128)S(1)}, f32[256,1,16,64]{3,2,1,0:T(8,128)}) fusion(f32[256,2,16,64]{3,2,1,0:T(8,128)} %bitcast.317), kind=kLoop, calls=%fused_computation.225 | loop fusion | bytes 4194304 | tf_op jit(solution)/shard_map/slice | solution.py:74
  225.8 2.5 copy.208
  228.4 2.4 fusion.5
  230.8 1.0 copy.210
  231.8 1.9 convolution_add_fusion
  233.7 1.3 copy.184
  235.0 1.6 fusion.157
  236.6 1.7 copy.212
  238.3 1.1 fusion.12
  239.8 1.1 convolution_add_fusion.2
  249.2 0.9 fusion.75
  250.2 0.8 fusion.165
  252.8 6.0 %scatter_custom_fusion = f32[16,2048]{0,1:T(8,128)S(1)} fusion(s32[2048]{0:T(1024)} %get-tuple-element.47, f32[2048,16]{1,0:T(8,128)S(1)} %bitcast.323, f32[]{:T(128)} %constant.170.clone.1), kind=kCustom, calls=%fused_computation.48 | custom fusion | bytes 131584 | tf_op jit(solution)/shard_map/scatter | solution.py:116
  258.8 1.0 copy.206
  (131 shorter events, 19.7 us)
Async XLA Ops:
  6.5 9.6 %copy-start = (bf16[16,64,128]{2,1,0:T(8,128)(2,1)S(1)}, bf16[16,64,128]{2,1,0:T(8,128)(2,1)}, u32[]{:S(2)}) copy-start(bf16[16,64,128]{2,1,0:T(8,128)(2,1)} %param.15) | copy-start | bytes 786436
  6.5 13.0 %copy-start.26 = (bf16[3,2048]{1,0:T(4,128)(2,1)S(1)}, bf16[3,2048]{1,0:T(4,128)(2,1)}, u32[]{:S(2)}) copy-start(bf16[3,2048]{1,0:T(4,128)(2,1)} %param.13) | copy-start | bytes 36868
  6.5 215.4 %all-gather.3.cloned.1.call-start = ((), (), s32[]{:S(2)}) async-start(), calls=%async_computation | async-start | bytes 4202496 | tf_op jit(solution)/shard_map/all_gather | solution.py:66
  9.8 28.1 %copy-start.29 = (s32[2,128]{1,0:T(2,128)S(1)}, s32[2,128]{1,0:T(2,128)}, u32[]{:S(2)}) copy-start(s32[2,128]{1,0:T(2,128)} %param.16) | copy-start | bytes 3076
  19.5 18.4 %copy-start.4 = (bf16[16,2048]{1,0:T(8,128)(2,1)}, bf16[16,2048]{1,0:T(8,128)(2,1)S(1)}, u32[]{:S(2)}) copy-start(bf16[16,2048]{1,0:T(8,128)(2,1)S(1)} %copy.172) | copy-start | bytes 196612
  27.2 28.8 %collective-permute-start = (bf16[19,128]{1,0:T(8,128)(2,1)}, bf16[19,128]{1,0:T(8,128)(2,1)}, u32[]{:S(2)}, u32[]{:S(2)}) collective-permute-start(bf16[19,128]{1,0:T(8,128)(2,1)} %get-tuple-element.44), channel_id=1, source_target_pairs={{0,1},{1,2},{2,3},{3,4},{4,5},{5,6},{6,7},{7,8},{8,9},{9,10},{10,1... | collective-permute-start | bytes 14600 | tf_op jit(solution)/shard_map/ppermute | solution.py:19
  32.1 23.8 %collective-permute-start.1 = (bf16[19,128]{1,0:T(8,128)(2,1)}, bf16[19,128]{1,0:T(8,128)(2,1)}, u32[]{:S(2)}, u32[]{:S(2)}) collective-permute-start(bf16[19,128]{1,0:T(8,128)(2,1)} %get-tuple-element.45), channel_id=1, source_target_pairs={{1,0},{2,1},{3,2},{4,3},{5,4},{6,5},{7,6},{8,7},{9,8},{10,9},{11,1... | collective-permute-start | bytes 14600 | tf_op jit(solution)/shard_map/ppermute | solution.py:21
  42.6 13.3 %copy-start.5 = (bf16[16,2048]{1,0:T(8,128)(2,1)S(1)}, bf16[16,2048]{1,0:T(8,128)(2,1)}, u32[]{:S(2)}) copy-start(bf16[16,2048]{1,0:T(8,128)(2,1)} %copy-done.4) | copy-start | bytes 196612
  236.6 2.8 %copy-start.2 = (f32[128,1,16,64]{3,2,1,0:T(8,128)S(1)}, f32[128,1,16,64]{3,2,1,0:T(8,128)}, u32[]{:S(2)}) copy-start(f32[128,1,16,64]{3,2,1,0:T(8,128)} %get-tuple-element.12) | copy-start | bytes 1572868
  242.4 4.2 %copy-start.25 = (bf16[1,2,64,64]{3,2,1,0:T(8,128)(2,1)S(1)}, bf16[1,2,64,64]{3,2,1,0:T(8,128)(2,1)}, u32[]{:S(2)}) copy-start(bf16[1,2,64,64]{3,2,1,0:T(8,128)(2,1)} %get-tuple-element.27) | copy-start | bytes 49156
  242.5 4.4 %copy-start.16 = (bf16[1,2,64,64]{3,2,1,0:T(8,128)(2,1)S(1)}, bf16[1,2,64,64]{3,2,1,0:T(8,128)(2,1)}, u32[]{:S(2)}) copy-start(bf16[1,2,64,64]{3,2,1,0:T(8,128)(2,1)} %get-tuple-element.22) | copy-start | bytes 49156
  242.5 4.5 %copy-start.15 = (bf16[1,2,64,64]{3,2,1,0:T(8,128)(2,1)S(1)}, bf16[1,2,64,64]{3,2,1,0:T(8,128)(2,1)}, u32[]{:S(2)}) copy-start(bf16[1,2,64,64]{3,2,1,0:T(8,128)(2,1)} %get-tuple-element.35) | copy-start | bytes 49156
  243.0 4.1 %copy-start.24 = (bf16[1,2,64,64]{3,2,1,0:T(8,128)(2,1)S(1)}, bf16[1,2,64,64]{3,2,1,0:T(8,128)(2,1)}, u32[]{:S(2)}) copy-start(bf16[1,2,64,64]{3,2,1,0:T(8,128)(2,1)} %get-tuple-element.21) | copy-start | bytes 49156
  243.0 4.3 %copy-start.14 = (bf16[1,2,64,64]{3,2,1,0:T(8,128)(2,1)S(1)}, bf16[1,2,64,64]{3,2,1,0:T(8,128)(2,1)}, u32[]{:S(2)}) copy-start(bf16[1,2,64,64]{3,2,1,0:T(8,128)(2,1)} %get-tuple-element.28) | copy-start | bytes 49156
  243.0 4.4 %copy-start.23 = (bf16[1,2,64,64]{3,2,1,0:T(8,128)(2,1)S(1)}, bf16[1,2,64,64]{3,2,1,0:T(8,128)(2,1)}, u32[]{:S(2)}) copy-start(bf16[1,2,64,64]{3,2,1,0:T(8,128)(2,1)} %get-tuple-element.20) | copy-start | bytes 49156
  243.0 4.6 %copy-start.13 = (bf16[1,2,64,64]{3,2,1,0:T(8,128)(2,1)S(1)}, bf16[1,2,64,64]{3,2,1,0:T(8,128)(2,1)}, u32[]{:S(2)}) copy-start(bf16[1,2,64,64]{3,2,1,0:T(8,128)(2,1)} %get-tuple-element.29) | copy-start | bytes 49156
  243.0 4.7 %copy-start.22 = (bf16[1,2,64,64]{3,2,1,0:T(8,128)(2,1)S(1)}, bf16[1,2,64,64]{3,2,1,0:T(8,128)(2,1)}, u32[]{:S(2)}) copy-start(bf16[1,2,64,64]{3,2,1,0:T(8,128)(2,1)} %get-tuple-element.19) | copy-start | bytes 49156
  243.0 4.9 %copy-start.12 = (bf16[1,2,64,64]{3,2,1,0:T(8,128)(2,1)S(1)}, bf16[1,2,64,64]{3,2,1,0:T(8,128)(2,1)}, u32[]{:S(2)}) copy-start(bf16[1,2,64,64]{3,2,1,0:T(8,128)(2,1)} %get-tuple-element.30) | copy-start | bytes 49156
  243.1 5.0 %copy-start.21 = (bf16[1,2,64,64]{3,2,1,0:T(8,128)(2,1)S(1)}, bf16[1,2,64,64]{3,2,1,0:T(8,128)(2,1)}, u32[]{:S(2)}) copy-start(bf16[1,2,64,64]{3,2,1,0:T(8,128)(2,1)} %get-tuple-element.23) | copy-start | bytes 49156
  243.1 5.2 %copy-start.11 = (bf16[1,2,64,64]{3,2,1,0:T(8,128)(2,1)S(1)}, bf16[1,2,64,64]{3,2,1,0:T(8,128)(2,1)}, u32[]{:S(2)}) copy-start(bf16[1,2,64,64]{3,2,1,0:T(8,128)(2,1)} %get-tuple-element.31) | copy-start | bytes 49156
  243.1 5.3 %copy-start.20 = (bf16[1,2,64,64]{3,2,1,0:T(8,128)(2,1)S(1)}, bf16[1,2,64,64]{3,2,1,0:T(8,128)(2,1)}, u32[]{:S(2)}) copy-start(bf16[1,2,64,64]{3,2,1,0:T(8,128)(2,1)} %get-tuple-element.24) | copy-start | bytes 49156
  243.1 5.5 %copy-start.10 = (bf16[1,2,64,64]{3,2,1,0:T(8,128)(2,1)S(1)}, bf16[1,2,64,64]{3,2,1,0:T(8,128)(2,1)}, u32[]{:S(2)}) copy-start(bf16[1,2,64,64]{3,2,1,0:T(8,128)(2,1)} %get-tuple-element.32) | copy-start | bytes 49156
  243.1 5.6 %copy-start.19 = (bf16[1,2,64,64]{3,2,1,0:T(8,128)(2,1)S(1)}, bf16[1,2,64,64]{3,2,1,0:T(8,128)(2,1)}, u32[]{:S(2)}) copy-start(bf16[1,2,64,64]{3,2,1,0:T(8,128)(2,1)} %get-tuple-element.25) | copy-start | bytes 49156
  243.1 5.8 %copy-start.9 = (bf16[1,2,64,64]{3,2,1,0:T(8,128)(2,1)S(1)}, bf16[1,2,64,64]{3,2,1,0:T(8,128)(2,1)}, u32[]{:S(2)}) copy-start(bf16[1,2,64,64]{3,2,1,0:T(8,128)(2,1)} %get-tuple-element.33) | copy-start | bytes 49156
  243.1 5.9 %copy-start.18 = (bf16[1,2,64,64]{3,2,1,0:T(8,128)(2,1)S(1)}, bf16[1,2,64,64]{3,2,1,0:T(8,128)(2,1)}, u32[]{:S(2)}) copy-start(bf16[1,2,64,64]{3,2,1,0:T(8,128)(2,1)} %get-tuple-element.26) | copy-start | bytes 49156
  243.1 6.1 %copy-start.8 = (bf16[1,2,64,64]{3,2,1,0:T(8,128)(2,1)S(1)}, bf16[1,2,64,64]{3,2,1,0:T(8,128)(2,1)}, u32[]{:S(2)}) copy-start(bf16[1,2,64,64]{3,2,1,0:T(8,128)(2,1)} %get-tuple-element.34) | copy-start | bytes 49156
  243.1 6.9 %copy-start.17 = (bf16[1,2,64,64]{3,2,1,0:T(8,128)(2,1)S(1)}, bf16[1,2,64,64]{3,2,1,0:T(8,128)(2,1)}, u32[]{:S(2)}) copy-start(bf16[1,2,64,64]{3,2,1,0:T(8,128)(2,1)} %get-tuple-element.18) | copy-start | bytes 49156
  243.1 7.1 %copy-start.6 = (bf16[16,64,64]{2,1,0:T(8,128)(2,1)S(1)}, bf16[16,64,64]{2,1,0:T(8,128)(2,1)}, u32[]{:S(2)}) copy-start(bf16[16,64,64]{2,1,0:T(8,128)(2,1)} %param.19) | copy-start | bytes 393220
  243.2 7.8 %copy-start.1 = (f32[128,16,64]{2,1,0:T(8,128)S(1)}, f32[128,16,64]{2,1,0:T(8,128)}, u32[]{:S(2)}) copy-start(f32[128,16,64]{2,1,0:T(8,128)} %fusion.8) | copy-start | bytes 1572868
  243.2 7.8 %copy-start.27 = (s32[128]{0:T(128)S(1)}, s32[128]{0:T(128)}, u32[]{:S(2)}) copy-start(s32[128]{0:T(128)} %slice_bitcast_fusion.13) | copy-start | bytes 1540
  244.3 7.8 %copy-start.7 = (f32[16,48,128]{2,0,1:T(8,128)S(1)}, f32[16,48,128]{2,0,1:T(8,128)}, u32[]{:S(2)}) copy-start(f32[16,48,128]{2,0,1:T(8,128)} %fusion.1) | copy-start | bytes 1179652
  244.3 7.8 %copy-start.28 = (s32[48]{0:T(128)S(1)}, s32[48]{0:T(128)}, u32[]{:S(2)}) copy-start(s32[48]{0:T(128)} %slice_bitcast_fusion.14) | copy-start | bytes 580
  (1 other events, 1.0 us)
Sparse Core Ops, SparseCore 0:
  18.4 203.4 all-gather.2
where the time goes:
time: 268 us; the launch traced here: 267 us
  waiting for transfers between devices  156 us (58%)
  local copies, waits for them, and re-layouts  49.3 us (18%)
  matrix products  27.2 us (10%)
  between operations  14 us (5%)
  starting transfers between devices  10.6 us (4%)
  other arithmetic  9.52 us (4%)
    all_gather x1, waiting for transfers between devices, per_device(): gathered = lax.all_gather(root_coef[None], 'leaf', axis=0, tiled=True)  156 us
    unnamed x67, local copies, waits for them, and re-layouts  11.6 us
    scatter x2, local copies, waits for them, and re-layouts, per_device(): jnp.zeros((columns, leaf_count * leaf_size), jnp.float32).at[:, tree_order]  6.93 us
    gather x2, local copies, waits for them, and re-layouts, per_device(): sorted_rhs = jnp.take(right_sides, tree_order, axis=1).astype(jnp.bfloat16)  6.37 us
    slice x5, local copies, waits for them, and re-layouts, per_device(): paired[:, 1]  6.31 us
    gather x1, local copies, waits for them, and re-layouts, per_device(): sorted_pts = jnp.take(coordinates, tree_order, axis=1)  6.18 us
    ppermute x1, starting transfers between devices, extended(): lax.ppermute(head, axis, [((i + 1) % count, i) for i in range(ends)])  5.72 us
    dot_general x1, matrix products, per_device(): jnp.einsum('nts,kns->knt', kernel, source_rhs, preferred_element_type=jnp...  5.69 us
  transfers between devices with their start and end apart: 3, of which 1 were waited for; matrix products, arithmetic and copies ran while one was open for 14% of the time, Pallas kernels for 0%

commit v1 on v0

v1 whole, which is shorter than its diff:
```python
import jax
import jax.numpy as jnp
from jax import lax
from jax.experimental import pallas as pl
from jax.experimental.pallas import tpu as pltpu
from jax.sharding import PartitionSpec as P

BF = jnp.bfloat16
F32 = jnp.float32
LEAF = 128
RANK = 64
COLS = 16
LEAVES = 16
PTS = LEAVES * LEAF
LOW = 5
HIGHS = 4
NLOW = 1 << LOW
NHIGH = 1 << HIGHS
VMEM = pl.BlockSpec(memory_space=pltpu.VMEM)
SMEM = pl.BlockSpec(memory_space=pltpu.SMEM)
ANY = pl.BlockSpec(memory_space=pl.ANY)


def halves(x):
    hi = x.astype(BF)
    return hi, (x - hi.astype(F32)).astype(BF)


def mm(a, b):
    return jnp.dot(a, b, preferred_element_type=F32)


def mm_nt(a, b):
    return lax.dot_general(a, b, (((1,), (1,)), ((), ())), preferred_element_type=F32)


def wide(a, b):
    ah, al = halves(a)
    bh, bl = halves(b)
    return mm(ah, bh) + (mm(ah, bl) + mm(al, bh))


def wide_nt(a, b):
    ah, al = halves(a)
    bh, bl = halves(b)
    return mm_nt(ah, bh) + (mm_nt(ah, bl) + mm_nt(al, bh))


def low_onehot(order):
    lane = jnp.bitwise_and(order, LEAF - 1)
    rows = lax.broadcasted_iota(jnp.int32, (LEAF, order.shape[1]), 0)
    return jnp.where(rows == lane, 1.0, 0.0).astype(BF)


def permuted(x, order, width):
    stacked = jnp.concatenate([x[:, h * LEAF : (h + 1) * LEAF] for h in range(LEAVES)], axis=0)
    rows = x.shape[0]
    for start in range(0, order.shape[1], width):
        piece = order[:, start : start + width]
        picked = mm(stacked, low_onehot(piece))
        block = jnp.right_shift(piece, 7)
        total = jnp.zeros((rows, width), F32)
        for h in range(LEAVES):
            total = total + jnp.where(block == h, picked[h * rows : (h + 1) * rows], 0.0)
        yield start, total.astype(BF)


def pack_message(x):
    return jnp.concatenate([x[:8], x[8:]], axis=1)


def up_kernel(rhs_ref, order_ref, basis_ref, transfer_ref, sorted_ref, coef_ref, message_ref):
    x = rhs_ref[...].astype(BF)
    order = order_ref[...]
    root = jnp.zeros((2 * COLS, RANK), F32)
    for start, piece in permuted(x, order, 2 * LEAF):
        sorted_ref[:, start : start + 2 * LEAF] = piece
        for i in range(2):
            n = start // LEAF + i
            coef = mm_nt(piece[:, i * LEAF : (i + 1) * LEAF], basis_ref[n])
            hi, lo = halves(coef)
            both = jnp.concatenate([hi, lo], axis=0)
            coef_ref[n] = both
            root = root + mm(both, transfer_ref[n])
    message = pack_message(root[:COLS] + root[COLS:]).astype(BF)
    message_ref[...] = jnp.broadcast_to(message[None], message_ref.shape)


def points_kernel(coords_ref, order_ref, sorted_ref, head_ref, tail_ref, points_ref):
    x = jnp.concatenate([coords_ref[...], jnp.zeros((13, PTS), BF)], axis=0)
    for start, piece in permuted(x, order_ref[...], 2 * LEAF):
        points_ref[:, start : start + 2 * LEAF] = piece
    head_ref[0:COLS] = sorted_ref[:, 0:LEAF]
    head_ref[COLS:] = points_ref[:, 0:LEAF]
    tail_ref[0:COLS] = sorted_ref[:, PTS - LEAF :]
    tail_ref[COLS:] = points_ref[:, PTS - LEAF :]


def far_kernel(pairs_ref, coef_ref, coupling_ref, basis_ref, out_ref, acc):
    acc[...] = jnp.zeros_like(acc)
    for j in range(LEAVES * 8):
        target, source = pairs_ref[0, j], pairs_ref[1, j]
        acc[target] += mm_nt(coef_ref[source], coupling_ref[j])
    for n in range(LEAVES):
        total = acc[n]
        hi, lo = halves(total[:COLS] + total[COLS:])
        both = mm(jnp.concatenate([hi, lo], axis=0), basis_ref[n])
        out_ref[:, n * LEAF : (n + 1) * LEAF] = both[:COLS] + both[COLS:]


def point_features(points):
    p = points.astype(F32)
    x, y, z = p[0:1], p[1:2], p[2:3]
    square = x * x + y * y + z * z
    s0 = square.astype(BF).astype(F32)
    rest = square - s0
    s1 = rest.astype(BF).astype(F32)
    s2 = rest - s1
    one = jnp.ones_like(square)
    zero = jnp.zeros((7, LEAF), F32)
    source = jnp.concatenate([x, y, z, one, one, one, s0, s1, s2, zero], axis=0)
    target = jnp.concatenate(
        [-2.0 * x, -2.0 * y, -2.0 * z, s0, s1, s2, one, one, one, zero], axis=0
    )
    return source, target


def near_kernel(
    pairs_ref, sorted_ref, points_ref, left_ref, right_ref, far_ref, after_ref, out_ref, rhs, source, target, acc
):
    del after_ref
    for n in range(LEAVES + 2):
        if n == 0:
            columns, points = left_ref[0:COLS], left_ref[COLS:]
        elif n == LEAVES + 1:
            columns, points = right_ref[0:COLS], right_ref[COLS:]
        else:
            here = slice((n - 1) * LEAF, n * LEAF)
            columns, points = sorted_ref[:, here], points_ref[:, here]
        rhs[n] = columns
        of_source, of_target = point_features(points)
        source[n] = of_source.T.astype(BF)
        target[n] = of_target.astype(BF)
    for n in range(LEAVES):
        acc[n] = far_ref[:, n * LEAF : (n + 1) * LEAF]

    for j in range(LEAVES * 3):
        to, of = pairs_ref[0, j], pairs_ref[1, j]
        squared = jnp.maximum(mm(source[of], target[to + 1]), 0.0)
        scaled = jnp.sqrt(3.0 * squared)
        values = ((0.125 + 0.125 * scaled) * jnp.exp(-scaled)).astype(BF)
        acc[to] += mm(rhs[of], values)
    for n in range(LEAVES):
        out_ref[:, n * LEAF : (n + 1) * LEAF] = acc[n]


def chains(transfer_ref, first, count, tree):
    for h in range(count):
        size = 1 << h
        for side in range(2):
            step = transfer_ref[first + h, side].astype(F32)
            if h == 0:
                tree[0][side] = step
            else:
                rows = tree[h - 1][...].reshape(size * RANK, RANK)
                hi, lo = halves(rows)
                step = step.astype(BF)
                tree[h][side * size : (side + 1) * size] = (mm(hi, step) + mm(lo, step)).reshape(
                    size, RANK, RANK
                )


def weights_kernel(device_ref, transfer_ref, coupling_ref, low_ref, high_ref, *tree):
    device = device_ref[0]
    low_tree, high_tree = tree[:LOW], tree[LOW:]
    chains(transfer_ref, 0, LOW, low_tree)
    chains(transfer_ref, LOW, HIGHS, high_tree)

    def own(index, count, branch):
        return branch[count - 1][jnp.bitwise_and(index, (1 << count) - 1)]

    def store(ref, at, count, lane, value):
        hi, lo = halves(value)
        ref[pl.ds(at, count), :, lane : lane + RANK] = hi.reshape(count, RANK, RANK)
        ref[pl.ds(at, count), :, lane + 2 * RANK : lane + 3 * RANK] = lo.reshape(count, RANK, RANK)

    low = jnp.bitwise_and(device, NLOW - 1)
    store(low_ref, 0, NLOW, 0, low_tree[LOW - 1][...].reshape(NLOW * RANK, RANK))
    store(low_ref, low, 1, RANK, jnp.zeros((RANK, RANK), F32))
    for h in range(LOW):
        node = jnp.right_shift(low, h)
        coupling = coupling_ref[h, jnp.bitwise_and(node, 1)]
        at = jnp.left_shift(jnp.bitwise_xor(node, 1), h)
        if h == 0:
            value = coupling.astype(F32).T
        else:
            hi, lo = halves(own(low, h, low_tree))
            end = mm(hi, coupling) + mm(lo, coupling)
            value = wide_nt(low_tree[h - 1][...].reshape(-1, RANK), end)
        store(low_ref, at, 1 << h, RANK, value)

    high = jnp.right_shift(device, LOW)
    high_ref[pl.ds(high, 1)] = jnp.zeros((1, RANK, 2 * RANK), BF)
    bottom = own(low, LOW, low_tree)
    for h in range(HIGHS):
        node = jnp.right_shift(high, h)
        coupling = coupling_ref[LOW + h, jnp.bitwise_and(node, 1)]
        at = jnp.left_shift(jnp.bitwise_xor(node, 1), h)
        path = bottom if h == 0 else wide(bottom, own(high, h, high_tree))
        hi, lo = halves(path)
        end = mm(hi, coupling) + mm(lo, coupling)
        value = end.T if h == 0 else wide_nt(high_tree[h - 1][...].reshape(-1, RANK), end)
        hi, lo = halves(value)
        high_ref[pl.ds(at, 1 << h), :, 0:RANK] = hi.reshape(-1, RANK, RANK)
        high_ref[pl.ds(at, 1 << h), :, RANK : 2 * RANK] = lo.reshape(-1, RANK, RANK)


def unpacked(message):
    return jnp.concatenate([message[:, :RANK], message[:, RANK:]], axis=0)


def middle_kernel(received_ref, weight_ref, message_ref, field_ref):
    total = jnp.zeros((COLS, 4 * RANK), F32)
    for s in range(NLOW):
        total = total + mm(unpacked(received_ref[s]), weight_ref[s])
    total = total[:, : 2 * RANK] + total[:, 2 * RANK :]
    field_ref[...] = total[:, RANK:]
    message_ref[...] = jnp.broadcast_to(pack_message(total[:, :RANK])[None], message_ref.shape)


def down_kernel(
    received_ref, weight_ref, field_ref, partial_ref, transfer_ref, basis_ref, order_ref, out_ref
):
    total = jnp.zeros((2 * COLS, 2 * RANK), F32)
    for g in range(NHIGH):
        hi, lo = halves(unpacked(received_ref[g]))
        total = total + mm(jnp.concatenate([hi, lo], axis=0), weight_ref[g])
    total = total[:COLS] + total[COLS:]
    field = field_ref[...] + (total[:, :RANK] + total[:, RANK:])
    hi, lo = halves(field)
    field = jnp.concatenate([hi, lo], axis=0)
    result = [jnp.zeros((COLS, LEAF), F32) for _ in range(LEAVES)]
    result = jnp.zeros((LEAVES * 2 * COLS, LEAF), F32)
    order = order_ref[...]
    for start in range(0, PTS, 2 * LEAF):
        pieces = []
        for n in range(start // LEAF, start // LEAF + 2):
            leaf_field = mm_nt(field, transfer_ref[n])
            hi, lo = halves(leaf_field[:COLS] + leaf_field[COLS:])
            both = mm(jnp.concatenate([hi, lo], axis=0), basis_ref[n])
            pieces.append(both[:COLS] + both[COLS:])
        values = jnp.concatenate(pieces, axis=1) + partial_ref[:, start : start + 2 * LEAF]
        hi, lo = halves(values)
        both = jnp.concatenate([hi, lo], axis=0)
        piece = order[:, start : start + 2 * LEAF]
        block = jnp.right_shift(piece, 7)
        masked = jnp.concatenate(
            [both * jnp.where(block == h, 1.0, 0.0).astype(BF) for h in range(LEAVES)], axis=0
        )
        result = result + mm_nt(masked, low_onehot(piece))
    for h in range(LEAVES):
        at = h * 2 * COLS
        out_ref[:, h * LEAF : (h + 1) * LEAF] = result[at : at + COLS] + result[at + COLS : at + 2 * COLS]


def call(kernel, out, specs, args, scratch=(), flops=0, transcendentals=0, moved=1 << 20):
    shapes = [jax.ShapeDtypeStruct(s, t) for s, t in out]
    result = pl.pallas_call(
        kernel,
        out_shape=shapes,
        in_specs=specs,
        out_specs=[VMEM] * len(out),
        scratch_shapes=list(scratch),
        compiler_params=pltpu.CompilerParams(vmem_limit_bytes=40 << 20),
        cost_estimate=pl.CostEstimate(
            flops=flops, bytes_accessed=moved, transcendentals=transcendentals
        ),
    )(*args)
    return result


def per_device(
    right_sides,
    coordinates,
    tree_order,
    leaf_basis,
    far_pairs,
    far_coupling,
    near_pairs,
    leaf_transfer,
    top_transfer,
    top_coupling,
):
    count = lax.axis_size("leaf")
    device = lax.axis_index("leaf").astype(jnp.int32).reshape(1)
    order = tree_order.reshape(1, PTS)
    sorted_rhs, coef, message = call(
        up_kernel,
        [((COLS, PTS), BF), ((LEAVES, 2 * COLS, RANK), BF), ((NLOW, 8, 2 * RANK), BF)],
        [VMEM] * 4,
        (right_sides, order, leaf_basis, leaf_transfer),
        flops=1 << 28,
    )
    low_groups = [[g * NLOW + s for s in range(NLOW)] for g in range(NHIGH)]
    high_groups = [[g * NLOW + s for g in range(NHIGH)] for s in range(NLOW)]
    received = lax.all_to_all(message, "leaf", 0, 0, axis_index_groups=low_groups, tiled=True)

    head, tail, points = call(
        points_kernel,
        [((2 * COLS, LEAF), BF), ((2 * COLS, LEAF), BF), ((COLS, PTS), BF)],
        [VMEM] * 3,
        (coordinates, order, sorted_rhs),
        flops=1 << 30,
    )
    left = lax.ppermute(tail, "leaf", [(i, i + 1) for i in range(count - 1)])
    right = lax.ppermute(head, "leaf", [(i + 1, i) for i in range(count - 1)])
    low_weight, high_weight = call(
        weights_kernel,
        [((NLOW, RANK, 4 * RANK), BF), ((NHIGH, RANK, 2 * RANK), BF)],
        [SMEM, VMEM, VMEM],
        (device, top_transfer, top_coupling),
        scratch=[pltpu.VMEM((2 << h, RANK, RANK), F32) for h in range(LOW)]
        + [pltpu.VMEM((2 << h, RANK, RANK), F32) for h in range(HIGHS)],
        flops=1 << 31,
    )
    (far,) = call(
        far_kernel,
        [((COLS, PTS), F32)],
        [SMEM, VMEM, VMEM, VMEM],
        (far_pairs, coef, far_coupling, leaf_basis),
        scratch=[pltpu.VMEM((LEAVES, 2 * COLS, RANK), F32)],
        flops=1 << 31,
    )
    message, field = call(
        middle_kernel,
        [((NHIGH, 8, 2 * RANK), F32), ((COLS, RANK), F32)],
        [VMEM] * 2,
        (received, low_weight),
        flops=1 << 27,
    )
    received = lax.all_to_all(message, "leaf", 0, 0, axis_index_groups=high_groups, tiled=True)
    (partial,) = call(
        near_kernel,
        [((COLS, PTS), F32)],
        [SMEM] + [VMEM] * 5 + [ANY],
        (near_pairs, sorted_rhs, points, left, right, far, field),
        scratch=[
            pltpu.VMEM((LEAVES + 2, COLS, LEAF), BF),
            pltpu.VMEM((LEAVES + 2, LEAF, COLS), BF),
            pltpu.VMEM((LEAVES + 2, COLS, LEAF), BF),
            pltpu.VMEM((LEAVES, COLS, LEAF), F32),
        ],
        flops=1 << 32,
        transcendentals=1 << 21,
    )
    (product,) = call(
        down_kernel,
        [((COLS, PTS), F32)],
        [VMEM] * 7,
        (received, high_weight, field, partial, leaf_transfer, leaf_basis, order),
        flops=1 << 28,
    )
    return product


def solution(mesh):
    return jax.shard_map(
        per_device,
        mesh=mesh,
        in_specs=(
            P(None, "leaf"),
            P(None, "leaf"),
            P("leaf"),
            P("leaf", None, None),
            P(None, "leaf"),
            P("leaf", None, None),
            P(None, "leaf"),
            P("leaf", None, None),
            P(),
            P(),
        ),
        out_specs=P(None, "leaf"),
        check_vma=False,
    )
```

time: 268 us -> 64.5 us (0.24)
  the two profiles are of different devices: /device:TPU:1 before, /device:TPU:2 now
where the time goes in v1:
time: 64.5 us; the launch traced here: 63.9 us
  starting transfers between devices  30.6 us (47%)
  Pallas kernels  17.1 us (27%)
  local copies, waits for them, and re-layouts  15 us (23%)
  waiting for transfers between devices  1 us (2%)
    pallas_call x7, Pallas kernels, call(): pl.pallas_call(kernel, out_shape=shapes, in_specs=specs, out_specs=[VMEM]...  17.1 us
    all_to_all x1, starting transfers between devices, per_device(): lax.all_to_all(message, 'leaf', 0, 0, axis_index_groups=low_groups, tiled...  15.5 us
    unnamed x47, local copies, waits for them, and re-layouts  15 us
    ppermute x1, starting transfers between devices, per_device(): right = lax.ppermute(head, 'leaf', [(i + 1, i) for i in range(count - 1)])  7.6 us
    all_to_all x1, starting transfers between devices, per_device(): lax.all_to_all(message, 'leaf', 0, 0, axis_index_groups=high_groups, tile...  5.37 us
    ppermute x1, starting transfers between devices, per_device(): left = lax.ppermute(tail, 'leaf', [(i, i + 1) for i in range(count - 1)])  2.17 us
  transfers between devices with their start and end apart: 4, of which 1 were waited for; matrix products, arithmetic and copies ran while one was open for 6% of the time, Pallas kernels for 15%

profile of v1, /device:TPU:2, one launch (start us, length us, event | category | flops | bytes accessed | tf_op | source)
XLA Modules:
  0.0 63.9 jit_solution(3007564150271820311)
XLA Ops:
  0.0 0.9 %copy-done = bf16[16,64,128]{2,1,0:T(8,128)(2,1)S(1)} copy-done((bf16[16,64,128]{2,1,0:T(8,128)(2,1)S(1)}, bf16[16,64,128]{2,1,0:T(8,128)(2,1)}, u32[]{:S(2)}) %copy-start) | copy-done | bytes 262168
  1.0 0.9 %copy-done.2 = bf16[16,64,64]{2,1,0:T(8,128)(2,1)S(1)} copy-done((bf16[16,64,64]{2,1,0:T(8,128)(2,1)S(1)}, bf16[16,64,64]{2,1,0:T(8,128)(2,1)}, u32[]{:S(2)}) %copy-start.2) | copy-done | bytes 131096
  1.9 0.7 %copy-done.6 = s32[2048]{0:T(1024)S(1)} copy-done((s32[2048]{0:T(1024)S(1)}, s32[2048]{0:T(1024)}, u32[]{:S(2)}) %copy-start.6) | copy-done | bytes 8216
  2.6 0.9 %copy-done.11 = f32[16,2048]{1,0:T(8,128)S(1)} copy-done((f32[16,2048]{1,0:T(8,128)S(1)}, f32[16,2048]{1,0:T(8,128)}, u32[]{:S(2)}) %copy-start.11) | copy-done | bytes 131096
  3.5 3.1 %shard_map.100 = (bf16[16,2048]{1,0:T(8,128)(2,1)S(1)}, bf16[16,32,64]{2,1,0:T(8,128)(2,1)S(1)}, bf16[32,8,128]{2,1,0:T(8,128)(2,1)}) custom-call(f32[16,2048]{1,0:T(8,128)S(1)} %copy-done.11, s32[1,2048]{1,0:T(1,128)S(1)} %bitcast.2, bf16[16,64,128]{2,1,0:T(8,128)(2,1)S(1)} %copy-done, bf16[16,64,64]{2,1,0:T(8,128)(2,1)S(1)} %copy-done.2), custom_call_target="tpu_custom_call" | custom-call | flops 268435456 | bytes 1048576 | tf_op jit(solution)/shard_map/pallas_call | solution.py:268
  6.6 0.7 %copy-done.15 = bf16[16,32,64]{2,1,0:T(8,128)(2,1)} copy-done((bf16[16,32,64]{2,1,0:T(8,128)(2,1)}, bf16[16,32,64]{2,1,0:T(8,128)(2,1)S(1)}, u32[]{:S(2)}) %copy-start.15) | copy-done | bytes 65560
  7.3 15.5 %all-to-all-start = ((bf16[32,8,128]{2,1,0:T(8,128)(2,1)}), bf16[32,8,128]{2,1,0:T(8,128)(2,1)S(1)}, u32[]{:S(2)}, u32[]{:S(2)}) async-start(bf16[32,8,128]{2,1,0:T(8,128)(2,1)} %get-tuple-element.15), calls=%async_computation | async-start | bytes 131072 | tf_op jit(solution)/shard_map/all_to_all | solution.py:306
  22.8 0.0 copy-start.7
  22.8 0.7 %copy-done.7 = s32[2048]{0:T(1024)S(1)} copy-done((s32[2048]{0:T(1024)S(1)}, s32[2048]{0:T(1024)}, u32[]{:S(2)}) %copy-start.7) | copy-done | bytes 8216
  23.5 0.7 %copy-done.12 = bf16[3,2048]{1,0:T(4,128)(2,1)S(1)} copy-done((bf16[3,2048]{1,0:T(4,128)(2,1)S(1)}, bf16[3,2048]{1,0:T(4,128)(2,1)}, u32[]{:S(2)}) %copy-start.12) | copy-done | bytes 12312
  24.2 0.5 shard_map.103
  24.7 0.6 copy-done.21
  25.3 2.2 %collective-permute-start = (bf16[32,128]{1,0:T(8,128)(2,1)S(1)}, bf16[32,128]{1,0:T(8,128)(2,1)S(1)}, u32[]{:S(2)}, u32[]{:S(2)}) collective-permute-start(bf16[32,128]{1,0:T(8,128)(2,1)S(1)} %get-tuple-element.22), channel_id=1, source_target_pairs={{0,1},{1,2},{2,3},{3,4},{4,5},{5,6},{6,7},{7,8},{8,9},{9,10},{10,1... | collective-permute-start | bytes 24584 | tf_op jit(solution)/shard_map/ppermute | solution.py:315
  27.5 7.6 %collective-permute-start.1 = (bf16[32,128]{1,0:T(8,128)(2,1)S(1)}, bf16[32,128]{1,0:T(8,128)(2,1)S(1)}, u32[]{:S(2)}, u32[]{:S(2)}) collective-permute-start(bf16[32,128]{1,0:T(8,128)(2,1)S(1)} %get-tuple-element.23), channel_id=1, source_target_pairs={{1,0},{2,1},{3,2},{4,3},{5,4},{6,5},{7,6},{8,7},{9,8},{10,9},{11,1... | collective-permute-start | bytes 24584 | tf_op jit(solution)/shard_map/ppermute | solution.py:316
  35.1 3.5 %shard_map.101 = (bf16[32,64,256]{2,1,0:T(8,128)(2,1)S(1)}, bf16[16,64,128]{2,1,0:T(8,128)(2,1)S(1)}) custom-call(s32[1]{0:T(128)} %bitcast.1.device_ref, bf16[9,2,64,64]{3,2,1,0:T(8,128)(2,1)S(1)} %copy-done.9, bf16[9,2,64,64]{3,2,1,0:T(8,128)(2,1)S(1)} %copy-done.10), custom_call_target="tpu_custom_call" | custom-call | flops 2147483648 | bytes 1048576 | tf_op jit(solution)/shard_map/pallas_call | solution.py:268
  38.6 0.7 %copy-done.4 = bf16[16,64,128]{2,1,0:T(8,128)(2,1)} copy-done((bf16[16,64,128]{2,1,0:T(8,128)(2,1)}, bf16[16,64,128]{2,1,0:T(8,128)(2,1)S(1)}, u32[]{:S(2)}) %copy-start.4) | copy-done | bytes 262168
  39.3 4.0 %copy.11.coupling_ref = bf16[128,64,64]{2,1,0:T(8,128)(2,1)S(1)} copy(bf16[128,64,64]{0,2,1:T(8,128)(2,1)} %param.15) | data formatting | bytes 2097152 | tf_op args[5]
  43.3 0.0 copy-start.16
  43.3 0.9 %copy-done.16 = bf16[16,32,64]{2,1,0:T(8,128)(2,1)S(1)} copy-done((bf16[16,32,64]{2,1,0:T(8,128)(2,1)S(1)}, bf16[16,32,64]{2,1,0:T(8,128)(2,1)}, u32[]{:S(2)}) %copy-start.16) | copy-done | bytes 65560
  44.2 2.0 %shard_map.104.far_ref = f32[16,2048]{1,0:T(8,128)S(1)} custom-call(s32[2,128]{1,0:T(2,128)S(1)} %copy-done.13, bf16[16,32,64]{2,1,0:T(8,128)(2,1)S(1)} %copy-done.16, bf16[128,64,64]{2,1,0:T(8,128)(2,1)S(1)} %copy.11.coupling_ref, bf16[16,64,128]{2,1,0:T(8,128)(2,1)S(1)} %copy-done.1), custom_call_target="tpu_custom_call" | custom-call | flops 2147483648 | bytes 1048576 | tf_op jit(solution)/shard_map/pallas_call | solution.py:268
  46.2 0.0 copy-start.19
  46.3 0.6 %copy-done.19 = f32[16,2048]{1,0:T(8,128)} copy-done((f32[16,2048]{1,0:T(8,128)}, f32[16,2048]{1,0:T(8,128)S(1)}, u32[]{:S(2)}) %copy-start.19) | copy-done | bytes 131096
  46.9 0.0 all-to-all-done.received_ref
  46.9 1.0 %shard_map.102 = (f32[16,8,128]{2,1,0:T(8,128)}, f32[16,64]{1,0:T(8,128)S(1)}) custom-call(bf16[32,8,128]{2,1,0:T(8,128)(2,1)S(1)} %all-to-all-done.received_ref, bf16[32,64,256]{2,1,0:T(8,128)(2,1)S(1)} %get-tuple-element.16.weight_ref), custom_call_target="tpu_custom_call" | custom-call | flops 134217728 | bytes 1048576 | tf_op jit(solution)/shard_map/pallas_call | solution.py:268
  47.9 5.4 %all-to-all-start.1 = ((f32[16,8,128]{2,1,0:T(8,128)}), f32[16,8,128]{2,1,0:T(8,128)S(1)}, u32[]{:S(2)}, u32[]{:S(2)}) async-start(f32[16,8,128]{2,1,0:T(8,128)} %get-tuple-element.17), calls=%async_computation.1 | async-start | bytes 131072 | tf_op jit(solution)/shard_map/all_to_all | solution.py:341
  53.3 0.0 collective-permute-done.1.right_ref
  53.3 0.8 %copy-done.18 = bf16[16,2048]{1,0:T(8,128)(2,1)S(1)} copy-done((bf16[16,2048]{1,0:T(8,128)(2,1)S(1)}, bf16[16,2048]{1,0:T(8,128)(2,1)}, u32[]{:S(2)}) %copy-start.18) | copy-done | bytes 65560
  54.2 0.9 %copy-done.20 = f32[16,2048]{1,0:T(8,128)S(1)} copy-done((f32[16,2048]{1,0:T(8,128)S(1)}, f32[16,2048]{1,0:T(8,128)}, u32[]{:S(2)}) %copy-start.20) | copy-done | bytes 131096
  55.1 0.8 %copy-done.22 = bf16[16,2048]{1,0:T(8,128)(2,1)S(1)} copy-done((bf16[16,2048]{1,0:T(8,128)(2,1)S(1)}, bf16[16,2048]{1,0:T(8,128)(2,1)}, u32[]{:S(2)}) %copy-start.22) | copy-done | bytes 65560
  55.9 2.6 %shard_map.105.partial_ref = f32[16,2048]{1,0:T(8,128)S(1)} custom-call(s32[2,48]{1,0:T(2,128)S(1)} %copy-done.14, bf16[16,2048]{1,0:T(8,128)(2,1)S(1)} %copy-done.18, bf16[16,2048]{1,0:T(8,128)(2,1)S(1)} %copy-done.22, bf16[32,128]{1,0:T(8,128)(2,1)S(1)} %collective-permute-done.left_ref, bf16[32,128]{1,0:T(8,128)(2,1)S(1)} %collective-permute-done.1.right_ref, ...), custom_call_target="tpu_custom_call" | custom-call | flops 4294967296 | bytes 1048576 | tf_op jit(solution)/shard_map/pallas_call | solution.py:268
  58.6 1.0 %all-to-all-done.1.received_ref = f32[16,8,128]{2,1,0:T(8,128)S(1)} async-done(((f32[16,8,128]{2,1,0:T(8,128)}), f32[16,8,128]{2,1,0:T(8,128)S(1)}, u32[]{:S(2)}, u32[]{:S(2)}) %all-to-all-start.1) | async-done | bytes 65568 | tf_op jit(solution)/shard_map/all_to_all | solution.py:341
  59.6 4.3 %shard_map.106 = f32[16,2048]{1,0:T(8,128)} custom-call(f32[16,8,128]{2,1,0:T(8,128)S(1)} %all-to-all-done.1.received_ref, bf16[16,64,128]{2,1,0:T(8,128)(2,1)S(1)} %copy-done.5, f32[16,64]{1,0:T(8,128)S(1)} %get-tuple-element.19.after_ref.field_ref, f32[16,2048]{1,0:T(8,128)S(1)} %shard_map.105.partial_ref, bf16[16,64,64]{2,1,0:T(8,128)(2,1)S(1)} %copy-done.3, ...), custom_call_target="tpu_custom_call" | custom-call | flops 268435456 | bytes 1048576 | tf_op jit(solution)/shard_map/pallas_call | solution.py:268
  (30 shorter events, 0.1 us)
Async XLA Ops:
  0.0 0.9 %copy-start = (bf16[16,64,128]{2,1,0:T(8,128)(2,1)S(1)}, bf16[16,64,128]{2,1,0:T(8,128)(2,1)}, u32[]{:S(2)}) copy-start(bf16[16,64,128]{2,1,0:T(8,128)(2,1)} %basis_ref.5) | copy-start | bytes 786436
  1.0 0.9 %copy-start.2 = (bf16[16,64,64]{2,1,0:T(8,128)(2,1)S(1)}, bf16[16,64,64]{2,1,0:T(8,128)(2,1)}, u32[]{:S(2)}) copy-start(bf16[16,64,64]{2,1,0:T(8,128)(2,1)} %transfer_ref.5) | copy-start | bytes 393220
  1.9 0.7 %copy-start.6 = (s32[2048]{0:T(1024)S(1)}, s32[2048]{0:T(1024)}, u32[]{:S(2)}) copy-start(s32[2048]{0:T(1024)} %param.12) | copy-start | bytes 24580
  2.6 0.9 %copy-start.11 = (f32[16,2048]{1,0:T(8,128)S(1)}, f32[16,2048]{1,0:T(8,128)}, u32[]{:S(2)}) copy-start(f32[16,2048]{1,0:T(8,128)} %rhs_ref.1) | copy-start | bytes 393220
  3.5 31.6 %copy-start.9 = (bf16[9,2,64,64]{3,2,1,0:T(8,128)(2,1)S(1)}, bf16[9,2,64,64]{3,2,1,0:T(8,128)(2,1)}, u32[]{:S(2)}) copy-start(bf16[9,2,64,64]{3,2,1,0:T(8,128)(2,1)} %transfer_ref.4) | copy-start | bytes 442372
  3.5 31.6 %copy-start.10 = (bf16[9,2,64,64]{3,2,1,0:T(8,128)(2,1)S(1)}, bf16[9,2,64,64]{3,2,1,0:T(8,128)(2,1)}, u32[]{:S(2)}) copy-start(bf16[9,2,64,64]{3,2,1,0:T(8,128)(2,1)} %coupling_ref.2) | copy-start | bytes 442372
  6.6 0.7 %copy-start.15 = (bf16[16,32,64]{2,1,0:T(8,128)(2,1)}, bf16[16,32,64]{2,1,0:T(8,128)(2,1)S(1)}, u32[]{:S(2)}) copy-start(bf16[16,32,64]{2,1,0:T(8,128)(2,1)S(1)} %get-tuple-element.24.coef_ref) | copy-start | bytes 196612
  7.3 27.8 %copy-start.17 = (bf16[16,2048]{1,0:T(8,128)(2,1)}, bf16[16,2048]{1,0:T(8,128)(2,1)S(1)}, u32[]{:S(2)}) copy-start(bf16[16,2048]{1,0:T(8,128)(2,1)S(1)} %get-tuple-element.20.sorted_ref) | copy-start | bytes 196612
  7.3 39.6 %all-to-all-start = ((bf16[32,8,128]{2,1,0:T(8,128)(2,1)}), bf16[32,8,128]{2,1,0:T(8,128)(2,1)S(1)}, u32[]{:S(2)}, u32[]{:S(2)}) async-start(bf16[32,8,128]{2,1,0:T(8,128)(2,1)} %get-tuple-element.15), calls=%async_computation | async-start | bytes 131072 | tf_op jit(solution)/shard_map/all_to_all | solution.py:306
  22.8 0.7 %copy-start.7 = (s32[2048]{0:T(1024)S(1)}, s32[2048]{0:T(1024)}, u32[]{:S(2)}) copy-start(s32[2048]{0:T(1024)} %param.12) | copy-start | bytes 24580
  23.5 0.7 %copy-start.12 = (bf16[3,2048]{1,0:T(4,128)(2,1)S(1)}, bf16[3,2048]{1,0:T(4,128)(2,1)}, u32[]{:S(2)}) copy-start(bf16[3,2048]{1,0:T(4,128)(2,1)} %coords_ref.1) | copy-start | bytes 36868
  24.6 0.6 copy-start.21
  25.3 28.0 %collective-permute-start = (bf16[32,128]{1,0:T(8,128)(2,1)S(1)}, bf16[32,128]{1,0:T(8,128)(2,1)S(1)}, u32[]{:S(2)}, u32[]{:S(2)}) collective-permute-start(bf16[32,128]{1,0:T(8,128)(2,1)S(1)} %get-tuple-element.22), channel_id=1, source_target_pairs={{0,1},{1,2},{2,3},{3,4},{4,5},{5,6},{6,7},{7,8},{8,9},{9,10},{10,1... | collective-permute-start | bytes 24584 | tf_op jit(solution)/shard_map/ppermute | solution.py:315
  27.5 25.9 %collective-permute-start.1 = (bf16[32,128]{1,0:T(8,128)(2,1)S(1)}, bf16[32,128]{1,0:T(8,128)(2,1)S(1)}, u32[]{:S(2)}, u32[]{:S(2)}) collective-permute-start(bf16[32,128]{1,0:T(8,128)(2,1)S(1)} %get-tuple-element.23), channel_id=1, source_target_pairs={{1,0},{2,1},{3,2},{4,3},{5,4},{6,5},{7,6},{8,7},{9,8},{10,9},{11,1... | collective-permute-start | bytes 24584 | tf_op jit(solution)/shard_map/ppermute | solution.py:316
  38.6 0.7 %copy-start.4 = (bf16[16,64,128]{2,1,0:T(8,128)(2,1)}, bf16[16,64,128]{2,1,0:T(8,128)(2,1)S(1)}, u32[]{:S(2)}) copy-start(bf16[16,64,128]{2,1,0:T(8,128)(2,1)S(1)} %get-tuple-element.18.weight_ref) | copy-start | bytes 786436
  39.3 4.0 %copy-start.1 = (bf16[16,64,128]{2,1,0:T(8,128)(2,1)S(1)}, bf16[16,64,128]{2,1,0:T(8,128)(2,1)}, u32[]{:S(2)}) copy-start(bf16[16,64,128]{2,1,0:T(8,128)(2,1)} %basis_ref.5) | copy-start | bytes 786436
  39.3 4.0 %copy-start.13 = (s32[2,128]{1,0:T(2,128)S(1)}, s32[2,128]{1,0:T(2,128)}, u32[]{:S(2)}) copy-start(s32[2,128]{1,0:T(2,128)} %pairs_ref.2) | copy-start | bytes 3076
  43.3 0.9 %copy-start.16 = (bf16[16,32,64]{2,1,0:T(8,128)(2,1)S(1)}, bf16[16,32,64]{2,1,0:T(8,128)(2,1)}, u32[]{:S(2)}) copy-start(bf16[16,32,64]{2,1,0:T(8,128)(2,1)} %copy-done.15) | copy-start | bytes 196612
  44.2 9.1 %copy-start.14 = (s32[2,48]{1,0:T(2,128)S(1)}, s32[2,48]{1,0:T(2,128)}, u32[]{:S(2)}) copy-start(s32[2,48]{1,0:T(2,128)} %pairs_ref.3) | copy-start | bytes 1156
  46.2 0.7 %copy-start.19 = (f32[16,2048]{1,0:T(8,128)}, f32[16,2048]{1,0:T(8,128)S(1)}, u32[]{:S(2)}) copy-start(f32[16,2048]{1,0:T(8,128)S(1)} %shard_map.104.far_ref) | copy-start | bytes 393220
  47.9 11.6 %all-to-all-start.1 = ((f32[16,8,128]{2,1,0:T(8,128)}), f32[16,8,128]{2,1,0:T(8,128)S(1)}, u32[]{:S(2)}, u32[]{:S(2)}) async-start(f32[16,8,128]{2,1,0:T(8,128)} %get-tuple-element.17), calls=%async_computation.1 | async-start | bytes 131072 | tf_op jit(solution)/shard_map/all_to_all | solution.py:341
  53.3 0.8 %copy-start.18 = (bf16[16,2048]{1,0:T(8,128)(2,1)S(1)}, bf16[16,2048]{1,0:T(8,128)(2,1)}, u32[]{:S(2)}) copy-start(bf16[16,2048]{1,0:T(8,128)(2,1)} %copy-done.17) | copy-start | bytes 196612
  54.2 0.9 %copy-start.20 = (f32[16,2048]{1,0:T(8,128)S(1)}, f32[16,2048]{1,0:T(8,128)}, u32[]{:S(2)}) copy-start(f32[16,2048]{1,0:T(8,128)} %copy-done.19) | copy-start | bytes 393220
  55.1 0.8 %copy-start.22 = (bf16[16,2048]{1,0:T(8,128)(2,1)S(1)}, bf16[16,2048]{1,0:T(8,128)(2,1)}, u32[]{:S(2)}) copy-start(bf16[16,2048]{1,0:T(8,128)(2,1)} %copy-done.21) | copy-start | bytes 196612
  55.9 3.7 %copy-start.3 = (bf16[16,64,64]{2,1,0:T(8,128)(2,1)S(1)}, bf16[16,64,64]{2,1,0:T(8,128)(2,1)}, u32[]{:S(2)}) copy-start(bf16[16,64,64]{2,1,0:T(8,128)(2,1)} %transfer_ref.5) | copy-start | bytes 393220
  55.9 3.7 %copy-start.5 = (bf16[16,64,128]{2,1,0:T(8,128)(2,1)S(1)}, bf16[16,64,128]{2,1,0:T(8,128)(2,1)}, u32[]{:S(2)}) copy-start(bf16[16,64,128]{2,1,0:T(8,128)(2,1)} %copy-done.4) | copy-start | bytes 786436
  55.9 3.7 %copy-start.8 = (s32[2048]{0:T(1024)S(1)}, s32[2048]{0:T(1024)}, u32[]{:S(2)}) copy-start(s32[2048]{0:T(1024)} %param.12) | copy-start | bytes 24580

commit v2 on v1

v2 whole, which is shorter than its diff:
```python
import jax
import jax.numpy as jnp
from jax import lax
from jax.experimental import pallas as pl
from jax.experimental.pallas import tpu as pltpu
from jax.sharding import PartitionSpec as P

BF = jnp.bfloat16
F32 = jnp.float32
LEAF = 128
RANK = 64
COLS = 16
LEAVES = 16
PTS = LEAVES * LEAF
LOW = 4
HIGHS = 4
NLOW = 1 << LOW
NHIGH = 1 << HIGHS
VMEM = pl.BlockSpec(memory_space=pltpu.VMEM)
SMEM = pl.BlockSpec(memory_space=pltpu.SMEM)
ANY = pl.BlockSpec(memory_space=pl.ANY)
HBM = pl.BlockSpec(memory_space=pltpu.HBM)


def halves(x):
    hi = x.astype(BF)
    return hi, (x - hi.astype(F32)).astype(BF)


def mm(a, b):
    return jnp.dot(a, b, preferred_element_type=F32)


def mm_nt(a, b):
    return lax.dot_general(a, b, (((1,), (1,)), ((), ())), preferred_element_type=F32)


def wide(a, b):
    ah, al = halves(a)
    bh, bl = halves(b)
    return mm(ah, bh) + (mm(ah, bl) + mm(al, bh))


def wide_nt(a, b):
    ah, al = halves(a)
    bh, bl = halves(b)
    return mm_nt(ah, bh) + (mm_nt(ah, bl) + mm_nt(al, bh))


def low_onehot(order):
    lane = jnp.bitwise_and(order, LEAF - 1)
    rows = lax.broadcasted_iota(jnp.int32, (LEAF, order.shape[1]), 0)
    return jnp.where(rows == lane, 1.0, 0.0).astype(BF)


def permuted(x, order, width):
    stacked = jnp.concatenate([x[:, h * LEAF : (h + 1) * LEAF] for h in range(LEAVES)], axis=0)
    rows = x.shape[0]
    for start in range(0, order.shape[1], width):
        piece = order[:, start : start + width]
        picked = mm(stacked, low_onehot(piece))
        block = jnp.right_shift(piece, 7)
        total = jnp.zeros((rows, width), F32)
        for h in range(LEAVES):
            total = total + jnp.where(block == h, picked[h * rows : (h + 1) * rows], 0.0)
        yield start, total.astype(BF)


def pack_message(x):
    return jnp.concatenate([x[:8], x[8:]], axis=1)


def fetch(sources, buffers, sems):
    copies = [
        pltpu.make_async_copy(source, buffer, sems.at[i])
        for i, (source, buffer) in enumerate(zip(sources, buffers, strict=True))
    ]
    for copy in copies:
        copy.start()
    return copies


def up_kernel(
    order_hbm, rhs_hbm, basis_hbm, transfer_hbm, sorted_ref, coef_ref, message_ref, order_ref, rhs_ref, basis_ref, transfer_ref, sems
):
    copies = fetch(
        (order_hbm, rhs_hbm, basis_hbm, transfer_hbm),
        (order_ref, rhs_ref, basis_ref, transfer_ref),
        sems,
    )
    copies[0].wait()
    copies[1].wait()
    x = rhs_ref[...].astype(BF)
    order = order_ref[...]
    root = jnp.zeros((2 * COLS, RANK), F32)
    for start, piece in permuted(x, order, 2 * LEAF):
        sorted_ref[:, start : start + 2 * LEAF] = piece
        if start == 0:
            copies[2].wait()
            copies[3].wait()
        for i in range(2):
            n = start // LEAF + i
            coef = mm_nt(piece[:, i * LEAF : (i + 1) * LEAF], basis_ref[n])
            hi, lo = halves(coef)
            both = jnp.concatenate([hi, lo], axis=0)
            coef_ref[n] = coef
            root = root + mm(both, transfer_ref[n])
    message = pack_message(root[:COLS] + root[COLS:])
    message_ref[...] = jnp.broadcast_to(message[None], message_ref.shape)


def points_kernel(device_ref, coords_hbm, order_hbm, sorted_ref, near_ref, across_ref, points_ref, coords_ref, order_ref, sems):
    copies = fetch((coords_hbm, order_hbm), (coords_ref, order_ref), sems)
    for copy in copies:
        copy.wait()
    x = jnp.concatenate([coords_ref[...], jnp.zeros((13, PTS), BF)], axis=0)
    for start, piece in permuted(x, order_ref[...], 2 * LEAF):
        points_ref[:, start : start + 2 * LEAF] = piece
    head = jnp.concatenate([sorted_ref[:, 0:LEAF], points_ref[:, 0:LEAF]], axis=0)
    tail = jnp.concatenate([sorted_ref[:, PTS - LEAF :], points_ref[:, PTS - LEAF :]], axis=0)
    even = jnp.bitwise_and(device_ref[0], 1) == 0

    @pl.when(even)
    def _():
        near_ref[...] = tail
        across_ref[...] = head

    @pl.when(jnp.logical_not(even))
    def _():
        near_ref[...] = head
        across_ref[...] = tail


def far_kernel(
    after_ref, coef_ref, pairs_hbm, coupling_hbm, basis_hbm, out_ref, pairs_ref, coupling_ref, basis_ref, by_column, picked, terms, fields, sems
):
    del after_ref
    copies = fetch(
        (pairs_hbm, coupling_hbm, basis_hbm), (pairs_ref, coupling_ref, basis_ref), sems
    )
    for n in range(LEAVES):
        by_column[:, n, :] = coef_ref[n]
    copies[0].wait()
    rows = lax.broadcasted_iota(jnp.int32, (LEAVES, LEAF), 0)
    targets = jnp.where(rows == pairs_ref[0:1, :], 1.0, 0.0).astype(BF)
    sources = jnp.where(rows == pairs_ref[1:2, :], 1.0, 0.0).astype(BF)
    sources = jnp.concatenate([sources, sources], axis=0)
    for k in range(COLS):
        hi, lo = halves(by_column[k])
        both = jnp.concatenate([hi, lo], axis=0)
        picked[k] = lax.dot_general(
            both, sources, (((0,), (0,)), ((), ())), preferred_element_type=F32
        )
    copies[1].wait()
    step = 8

    def some_rows(i, carry):
        at = pl.multiple_of(i * step, step)
        block = coupling_ref[pl.ds(at, step)].astype(F32)
        for k in range(COLS):
            terms[k, pl.ds(at, step), :] = jnp.sum(block * picked[k][None], axis=1)
        return carry

    lax.fori_loop(0, RANK // step, some_rows, 0)
    for k in range(COLS):
        hi, lo = halves(terms[k])
        fields[:, k, :] = mm_nt(targets, hi) + mm_nt(targets, lo)
    copies[2].wait()
    for n in range(LEAVES):
        hi, lo = halves(fields[n])
        both = mm(jnp.concatenate([hi, lo], axis=0), basis_ref[n])
        out_ref[:, n * LEAF : (n + 1) * LEAF] = both[:COLS] + both[COLS:]


def point_features(points):
    p = points.astype(F32)
    x, y, z = p[0:1], p[1:2], p[2:3]
    square = x * x + y * y + z * z
    s0 = square.astype(BF).astype(F32)
    rest = square - s0
    s1 = rest.astype(BF).astype(F32)
    s2 = rest - s1
    one = jnp.ones_like(square)
    zero = jnp.zeros((7, LEAF), F32)
    source = jnp.concatenate([x, y, z, one, one, one, s0, s1, s2, zero], axis=0)
    target = jnp.concatenate(
        [-2.0 * x, -2.0 * y, -2.0 * z, s0, s1, s2, one, one, one, zero], axis=0
    )
    return source, target


def near_kernel(
    device_ref, pairs_ref, sorted_ref, points_ref, inner_ref, across_ref, far_ref, out_ref, rhs, source, target, acc
):
    even = jnp.bitwise_and(device_ref[0], 1) == 0
    inner, across = inner_ref[...], across_ref[...]

    def prepare(n, columns, points):
        rhs[n] = columns
        of_source, of_target = point_features(points)
        source[n] = of_source.T.astype(BF)
        target[n] = of_target.astype(BF)

    prepare(jnp.where(even, LEAVES + 1, 0), inner[:COLS], inner[COLS:])
    prepare(jnp.where(even, 0, LEAVES + 1), across[:COLS], across[COLS:])
    for n in range(LEAVES):
        here = slice(n * LEAF, (n + 1) * LEAF)
        prepare(n + 1, sorted_ref[:, here], points_ref[:, here])
        acc[n] = far_ref[:, here]

    for j in range(LEAVES * 3):
        to, of = pairs_ref[0, j], pairs_ref[1, j]
        squared = jnp.maximum(mm(source[of], target[to + 1]), 0.0)
        scaled = jnp.sqrt(3.0 * squared)
        values = ((0.125 + 0.125 * scaled) * jnp.exp(-scaled)).astype(BF)
        acc[to] += mm(rhs[of], values)
    for n in range(LEAVES):
        out_ref[:, n * LEAF : (n + 1) * LEAF] = acc[n]


def times(a, b):
    hi, lo = halves(a)
    both = mm(jnp.concatenate([hi, lo], axis=0), b)
    return both[: a.shape[0]] + both[a.shape[0] :]


def weights_kernel(device_ref, transfer_hbm, coupling_hbm, low_ref, high_ref, transfer_ref, coupling_ref, sems):
    copies = fetch((transfer_hbm, coupling_hbm), (transfer_ref, coupling_ref), sems)
    device = device_ref[0]
    core = jnp.bitwise_and(device, 1)
    low = jnp.bitwise_and(jnp.right_shift(device, 1), NLOW - 1)
    high = jnp.right_shift(device, LOW + 1)
    for copy in copies:
        copy.wait()
    mine, other = transfer_ref[0, core], transfer_ref[0, 1 - core]

    hi, lo = halves(coupling_ref[0, 1 - core].astype(F32).T)
    zero = jnp.zeros((RANK, RANK), BF)
    low_ref[pl.ds(low, 1), :, 2 * RANK :] = jnp.concatenate([zero, hi, zero, lo], axis=1)[None]

    senders = mine.astype(F32)
    path = jnp.concatenate([mine, other], axis=0).astype(F32)
    for level in range(1, LOW + 1):
        h = level - 1
        node = jnp.right_shift(low, h)
        side = jnp.bitwise_and(node, 1)
        at = jnp.left_shift(jnp.bitwise_xor(node, 1), h)
        end = times(path, coupling_ref[level, side])
        hi, lo = halves(wide_nt(senders, end))
        low_ref[pl.ds(at, 1 << h), :, 2 * RANK :] = jnp.concatenate([hi, lo], axis=1).reshape(
            1 << h, RANK, 4 * RANK
        )
        path = times(path, transfer_ref[level, side])
        senders = jnp.concatenate(
            [times(senders, transfer_ref[level, 0]), times(senders, transfer_ref[level, 1])], axis=0
        )
    hi, lo = halves(senders)
    low_ref[:, :, : 2 * RANK] = jnp.concatenate([hi, lo], axis=1).reshape(NLOW, RANK, 2 * RANK)

    path = path[:RANK]
    high_ref[pl.ds(high, 1)] = jnp.zeros((1, RANK, 2 * RANK), BF)
    for h in range(HIGHS):
        level = LOW + 1 + h
        node = jnp.right_shift(high, h)
        side = jnp.bitwise_and(node, 1)
        at = jnp.left_shift(jnp.bitwise_xor(node, 1), h)
        end = times(path, coupling_ref[level, side])
        hi, lo = halves(end.T if h == 0 else wide_nt(senders, end))
        high_ref[pl.ds(at, 1 << h)] = jnp.concatenate([hi, lo], axis=1).reshape(
            1 << h, RANK, 2 * RANK
        )
        if h == HIGHS - 1:
            break
        path = times(path, transfer_ref[level, side])
        if h == 0:
            senders = transfer_ref[level].reshape(2 * RANK, RANK).astype(F32)
        else:
            senders = jnp.concatenate(
                [times(senders, transfer_ref[level, 0]), times(senders, transfer_ref[level, 1])], axis=0
            )


def unpacked(message):
    x = jnp.concatenate([message[:, :RANK], message[:, RANK:]], axis=0)
    hi, lo = halves(x)
    return jnp.concatenate([hi, lo], axis=0)


def middle_kernel(device_ref, received_ref, weight_ref, message_ref, field_ref):
    device = device_ref[0]
    total = jnp.zeros((2 * COLS, 6 * RANK), F32)
    for s in range(NLOW):
        total = total + mm(unpacked(received_ref[s]), weight_ref[s])
    total = total[:COLS] + total[COLS:]
    node = total[:, :RANK] + total[:, RANK : 2 * RANK]
    fields = total[:, 2 * RANK : 4 * RANK] + total[:, 4 * RANK :]
    field_ref[...] = fields[:, :RANK]
    message_ref[...] = jnp.broadcast_to(pack_message(node)[None], message_ref.shape)
    high, core = jnp.right_shift(device, LOW + 1), jnp.bitwise_and(device, 1)
    message_ref[high * 2 + 1 - core] = pack_message(fields[:, RANK:])


def down_kernel(
    device_ref, received_ref, weight_ref, field_ref, partial_ref, transfer_hbm, basis_hbm, order_hbm, out_ref, transfer_ref, basis_ref, order_ref, sems
):
    copies = fetch(
        (transfer_hbm, basis_hbm, order_hbm), (transfer_ref, basis_ref, order_ref), sems
    )
    device = device_ref[0]
    high, core = jnp.right_shift(device, LOW + 1), jnp.bitwise_and(device, 1)
    total = jnp.zeros((2 * COLS, 2 * RANK), F32)
    for g in range(NHIGH):
        total = total + mm(unpacked(received_ref[2 * g] + received_ref[2 * g + 1]), weight_ref[g])
    total = total[:COLS] + total[COLS:]
    sibling = received_ref[high * 2 + 1 - core]
    field = field_ref[...] + (total[:, :RANK] + total[:, RANK:])
    field = field + jnp.concatenate([sibling[:, :RANK], sibling[:, RANK:]], axis=0)
    hi, lo = halves(field)
    field = jnp.concatenate([hi, lo], axis=0)
    result = jnp.zeros((LEAVES * 2 * COLS, LEAF), F32)
    for copy in copies:
        copy.wait()
    order = order_ref[...]
    for start in range(0, PTS, 2 * LEAF):
        pieces = []
        for n in range(start // LEAF, start // LEAF + 2):
            leaf_field = mm_nt(field, transfer_ref[n])
            hi, lo = halves(leaf_field[:COLS] + leaf_field[COLS:])
            both = mm(jnp.concatenate([hi, lo], axis=0), basis_ref[n])
            pieces.append(both[:COLS] + both[COLS:])
        values = jnp.concatenate(pieces, axis=1) + partial_ref[:, start : start + 2 * LEAF]
        hi, lo = halves(values)
        both = jnp.concatenate([hi, lo], axis=0)
        piece = order[:, start : start + 2 * LEAF]
        block = jnp.right_shift(piece, 7)
        masked = jnp.concatenate(
            [both * jnp.where(block == h, 1.0, 0.0).astype(BF) for h in range(LEAVES)], axis=0
        )
        result = result + mm_nt(masked, low_onehot(piece))
    for h in range(LEAVES):
        at = h * 2 * COLS
        out_ref[:, h * LEAF : (h + 1) * LEAF] = result[at : at + COLS] + result[at + COLS : at + 2 * COLS]


def call(kernel, out, inputs, buffers=(), scratch=(), flops=0, transcendentals=0):
    shapes = [jax.ShapeDtypeStruct(s, t) for s, t in out]
    scratches = [pltpu.VMEM(s, t) for s, t in buffers] + [pltpu.VMEM(s, t) for s, t in scratch]
    if buffers:
        scratches.append(pltpu.SemaphoreType.DMA((len(buffers),)))
    return pl.pallas_call(
        kernel,
        out_shape=shapes,
        in_specs=[space for space, _ in inputs],
        out_specs=[VMEM] * len(out),
        scratch_shapes=scratches,
        compiler_params=pltpu.CompilerParams(vmem_limit_bytes=16 << 20),
        cost_estimate=pl.CostEstimate(
            flops=flops, bytes_accessed=1 << 20, transcendentals=transcendentals
        ),
    )(*[array for _, array in inputs])


def per_device(
    right_sides,
    coordinates,
    tree_order,
    leaf_basis,
    far_pairs,
    far_coupling,
    near_pairs,
    leaf_transfer,
    top_transfer,
    top_coupling,
):
    count = lax.axis_size("leaf")
    device = lax.axis_index("leaf").astype(jnp.int32).reshape(1)
    order = tree_order.reshape(1, PTS)
    basis_like = (leaf_basis.shape, BF)
    transfer_like = (leaf_transfer.shape, BF)
    order_like = (order.shape, jnp.int32)
    sorted_rhs, coef, message = call(
        up_kernel,
        [((COLS, PTS), BF), ((LEAVES, COLS, RANK), F32), ((NLOW, 8, 2 * RANK), F32)],
        [(HBM, order), (HBM, right_sides), (HBM, leaf_basis), (HBM, leaf_transfer)],
        buffers=[order_like, (right_sides.shape, F32), basis_like, transfer_like],
        flops=1 << 28,
    )
    low_groups = [
        [(g * NLOW + z) * 2 + c for z in range(NLOW)] for g in range(NHIGH) for c in range(2)
    ]
    high_groups = [
        [(g * NLOW + z) * 2 + c for g in range(NHIGH) for c in range(2)] for z in range(NLOW)
    ]
    received = lax.all_to_all(message, "leaf", 0, 0, axis_index_groups=low_groups, tiled=True)

    inner, across, points = call(
        points_kernel,
        [((2 * COLS, LEAF), BF), ((2 * COLS, LEAF), BF), ((COLS, PTS), BF)],
        [(SMEM, device), (HBM, coordinates), (HBM, order), (VMEM, sorted_rhs)],
        buffers=[(coordinates.shape, BF), order_like],
        flops=1 << 28,
    )
    inner = lax.ppermute(inner, "leaf", [(i, i ^ 1) for i in range(count)])
    pairs = [(i, i + 1) for i in range(1, count - 1, 2)]
    across = lax.ppermute(across, "leaf", pairs + [(j, i) for i, j in pairs])
    low_weight, high_weight = call(
        weights_kernel,
        [((NLOW, RANK, 6 * RANK), BF), ((NHIGH, RANK, 2 * RANK), BF)],
        [(SMEM, device), (HBM, top_transfer), (HBM, top_coupling)],
        buffers=[(top_transfer.shape, BF), (top_coupling.shape, BF)],
        flops=1 << 30,
    )
    message, field = call(
        middle_kernel,
        [((2 * NHIGH, 8, 2 * RANK), F32), ((COLS, RANK), F32)],
        [(SMEM, device), (VMEM, received), (VMEM, low_weight)],
        flops=1 << 27,
    )
    received = lax.all_to_all(message, "leaf", 0, 0, axis_index_groups=high_groups, tiled=True)
    coupling = far_coupling.transpose(1, 2, 0)
    (far,) = call(
        far_kernel,
        [((COLS, PTS), F32)],
        [(ANY, field), (VMEM, coef), (HBM, far_pairs), (HBM, coupling), (HBM, leaf_basis)],
        buffers=[(far_pairs.shape, jnp.int32), (coupling.shape, BF), basis_like],
        scratch=[
            ((COLS, LEAVES, RANK), F32),
            ((COLS, RANK, LEAF), F32),
            ((COLS, RANK, LEAF), F32),
            ((LEAVES, COLS, RANK), F32),
        ],
        flops=1 << 31,
    )
    (partial,) = call(
        near_kernel,
        [((COLS, PTS), F32)],
        [
            (SMEM, device),
            (SMEM, near_pairs),
            (VMEM, sorted_rhs),
            (VMEM, points),
            (VMEM, inner),
            (VMEM, across),
            (VMEM, far),
        ],
        scratch=[
            ((LEAVES + 2, COLS, LEAF), BF),
            ((LEAVES + 2, LEAF, COLS), BF),
            ((LEAVES + 2, COLS, LEAF), BF),
            ((LEAVES, COLS, LEAF), F32),
        ],
        flops=1 << 31,
        transcendentals=1 << 21,
    )
    (product,) = call(
        down_kernel,
        [((COLS, PTS), F32)],
        [
            (SMEM, device),
            (VMEM, received),
            (VMEM, high_weight),
            (VMEM, field),
            (VMEM, partial),
            (HBM, leaf_transfer),
            (HBM, leaf_basis),
            (HBM, order),
        ],
        buffers=[transfer_like, basis_like, order_like],
        flops=1 << 28,
    )
    return product


def solution(mesh):
    return jax.shard_map(
        per_device,
        mesh=mesh,
        in_specs=(
            P(None, "leaf"),
            P(None, "leaf"),
            P("leaf"),
            P("leaf", None, None),
            P(None, "leaf"),
            P("leaf", None, None),
            P(None, "leaf"),
            P("leaf", None, None),
            P(),
            P(),
        ),
        out_specs=P(None, "leaf"),
        check_vma=False,
    )
```

time: 64.5 us -> 58.7 us (0.910)
  the two profiles are of different devices: /device:TPU:2 before, /device:TPU:1 now
where the time goes in v2:
time: 58.7 us; the launch traced here: 58.1 us
  starting transfers between devices  31.4 us (53%)
  Pallas kernels  19.6 us (33%)
  local copies, waits for them, and re-layouts  5.51 us (9%)
  waiting for transfers between devices  1.44 us (2%)
    pallas_call x7, Pallas kernels, call(): pl.pallas_call(kernel, out_shape=shapes, in_specs=[space for space, _ in...  19.6 us
    all_to_all x1, starting transfers between devices, per_device(): lax.all_to_all(message, 'leaf', 0, 0, axis_index_groups=low_groups, tiled...  15.8 us
    all_to_all x1, starting transfers between devices, per_device(): lax.all_to_all(message, 'leaf', 0, 0, axis_index_groups=high_groups, tile...  9.33 us
    unnamed x26, local copies, waits for them, and re-layouts  5.51 us
    ppermute x1, starting transfers between devices, per_device(): across = lax.ppermute(across, 'leaf', pairs + [(j, i) for i, j in pairs])  3.45 us
    ppermute x1, starting transfers between devices, per_device(): inner = lax.ppermute(inner, 'leaf', [(i, i ^ 1) for i in range(count)])  2.86 us
    all_to_all x1, waiting for transfers between devices, per_device(): lax.all_to_all(message, 'leaf', 0, 0, axis_index_groups=low_groups, tiled...  1.44 us
  transfers between devices with their start and end apart: 4, of which 1 were waited for; matrix products, arithmetic and copies ran while one was open for 0% of the time, Pallas kernels for 20%

profile of v2, /device:TPU:1, one launch (start us, length us, event | category | flops | bytes accessed | tf_op | source)
XLA Modules:
  0.0 58.1 jit_solution(13696670845505658529)
XLA Ops:
  0.0 0.9 %copy-done = bf16[16,64,128]{2,1,0:T(8,128)(2,1)S(1)} copy-done((bf16[16,64,128]{2,1,0:T(8,128)(2,1)S(1)}, bf16[16,64,128]{2,1,0:T(8,128)(2,1)}, u32[]{:S(2)}) %copy-start) | copy-done | bytes 262168
  1.0 0.9 %copy-done.2 = bf16[16,64,64]{2,1,0:T(8,128)(2,1)S(1)} copy-done((bf16[16,64,64]{2,1,0:T(8,128)(2,1)S(1)}, bf16[16,64,64]{2,1,0:T(8,128)(2,1)}, u32[]{:S(2)}) %copy-start.2) | copy-done | bytes 131096
  1.9 0.7 %copy-done.4 = s32[2048]{0:T(1024)S(1)} copy-done((s32[2048]{0:T(1024)S(1)}, s32[2048]{0:T(1024)}, u32[]{:S(2)}) %copy-start.4) | copy-done | bytes 8216
  2.6 0.9 %copy-done.9 = f32[16,2048]{1,0:T(8,128)S(1)} copy-done((f32[16,2048]{1,0:T(8,128)S(1)}, f32[16,2048]{1,0:T(8,128)}, u32[]{:S(2)}) %copy-start.9) | copy-done | bytes 131096
  3.5 3.3 %shard_map.100 = (bf16[16,2048]{1,0:T(8,128)(2,1)S(1)}, f32[16,16,64]{2,1,0:T(8,128)S(1)}, f32[16,8,128]{2,1,0:T(8,128)}) custom-call(s32[1,2048]{1,0:T(1,128)S(1)} %bitcast.3, f32[16,2048]{1,0:T(8,128)S(1)} %copy-done.9, bf16[16,64,128]{2,1,0:T(8,128)(2,1)S(1)} %copy-done, bf16[16,64,64]{2,1,0:T(8,128)(2,1)S(1)} %copy-done.2), custom_call_target="tpu_custom_call" | custom-call | flops 268435456 | bytes 1048576 | tf_op jit(solution)/shard_map/pallas_call | solution.py:350
  6.9 0.0 copy-start.10
  6.9 15.8 %all-to-all-start = ((f32[16,8,128]{2,1,0:T(8,128)}), f32[16,8,128]{2,1,0:T(8,128)S(1)}, u32[]{:S(2)}, u32[]{:S(2)}) async-start(f32[16,8,128]{2,1,0:T(8,128)} %get-tuple-element.15), calls=%async_computation | async-start | bytes 131072 | tf_op jit(solution)/shard_map/all_to_all | solution.py:394
  22.6 0.0 copy-start.5
  22.6 0.0 copy-done.10
  22.7 0.7 %copy-done.5 = s32[2048]{0:T(1024)S(1)} copy-done((s32[2048]{0:T(1024)S(1)}, s32[2048]{0:T(1024)}, u32[]{:S(2)}) %copy-start.5) | copy-done | bytes 8216
  23.3 0.5 shard_map.103
  23.8 2.9 %collective-permute-start = (bf16[32,128]{1,0:T(8,128)(2,1)S(1)}, bf16[32,128]{1,0:T(8,128)(2,1)S(1)}, u32[]{:S(2)}, u32[]{:S(2)}) collective-permute-start(bf16[32,128]{1,0:T(8,128)(2,1)S(1)} %get-tuple-element.22), channel_id=1, source_target_pairs={{0,1},{1,0},{2,3},{3,2},{4,5},{5,4},{6,7},{7,6},{8,9},{9,8},{10,11... | collective-permute-start | bytes 24584 | tf_op jit(solution)/shard_map/ppermute | solution.py:403
  26.7 3.4 %collective-permute-start.1 = (bf16[32,128]{1,0:T(8,128)(2,1)S(1)}, bf16[32,128]{1,0:T(8,128)(2,1)S(1)}, u32[]{:S(2)}, u32[]{:S(2)}) collective-permute-start(bf16[32,128]{1,0:T(8,128)(2,1)S(1)} %get-tuple-element.23), channel_id=1, source_target_pairs={{1,2},{3,4},{5,6},{7,8},{9,10},{11,12},{13,14},{15,16},{17,18},{19... | collective-permute-start | bytes 24584 | tf_op jit(solution)/shard_map/ppermute | solution.py:405
  30.2 0.0 copy-done.7
  30.2 0.0 copy-done.8
  30.2 0.0 copy-start.6
  30.2 2.6 %shard_map.101 = (bf16[16,64,384]{2,1,0:T(8,128)(2,1)S(1)}, bf16[16,64,128]{2,1,0:T(8,128)(2,1)S(1)}) custom-call(s32[1]{0:T(128)} %bitcast.device_ref, bf16[9,2,64,64]{3,2,1,0:T(8,128)(2,1)S(1)} %copy-done.7, bf16[9,2,64,64]{3,2,1,0:T(8,128)(2,1)S(1)} %copy-done.8), custom_call_target="tpu_custom_call" | custom-call | flops 1073741824 | bytes 1048576 | tf_op jit(solution)/shard_map/pallas_call | solution.py:350
  32.8 1.4 %all-to-all-done.received_ref = f32[16,8,128]{2,1,0:T(8,128)S(1)} async-done(((f32[16,8,128]{2,1,0:T(8,128)}), f32[16,8,128]{2,1,0:T(8,128)S(1)}, u32[]{:S(2)}, u32[]{:S(2)}) %all-to-all-start) | async-done | bytes 65568 | tf_op jit(solution)/shard_map/all_to_all | solution.py:394
  34.2 1.2 %shard_map.102 = (f32[32,8,128]{2,1,0:T(8,128)}, f32[16,64]{1,0:T(8,128)S(1)}) custom-call(s32[1]{0:T(128)} %bitcast.device_ref, f32[16,8,128]{2,1,0:T(8,128)S(1)} %all-to-all-done.received_ref, bf16[16,64,384]{2,1,0:T(8,128)(2,1)S(1)} %get-tuple-element.16.weight_ref), custom_call_target="tpu_custom_call" | custom-call | flops 134217728 | bytes 1048576 | tf_op jit(solution)/shard_map/pallas_call | solution.py:350
  35.4 9.3 %all-to-all-start.1 = ((f32[32,8,128]{2,1,0:T(8,128)}), f32[32,8,128]{2,1,0:T(8,128)S(1)}, u32[]{:S(2)}, u32[]{:S(2)}) async-start(f32[32,8,128]{2,1,0:T(8,128)} %get-tuple-element.17), calls=%async_computation.1 | async-start | bytes 262144 | tf_op jit(solution)/shard_map/all_to_all | solution.py:419
  44.7 0.0 copy-start.11
  44.8 0.0 copy-done.6
  44.8 0.0 copy-done.1
  44.8 0.7 %copy-done.11 = s32[2,128]{1,0:T(2,128)S(1)} copy-done((s32[2,128]{1,0:T(2,128)S(1)}, s32[2,128]{1,0:T(2,128)}, u32[]{:S(2)}) %copy-start.11) | copy-done | bytes 1048
  45.4 4.9 %shard_map.104.far_ref = f32[16,2048]{1,0:T(8,128)S(1)} custom-call(f32[16,64]{1,0:T(8,128)S(1)} %get-tuple-element.19.after_ref.field_ref, f32[16,16,64]{2,1,0:T(8,128)S(1)} %get-tuple-element.24.coef_ref, s32[2,128]{1,0:T(2,128)S(1)} %copy-done.11, bf16[64,64,128]{2,1,0:T(8,128)(2,1)S(1)} %bitcast.6, bf16[16,64,128]{2,1,0:T(8,128)(2,1)S(1)} %copy-done.1), custom_call_target="tpu_custom_call" | custom-call | flops 2147483648 | bytes 1048576 | tf_op jit(solution)/shard_map/pallas_call | solution.py:350
  50.4 0.0 copy-start.12
  50.4 0.0 collective-permute-done.inner_ref
  50.4 0.0 collective-permute-done.1.across_ref
  50.4 0.6 %copy-done.12 = s32[2,48]{1,0:T(2,128)S(1)} copy-done((s32[2,48]{1,0:T(2,128)S(1)}, s32[2,48]{1,0:T(2,128)}, u32[]{:S(2)}) %copy-start.12) | copy-done | bytes 408
  51.1 2.6 %shard_map.105.partial_ref = f32[16,2048]{1,0:T(8,128)S(1)} custom-call(s32[1]{0:T(128)} %bitcast.device_ref, s32[2,48]{1,0:T(2,128)S(1)} %copy-done.12, bf16[16,2048]{1,0:T(8,128)(2,1)S(1)} %get-tuple-element.20.sorted_ref, bf16[16,2048]{1,0:T(8,128)(2,1)S(1)} %get-tuple-element.21.points_ref, bf16[32,128]{1,0:T(8,128)(2,1)S(1)} %collective-permute-done.inner_ref, ...), custom_call_target="tpu_custom_call" | custom-call | flops 2147483648 | bytes 1048576 | tf_op jit(solution)/shard_map/pallas_call | solution.py:350
  53.7 0.0 all-to-all-done.1.received_ref
  53.7 4.4 %shard_map.106 = f32[16,2048]{1,0:T(8,128)} custom-call(s32[1]{0:T(128)} %bitcast.device_ref, f32[32,8,128]{2,1,0:T(8,128)S(1)} %all-to-all-done.1.received_ref, bf16[16,64,128]{2,1,0:T(8,128)(2,1)S(1)} %get-tuple-element.18.weight_ref, f32[16,64]{1,0:T(8,128)S(1)} %get-tuple-element.19.after_ref.field_ref, f32[16,2048]{1,0:T(8,128)S(1)} %shard_map.105.partial_ref, ...), custom_call_target="tpu_custom_call" | custom-call | flops 268435456 | bytes 1048576 | tf_op jit(solution)/shard_map/pallas_call | solution.py:350
  (9 shorter events, 0.0 us)
Async XLA Ops:
  0.0 0.9 %copy-start = (bf16[16,64,128]{2,1,0:T(8,128)(2,1)S(1)}, bf16[16,64,128]{2,1,0:T(8,128)(2,1)}, u32[]{:S(2)}) copy-start(bf16[16,64,128]{2,1,0:T(8,128)(2,1)} %basis_hbm.5) | copy-start | bytes 786436
  1.0 0.9 %copy-start.2 = (bf16[16,64,64]{2,1,0:T(8,128)(2,1)S(1)}, bf16[16,64,64]{2,1,0:T(8,128)(2,1)}, u32[]{:S(2)}) copy-start(bf16[16,64,64]{2,1,0:T(8,128)(2,1)} %transfer_hbm.5) | copy-start | bytes 393220
  1.9 0.7 %copy-start.4 = (s32[2048]{0:T(1024)S(1)}, s32[2048]{0:T(1024)}, u32[]{:S(2)}) copy-start(s32[2048]{0:T(1024)} %param.12) | copy-start | bytes 24580
  2.6 0.9 %copy-start.9 = (f32[16,2048]{1,0:T(8,128)S(1)}, f32[16,2048]{1,0:T(8,128)}, u32[]{:S(2)}) copy-start(f32[16,2048]{1,0:T(8,128)} %rhs_hbm.1) | copy-start | bytes 393220
  6.9 15.8 %copy-start.10 = (bf16[3,2048]{1,0:T(4,128)(2,1)S(1)}, bf16[3,2048]{1,0:T(4,128)(2,1)}, u32[]{:S(2)}) copy-start(bf16[3,2048]{1,0:T(4,128)(2,1)} %coords_hbm.1) | copy-start | bytes 36868
  6.9 27.3 %all-to-all-start = ((f32[16,8,128]{2,1,0:T(8,128)}), f32[16,8,128]{2,1,0:T(8,128)S(1)}, u32[]{:S(2)}, u32[]{:S(2)}) async-start(f32[16,8,128]{2,1,0:T(8,128)} %get-tuple-element.15), calls=%async_computation | async-start | bytes 131072 | tf_op jit(solution)/shard_map/all_to_all | solution.py:394
  22.6 0.7 %copy-start.5 = (s32[2048]{0:T(1024)S(1)}, s32[2048]{0:T(1024)}, u32[]{:S(2)}) copy-start(s32[2048]{0:T(1024)} %param.12) | copy-start | bytes 24580
  23.3 6.8 %copy-start.7 = (bf16[9,2,64,64]{3,2,1,0:T(8,128)(2,1)S(1)}, bf16[9,2,64,64]{3,2,1,0:T(8,128)(2,1)}, u32[]{:S(2)}) copy-start(bf16[9,2,64,64]{3,2,1,0:T(8,128)(2,1)} %transfer_hbm.4) | copy-start | bytes 442372
  23.3 6.8 %copy-start.8 = (bf16[9,2,64,64]{3,2,1,0:T(8,128)(2,1)S(1)}, bf16[9,2,64,64]{3,2,1,0:T(8,128)(2,1)}, u32[]{:S(2)}) copy-start(bf16[9,2,64,64]{3,2,1,0:T(8,128)(2,1)} %coupling_hbm.1) | copy-start | bytes 442372
  23.8 26.5 %collective-permute-start = (bf16[32,128]{1,0:T(8,128)(2,1)S(1)}, bf16[32,128]{1,0:T(8,128)(2,1)S(1)}, u32[]{:S(2)}, u32[]{:S(2)}) collective-permute-start(bf16[32,128]{1,0:T(8,128)(2,1)S(1)} %get-tuple-element.22), channel_id=1, source_target_pairs={{0,1},{1,0},{2,3},{3,2},{4,5},{5,4},{6,7},{7,6},{8,9},{9,8},{10,11... | collective-permute-start | bytes 24584 | tf_op jit(solution)/shard_map/ppermute | solution.py:403
  26.7 23.7 %collective-permute-start.1 = (bf16[32,128]{1,0:T(8,128)(2,1)S(1)}, bf16[32,128]{1,0:T(8,128)(2,1)S(1)}, u32[]{:S(2)}, u32[]{:S(2)}) collective-permute-start(bf16[32,128]{1,0:T(8,128)(2,1)S(1)} %get-tuple-element.23), channel_id=1, source_target_pairs={{1,2},{3,4},{5,6},{7,8},{9,10},{11,12},{13,14},{15,16},{17,18},{19... | collective-permute-start | bytes 24584 | tf_op jit(solution)/shard_map/ppermute | solution.py:405
  30.2 14.6 %copy-start.6 = (bf16[128,64,64]{0,2,1:T(8,128)(2,1)S(1)}, bf16[128,64,64]{0,2,1:T(8,128)(2,1)}, u32[]{:S(2)}) copy-start(bf16[128,64,64]{0,2,1:T(8,128)(2,1)} %param.15) | copy-start | bytes 3145732
  35.4 9.4 %copy-start.1 = (bf16[16,64,128]{2,1,0:T(8,128)(2,1)S(1)}, bf16[16,64,128]{2,1,0:T(8,128)(2,1)}, u32[]{:S(2)}) copy-start(bf16[16,64,128]{2,1,0:T(8,128)(2,1)} %basis_hbm.5) | copy-start | bytes 786436
  35.4 18.3 %all-to-all-start.1 = ((f32[32,8,128]{2,1,0:T(8,128)}), f32[32,8,128]{2,1,0:T(8,128)S(1)}, u32[]{:S(2)}, u32[]{:S(2)}) async-start(f32[32,8,128]{2,1,0:T(8,128)} %get-tuple-element.17), calls=%async_computation.1 | async-start | bytes 262144 | tf_op jit(solution)/shard_map/all_to_all | solution.py:419
  44.7 0.7 %copy-start.11 = (s32[2,128]{1,0:T(2,128)S(1)}, s32[2,128]{1,0:T(2,128)}, u32[]{:S(2)}) copy-start(s32[2,128]{1,0:T(2,128)} %pairs_hbm.1) | copy-start | bytes 3076
  50.4 0.7 %copy-start.12 = (s32[2,48]{1,0:T(2,128)S(1)}, s32[2,48]{1,0:T(2,128)}, u32[]{:S(2)}) copy-start(s32[2,48]{1,0:T(2,128)} %pairs_ref.1) | copy-start | bytes 1156
  51.1 2.7 %copy-start.3 = (bf16[16,64,64]{2,1,0:T(8,128)(2,1)S(1)}, bf16[16,64,64]{2,1,0:T(8,128)(2,1)}, u32[]{:S(2)}) copy-start(bf16[16,64,64]{2,1,0:T(8,128)(2,1)} %transfer_hbm.5) | copy-start | bytes 393220

commit v3 on v2

--- a/solution.py
+++ b/solution.py
@@ -11,11 +11,14 @@
 RANK = 64
 COLS = 16
 LEAVES = 16
+WIDE = 256
+BLOCKS = 8
 PTS = LEAVES * LEAF
 LOW = 4
 HIGHS = 4
 NLOW = 1 << LOW
 NHIGH = 1 << HIGHS
+LOG2E = 1.4426950408889634
 VMEM = pl.BlockSpec(memory_space=pltpu.VMEM)
 SMEM = pl.BlockSpec(memory_space=pltpu.SMEM)
 ANY = pl.BlockSpec(memory_space=pl.ANY)
@@ -48,20 +51,20 @@
 
 
 def low_onehot(order):
-    lane = jnp.bitwise_and(order, LEAF - 1)
-    rows = lax.broadcasted_iota(jnp.int32, (LEAF, order.shape[1]), 0)
-    return jnp.where(rows == lane, 1.0, 0.0).astype(BF)
+    lane = jnp.bitwise_and(order, WIDE - 1).astype(F32).astype(BF)
+    rows = lax.broadcasted_iota(jnp.int32, (WIDE, order.shape[1]), 0).astype(F32).astype(BF)
+    return jnp.where(rows == lane, jnp.ones((), BF), jnp.zeros((), BF))
 
 
 def permuted(x, order, width):
-    stacked = jnp.concatenate([x[:, h * LEAF : (h + 1) * LEAF] for h in range(LEAVES)], axis=0)
+    stacked = jnp.concatenate([x[:, h * WIDE : (h + 1) * WIDE] for h in range(BLOCKS)], axis=0)
     rows = x.shape[0]
     for start in range(0, order.shape[1], width):
         piece = order[:, start : start + width]
         picked = mm(stacked, low_onehot(piece))
-        block = jnp.right_shift(piece, 7)
+        block = jnp.right_shift(piece, 8)
         total = jnp.zeros((rows, width), F32)
-        for h in range(LEAVES):
+        for h in range(BLOCKS):
             total = total + jnp.where(block == h, picked[h * rows : (h + 1) * rows], 0.0)
         yield start, total.astype(BF)
 
@@ -92,19 +95,24 @@
     copies[1].wait()
     x = rhs_ref[...].astype(BF)
     order = order_ref[...]
-    root = jnp.zeros((2 * COLS, RANK), F32)
-    for start, piece in permuted(x, order, 2 * LEAF):
-        sorted_ref[:, start : start + 2 * LEAF] = piece
-        if start == 0:
-            copies[2].wait()
-            copies[3].wait()
-        for i in range(2):
-            n = start // LEAF + i
-            coef = mm_nt(piece[:, i * LEAF : (i + 1) * LEAF], basis_ref[n])
-            hi, lo = halves(coef)
-            both = jnp.concatenate([hi, lo], axis=0)
-            coef_ref[n] = coef
-            root = root + mm(both, transfer_ref[n])
+    block = jnp.right_shift(order, 8)
+    places = low_onehot(order)
+    copies[2].wait()
+    copies[3].wait()
+    stacked = jnp.concatenate([x[:, h * WIDE : (h + 1) * WIDE] for h in range(BLOCKS)], axis=0)
+    picked = mm(stacked, places)
+    total = jnp.where(block == 0, picked[:COLS], 0.0)
+    for h in range(1, BLOCKS):
+        total = total + jnp.where(block == h, picked[h * COLS : (h + 1) * COLS], 0.0)
+    total = total.astype(BF)
+    sorted_ref[...] = total
+    coefs = []
+    for n in range(LEAVES):
+        coef = mm_nt(total[:, n * LEAF : (n + 1) * LEAF], basis_ref[n])
+        coefs.append(coef)
+        coef_ref[n] = coef
+    hi, lo = halves(jnp.concatenate(coefs, axis=1))
+    root = mm(jnp.concatenate([hi, lo], axis=0), transfer_ref[...].reshape(LEAVES * RANK, RANK))
     message = pack_message(root[:COLS] + root[COLS:])
     message_ref[...] = jnp.broadcast_to(message[None], message_ref.shape)
 
@@ -131,47 +139,6 @@
         across_ref[...] = tail
 
 
-def far_kernel(
-    after_ref, coef_ref, pairs_hbm, coupling_hbm, basis_hbm, out_ref, pairs_ref, coupling_ref, basis_ref, by_column, picked, terms, fields, sems
-):
-    del after_ref
-    copies = fetch(
-        (pairs_hbm, coupling_hbm, basis_hbm), (pairs_ref, coupling_ref, basis_ref), sems
-    )
-    for n in range(LEAVES):
-        by_column[:, n, :] = coef_ref[n]
-    copies[0].wait()
-    rows = lax.broadcasted_iota(jnp.int32, (LEAVES, LEAF), 0)
-    targets = jnp.where(rows == pairs_ref[0:1, :], 1.0, 0.0).astype(BF)
-    sources = jnp.where(rows == pairs_ref[1:2, :], 1.0, 0.0).astype(BF)
-    sources = jnp.concatenate([sources, sources], axis=0)
-    for k in range(COLS):
-        hi, lo = halves(by_column[k])
-        both = jnp.concatenate([hi, lo], axis=0)
-        picked[k] = lax.dot_general(
-            both, sources, (((0,), (0,)), ((), ())), preferred_element_type=F32
-        )
-    copies[1].wait()
-    step = 8
-
-    def some_rows(i, carry):
-        at = pl.multiple_of(i * step, step)
-        block = coupling_ref[pl.ds(at, step)].astype(F32)
-        for k in range(COLS):
-            terms[k, pl.ds(at, step), :] = jnp.sum(block * picked[k][None], axis=1)
-        return carry
-
-    lax.fori_loop(0, RANK // step, some_rows, 0)
-    for k in range(COLS):
-        hi, lo = halves(terms[k])
-        fields[:, k, :] = mm_nt(targets, hi) + mm_nt(targets, lo)
-    copies[2].wait()
-    for n in range(LEAVES):
-        hi, lo = halves(fields[n])
-        both = mm(jnp.concatenate([hi, lo], axis=0), basis_ref[n])
-        out_ref[:, n * LEAF : (n + 1) * LEAF] = both[:COLS] + both[COLS:]
-
-
 def point_features(points):
     p = points.astype(F32)
     x, y, z = p[0:1], p[1:2], p[2:3]
@@ -181,7 +148,7 @@
     s1 = rest.astype(BF).astype(F32)
     s2 = rest - s1
     one = jnp.ones_like(square)
-    zero = jnp.zeros((7, LEAF), F32)
+    zero = jnp.zeros((7, points.shape[1]), F32)
     source = jnp.concatenate([x, y, z, one, one, one, s0, s1, s2, zero], axis=0)
     target = jnp.concatenate(
         [-2.0 * x, -2.0 * y, -2.0 * z, s0, s1, s2, one, one, one, zero], axis=0
@@ -189,33 +156,65 @@
     return source, target
 
 
-def near_kernel(
-    device_ref, pairs_ref, sorted_ref, points_ref, inner_ref, across_ref, far_ref, out_ref, rhs, source, target, acc
+def local_kernel(
+    device_ref, near_ref, far_ref, after_ref, coef_ref, coupling_ref, basis_ref, sorted_ref, points_ref, inner_ref, across_ref, out_ref,
+    by_pair, spread, far, rhs, source, target, near
 ):
+    del after_ref
+    rows = lax.broadcasted_iota(jnp.int32, (LEAF, LEAF), 0)
+    columns = lax.broadcasted_iota(jnp.int32, (LEAF, LEAF), 1)
+    identity = jnp.where(rows == columns, 1.0, 0.0).astype(BF)
+    for a in range(RANK // 2):
+        two = jnp.concatenate([coupling_ref[a], coupling_ref[a + RANK // 2]], axis=0)
+        by_pair[a * LEAF : (a + 1) * LEAF, :] = mm_nt(identity, two)
+    zero = jnp.zeros((2 * COLS, RANK), BF)
+    for n in range(LEAVES):
+        hi, lo = halves(coef_ref[n])
+        both = jnp.concatenate([hi, lo], axis=0)
+        spread[n] = jnp.concatenate(
+            [jnp.concatenate([both, zero], axis=1), jnp.concatenate([zero, both], axis=1)], axis=0
+        )
+    far[...] = jnp.zeros_like(far)
+    near[...] = jnp.zeros_like(near)
+
     even = jnp.bitwise_and(device_ref[0], 1) == 0
-    inner, across = inner_ref[...], across_ref[...]
-
-    def prepare(n, columns, points):
-        rhs[n] = columns
-        of_source, of_target = point_features(points)
-        source[n] = of_source.T.astype(BF)
-        target[n] = of_target.astype(BF)
-
-    prepare(jnp.where(even, LEAVES + 1, 0), inner[:COLS], inner[COLS:])
-    prepare(jnp.where(even, 0, LEAVES + 1), across[:COLS], across[COLS:])
+    inner, across = inner_ref[...].astype(F32), across_ref[...].astype(F32)
+    left = jnp.where(even, across, inner).astype(BF)
+    right = jnp.where(even, inner, across).astype(BF)
+    columns = jnp.concatenate([left[:COLS], sorted_ref[...], right[:COLS]], axis=1)
+    points = jnp.concatenate([left[COLS:], points_ref[...], right[COLS:]], axis=1)
+    of_source, of_target = point_features(points)
+    of_target = of_target.astype(BF)
+    for n in range(LEAVES + 2):
+        here = slice(n * LEAF, (n + 1) * LEAF)
+        rhs[n] = columns[:, here]
+        source[n] = of_source[:, here].T.astype(BF)
+        target[n] = of_target[:, here]
+
+    def far_pair(j):
+        to, of = far_ref[0, j], far_ref[1, j]
+        rows = by_pair[pl.ds(j, RANK // 2, stride=LEAF), :].astype(BF)
+        far[to] += mm_nt(rows, spread[of])
+
+    def near_pair(j):
+        to, of = near_ref[0, j], near_ref[1, j]
+        squared = jnp.maximum(mm(source[of], target[to + 1]) * (3.0 * LOG2E * LOG2E), 1e-30)
+        scaled = squared * lax.rsqrt(squared)
+        values = ((0.125 + (0.125 / LOG2E) * scaled) * jnp.exp2(-scaled)).astype(BF)
+        near[to] += mm(rhs[of], values)
+
+    for j in range(8 * LEAVES):
+        far_pair(j)
+    for j in range(3 * LEAVES):
+        near_pair(j)
     for n in range(LEAVES):
-        here = slice(n * LEAF, (n + 1) * LEAF)
-        prepare(n + 1, sorted_ref[:, here], points_ref[:, here])
-        acc[n] = far_ref[:, here]
-
-    for j in range(LEAVES * 3):
-        to, of = pairs_ref[0, j], pairs_ref[1, j]
-        squared = jnp.maximum(mm(source[of], target[to + 1]), 0.0)
-        scaled = jnp.sqrt(3.0 * squared)
-        values = ((0.125 + 0.125 * scaled) * jnp.exp(-scaled)).astype(BF)
-        acc[to] += mm(rhs[of], values)
-    for n in range(LEAVES):
-        out_ref[:, n * LEAF : (n + 1) * LEAF] = acc[n]
+        x = far[n].T
+        field = jnp.concatenate(
+            [x[:COLS] + x[COLS : 2 * COLS], x[2 * COLS : 3 * COLS] + x[3 * COLS :]], axis=1
+        )
+        hi, lo = halves(field)
+        both = mm(jnp.concatenate([hi, lo], axis=0), basis_ref[n])
+        out_ref[:, n * LEAF : (n + 1) * LEAF] = near[n] + (both[:COLS] + both[COLS:])
 
 
 def times(a, b):
@@ -280,17 +279,18 @@
             )
 
 
-def unpacked(message):
-    x = jnp.concatenate([message[:, :RANK], message[:, RANK:]], axis=0)
-    hi, lo = halves(x)
+def unpacked(messages):
+    x = jnp.concatenate([m[:, :RANK] for m in messages], axis=1)
+    y = jnp.concatenate([m[:, RANK:] for m in messages], axis=1)
+    hi, lo = halves(jnp.concatenate([x, y], axis=0))
     return jnp.concatenate([hi, lo], axis=0)
 
 
 def middle_kernel(device_ref, received_ref, weight_ref, message_ref, field_ref):
     device = device_ref[0]
-    total = jnp.zeros((2 * COLS, 6 * RANK), F32)
-    for s in range(NLOW):
-        total = total + mm(unpacked(received_ref[s]), weight_ref[s])
+    total = mm(
+        unpacked([received_ref[s] for s in range(NLOW)]), weight_ref[...].reshape(NLOW * RANK, 6 * RANK)
+    )
     total = total[:COLS] + total[COLS:]
     node = total[:, :RANK] + total[:, RANK : 2 * RANK]
     fields = total[:, 2 * RANK : 4 * RANK] + total[:, 4 * RANK :]
@@ -308,41 +308,36 @@
     )
     device = device_ref[0]
     high, core = jnp.right_shift(device, LOW + 1), jnp.bitwise_and(device, 1)
-    total = jnp.zeros((2 * COLS, 2 * RANK), F32)
-    for g in range(NHIGH):
-        total = total + mm(unpacked(received_ref[2 * g] + received_ref[2 * g + 1]), weight_ref[g])
+    total = mm(
+        unpacked([received_ref[2 * g] + received_ref[2 * g + 1] for g in range(NHIGH)]),
+        weight_ref[...].reshape(NHIGH * RANK, 2 * RANK),
+    )
     total = total[:COLS] + total[COLS:]
     sibling = received_ref[high * 2 + 1 - core]
     field = field_ref[...] + (total[:, :RANK] + total[:, RANK:])
     field = field + jnp.concatenate([sibling[:, :RANK], sibling[:, RANK:]], axis=0)
     hi, lo = halves(field)
-    field = jnp.concatenate([hi, lo], axis=0)
-    result = jnp.zeros((LEAVES * 2 * COLS, LEAF), F32)
     for copy in copies:
         copy.wait()
+    fields = mm_nt(
+        jnp.concatenate([hi, lo], axis=0), transfer_ref[...].reshape(LEAVES * RANK, RANK)
+    )
+    hi, lo = halves(fields[:COLS] + fields[COLS:])
+    both = jnp.concatenate([hi, lo], axis=0)
+    values = [mm(both[:, n * RANK : (n + 1) * RANK], basis_ref[n]) for n in range(LEAVES)]
+    values = jnp.concatenate([v[:COLS] + v[COLS:] for v in values], axis=1) + partial_ref[...]
+    hi, lo = halves(values)
+    both = jnp.concatenate([hi, lo], axis=0)
     order = order_ref[...]
-    for start in range(0, PTS, 2 * LEAF):
-        pieces = []
-        for n in range(start // LEAF, start // LEAF + 2):
-            leaf_field = mm_nt(field, transfer_ref[n])
-            hi, lo = halves(leaf_field[:COLS] + leaf_field[COLS:])
-            both = mm(jnp.concatenate([hi, lo], axis=0), basis_ref[n])
-            pieces.append(both[:COLS] + both[COLS:])
-        values = jnp.concatenate(pieces, axis=1) + partial_ref[:, start : start + 2 * LEAF]
-        hi, lo = halves(values)
-        both = jnp.concatenate([hi, lo], axis=0)
-        piece = order[:, start : start + 2 * LEAF]
-        block = jnp.right_shift(piece, 7)
-        masked = jnp.concatenate(
-            [both * jnp.where(block == h, 1.0, 0.0).astype(BF) for h in range(LEAVES)], axis=0
-        )
-        result = result + mm_nt(masked, low_onehot(piece))
-    for h in range(LEAVES):
+    block = jnp.right_shift(order, 8)
+    masked = [both * jnp.where(block == h, 1.0, 0.0).astype(BF) for h in range(BLOCKS)]
+    result = mm_nt(jnp.concatenate(masked, axis=0), low_onehot(order))
+    for h in range(BLOCKS):
         at = h * 2 * COLS
-        out_ref[:, h * LEAF : (h + 1) * LEAF] = result[at : at + COLS] + result[at + COLS : at + 2 * COLS]
-
-
-def call(kernel, out, inputs, buffers=(), scratch=(), flops=0, transcendentals=0):
+        out_ref[:, h * WIDE : (h + 1) * WIDE] = result[at : at + COLS] + result[at + COLS : at + 2 * COLS]
+
+
+def call(kernel, out, inputs, buffers=(), scratch=(), flops=0, transcendentals=0, vmem=16):
     shapes = [jax.ShapeDtypeStruct(s, t) for s, t in out]
     scratches = [pltpu.VMEM(s, t) for s, t in buffers] + [pltpu.VMEM(s, t) for s, t in scratch]
     if buffers:
@@ -353,7 +348,7 @@
         in_specs=[space for space, _ in inputs],
         out_specs=[VMEM] * len(out),
         scratch_shapes=scratches,
-        compiler_params=pltpu.CompilerParams(vmem_limit_bytes=16 << 20),
+        compiler_params=pltpu.CompilerParams(vmem_limit_bytes=vmem << 20),
         cost_estimate=pl.CostEstimate(
             flops=flops, bytes_accessed=1 << 20, transcendentals=transcendentals
         ),
@@ -383,6 +378,7 @@
         [((COLS, PTS), BF), ((LEAVES, COLS, RANK), F32), ((NLOW, 8, 2 * RANK), F32)],
         [(HBM, order), (HBM, right_sides), (HBM, leaf_basis), (HBM, leaf_transfer)],
         buffers=[order_like, (right_sides.shape, F32), basis_like, transfer_like],
+        vmem=62,
         flops=1 << 28,
     )
     low_groups = [
@@ -418,38 +414,32 @@
     )
     received = lax.all_to_all(message, "leaf", 0, 0, axis_index_groups=high_groups, tiled=True)
     coupling = far_coupling.transpose(1, 2, 0)
-    (far,) = call(
-        far_kernel,
-        [((COLS, PTS), F32)],
-        [(ANY, field), (VMEM, coef), (HBM, far_pairs), (HBM, coupling), (HBM, leaf_basis)],
-        buffers=[(far_pairs.shape, jnp.int32), (coupling.shape, BF), basis_like],
-        scratch=[
-            ((COLS, LEAVES, RANK), F32),
-            ((COLS, RANK, LEAF), F32),
-            ((COLS, RANK, LEAF), F32),
-            ((LEAVES, COLS, RANK), F32),
-        ],
-        flops=1 << 31,
-    )
     (partial,) = call(
-        near_kernel,
+        local_kernel,
         [((COLS, PTS), F32)],
         [
             (SMEM, device),
             (SMEM, near_pairs),
+            (SMEM, far_pairs),
+            (ANY, field),
+            (VMEM, coef),
+            (VMEM, coupling),
+            (VMEM, leaf_basis),
             (VMEM, sorted_rhs),
             (VMEM, points),
             (VMEM, inner),
             (VMEM, across),
-            (VMEM, far),
         ],
         scratch=[
+            ((LEAF * RANK // 2, 2 * RANK), F32),
+            ((LEAVES, 4 * COLS, 2 * RANK), BF),
+            ((LEAVES, RANK // 2, 4 * COLS), F32),
             ((LEAVES + 2, COLS, LEAF), BF),
             ((LEAVES + 2, LEAF, COLS), BF),
             ((LEAVES + 2, COLS, LEAF), BF),
             ((LEAVES, COLS, LEAF), F32),
         ],
-        flops=1 << 31,
+        flops=1 << 32,
         transcendentals=1 << 21,
     )
     (product,) = call(

time: 58.7 us -> 50.4 us (0.86)
  Pallas kernels: 19.6 us -> 12.7 us
  local copies, waits for them, and re-layouts: 5.51 us -> 1.34 us
  waiting for transfers between devices: 1.44 us -> 4.22 us
    pallas_call x7 -> x6, Pallas kernels: 19.6 us -> 12.7 us  [call(): pl.pallas_call(kernel, out_shape=shapes, in_specs=[space for space, _ in...]
    unnamed x26 -> x22, local copies, waits for them, and re-layouts: 5.51 us -> 1.34 us
    all_to_all x1, waiting for transfers between devices: 0.01 us -> 2.66 us  [per_device(): lax.all_to_all(message, 'leaf', 0, 0, axis_index_groups=high_groups, tile...]
  transfers between devices with their start and end apart: 4 -> 4, of which waited for: 1 -> 2; matrix products, arithmetic and copies ran while one was open for 0% -> 0% of each run, Pallas kernels for 20% -> 17%
where the time goes in v3:
time: 50.4 us; the launch traced here: 50 us
  starting transfers between devices  31.5 us (62%)
  Pallas kernels  12.7 us (25%)
  waiting for transfers between devices  4.22 us (8%)
  local copies, waits for them, and re-layouts  1.34 us (3%)
    all_to_all x1, starting transfers between devices, per_device(): lax.all_to_all(message, 'leaf', 0, 0, axis_index_groups=low_groups, tiled...  15.9 us
    pallas_call x6, Pallas kernels, call(): pl.pallas_call(kernel, out_shape=shapes, in_specs=[space for space, _ in...  12.7 us
    all_to_all x1, starting transfers between devices, per_device(): lax.all_to_all(message, 'leaf', 0, 0, axis_index_groups=high_groups, tile...  9.32 us
    ppermute x1, starting transfers between devices, per_device(): across = lax.ppermute(across, 'leaf', pairs + [(j, i) for i, j in pairs])  3.45 us
    ppermute x1, starting transfers between devices, per_device(): inner = lax.ppermute(inner, 'leaf', [(i, i ^ 1) for i in range(count)])  2.86 us
    all_to_all x1, waiting for transfers between devices, per_device(): lax.all_to_all(message, 'leaf', 0, 0, axis_index_groups=high_groups, tile...  2.66 us
    all_to_all x1, waiting for transfers between devices, per_device(): lax.all_to_all(message, 'leaf', 0, 0, axis_index_groups=low_groups, tiled...  1.55 us
    unnamed x22, local copies, waits for them, and re-layouts  1.34 us
  transfers between devices with their start and end apart: 4, of which 2 were waited for; matrix products, arithmetic and copies ran while one was open for 0% of the time, Pallas kernels for 17%

profile of v3, /device:TPU:1, one launch (start us, length us, event | category | flops | bytes accessed | tf_op | source)
XLA Modules:
  0.0 50.0 jit_solution(10298003675886247746)
XLA Ops:
  0.0 2.5 %shard_map.100 = (bf16[16,2048]{1,0:T(8,128)(2,1)}, f32[16,16,64]{2,1,0:T(8,128)}, f32[16,8,128]{2,1,0:T(8,128)}) custom-call(s32[1,2048]{1,0:T(1,128)} %bitcast.3, f32[16,2048]{1,0:T(8,128)} %rhs_hbm.1, bf16[16,64,128]{2,1,0:T(8,128)(2,1)} %basis_hbm.3, bf16[16,64,64]{2,1,0:T(8,128)(2,1)} %transfer_hbm.5), custom_call_target="tpu_custom_call" | custom-call | flops 268435456 | bytes 1048576 | tf_op jit(solution)/shard_map/pallas_call | solution.py:345
  2.5 0.0 copy-start.6
  2.5 0.0 copy-start.10
  2.5 15.9 %all-to-all-start = ((f32[16,8,128]{2,1,0:T(8,128)}), f32[16,8,128]{2,1,0:T(8,128)S(1)}, u32[]{:S(2)}, u32[]{:S(2)}) async-start(f32[16,8,128]{2,1,0:T(8,128)} %get-tuple-element.15), calls=%async_computation | async-start | bytes 131072 | tf_op jit(solution)/shard_map/all_to_all | solution.py:390
  18.4 0.0 copy-start.2
  18.4 0.0 copy-done.6
  18.4 0.0 copy-done.10
  18.4 0.7 %copy-done.2 = s32[2048]{0:T(1024)S(1)} copy-done((s32[2048]{0:T(1024)S(1)}, s32[2048]{0:T(1024)}, u32[]{:S(2)}) %copy-start.2) | copy-done | bytes 8216
  19.1 0.0 copy-start.4
  19.1 0.0 copy-start.5
  19.1 0.4 shard_map.103
  19.5 2.9 %collective-permute-start = (bf16[32,128]{1,0:T(8,128)(2,1)S(1)}, bf16[32,128]{1,0:T(8,128)(2,1)S(1)}, u32[]{:S(2)}, u32[]{:S(2)}) collective-permute-start(bf16[32,128]{1,0:T(8,128)(2,1)S(1)} %get-tuple-element.23), channel_id=1, source_target_pairs={{0,1},{1,0},{2,3},{3,2},{4,5},{5,4},{6,7},{7,6},{8,9},{9,8},{10,11... | collective-permute-start | bytes 24584 | tf_op jit(solution)/shard_map/ppermute | solution.py:399
  22.3 3.4 %collective-permute-start.1 = (bf16[32,128]{1,0:T(8,128)(2,1)S(1)}, bf16[32,128]{1,0:T(8,128)(2,1)S(1)}, u32[]{:S(2)}, u32[]{:S(2)}) collective-permute-start(bf16[32,128]{1,0:T(8,128)(2,1)S(1)} %get-tuple-element.24), channel_id=1, source_target_pairs={{1,2},{3,4},{5,6},{7,8},{9,10},{11,12},{13,14},{15,16},{17,18},{19... | collective-permute-start | bytes 24584 | tf_op jit(solution)/shard_map/ppermute | solution.py:401
  25.8 0.0 copy-done.4
  25.8 0.0 copy-done.5
  25.8 0.0 copy-start.3
  25.8 2.6 %shard_map.101 = (bf16[16,64,384]{2,1,0:T(8,128)(2,1)S(1)}, bf16[16,64,128]{2,1,0:T(8,128)(2,1)S(1)}) custom-call(s32[1]{0:T(128)} %bitcast.device_ref, bf16[9,2,64,64]{3,2,1,0:T(8,128)(2,1)S(1)} %copy-done.4, bf16[9,2,64,64]{3,2,1,0:T(8,128)(2,1)S(1)} %copy-done.5), custom_call_target="tpu_custom_call" | custom-call | flops 1073741824 | bytes 1048576 | tf_op jit(solution)/shard_map/pallas_call | solution.py:345
  28.4 1.6 %all-to-all-done.received_ref = f32[16,8,128]{2,1,0:T(8,128)S(1)} async-done(((f32[16,8,128]{2,1,0:T(8,128)}), f32[16,8,128]{2,1,0:T(8,128)S(1)}, u32[]{:S(2)}, u32[]{:S(2)}) %all-to-all-start) | async-done | bytes 65568 | tf_op jit(solution)/shard_map/all_to_all | solution.py:390
  30.0 1.1 %shard_map.102 = (f32[32,8,128]{2,1,0:T(8,128)}, f32[16,64]{1,0:T(8,128)S(1)}) custom-call(s32[1]{0:T(128)} %bitcast.device_ref, f32[16,8,128]{2,1,0:T(8,128)S(1)} %all-to-all-done.received_ref, bf16[16,64,384]{2,1,0:T(8,128)(2,1)S(1)} %get-tuple-element.16.weight_ref), custom_call_target="tpu_custom_call" | custom-call | flops 134217728 | bytes 1048576 | tf_op jit(solution)/shard_map/pallas_call | solution.py:345
  31.0 9.3 %all-to-all-start.1 = ((f32[32,8,128]{2,1,0:T(8,128)}), f32[32,8,128]{2,1,0:T(8,128)S(1)}, u32[]{:S(2)}, u32[]{:S(2)}) async-start(f32[32,8,128]{2,1,0:T(8,128)} %get-tuple-element.17), calls=%async_computation.1 | async-start | bytes 262144 | tf_op jit(solution)/shard_map/all_to_all | solution.py:415
  40.4 0.0 collective-permute-done.inner_ref
  40.4 0.0 collective-permute-done.1.across_ref
  40.4 0.0 copy-start.7
  40.4 0.0 copy-done.3
  40.4 0.0 copy-done.9
  40.4 0.0 copy-done
  40.4 0.0 copy-done.8
  40.4 0.6 %copy-done.7 = s32[2,48]{1,0:T(2,128)S(1)} copy-done((s32[2,48]{1,0:T(2,128)S(1)}, s32[2,48]{1,0:T(2,128)}, u32[]{:S(2)}) %copy-start.7) | copy-done | bytes 408
  41.1 4.3 %shard_map.104.partial_ref = f32[16,2048]{1,0:T(8,128)S(1)} custom-call(s32[1]{0:T(128)} %bitcast.device_ref, s32[2,48]{1,0:T(2,128)S(1)} %copy-done.7, s32[2,128]{1,0:T(2,128)S(1)} %copy-done.8, f32[16,64]{1,0:T(8,128)S(1)} %get-tuple-element.19.after_ref.field_ref, f32[16,16,64]{2,1,0:T(8,128)S(1)} %copy-done.9, bf16[64,64,128]{2,1,0:T(8,128)(2,1)S(1)} %bitcast.6, ...), custom_call_target="tpu_custom_call" | custom-call | flops 4294967296 | bytes 1048576 | tf_op jit(solution)/shard_map/pallas_call | solution.py:345
  45.4 2.7 %all-to-all-done.1.received_ref = f32[32,8,128]{2,1,0:T(8,128)S(1)} async-done(((f32[32,8,128]{2,1,0:T(8,128)}), f32[32,8,128]{2,1,0:T(8,128)S(1)}, u32[]{:S(2)}, u32[]{:S(2)}) %all-to-all-start.1) | async-done | bytes 131104 | tf_op jit(solution)/shard_map/all_to_all | solution.py:415
  48.1 0.0 copy-done.1
  48.1 1.9 %shard_map.105 = f32[16,2048]{1,0:T(8,128)} custom-call(s32[1]{0:T(128)} %bitcast.device_ref, f32[32,8,128]{2,1,0:T(8,128)S(1)} %all-to-all-done.1.received_ref, bf16[16,64,128]{2,1,0:T(8,128)(2,1)S(1)} %get-tuple-element.18.weight_ref, f32[16,64]{1,0:T(8,128)S(1)} %get-tuple-element.19.after_ref.field_ref, f32[16,2048]{1,0:T(8,128)S(1)} %shard_map.104.partial_ref, ...), custom_call_target="tpu_custom_call" | custom-call | flops 268435456 | bytes 1048576 | tf_op jit(solution)/shard_map/pallas_call | solution.py:345
  (4 shorter events, 0.0 us)
Async XLA Ops:
  2.5 15.9 %copy-start.6 = (bf16[3,2048]{1,0:T(4,128)(2,1)S(1)}, bf16[3,2048]{1,0:T(4,128)(2,1)}, u32[]{:S(2)}) copy-start(bf16[3,2048]{1,0:T(4,128)(2,1)} %coords_hbm.1) | copy-start | bytes 36868
  2.5 15.9 %copy-start.10 = (bf16[16,2048]{1,0:T(8,128)(2,1)S(1)}, bf16[16,2048]{1,0:T(8,128)(2,1)}, u32[]{:S(2)}) copy-start(bf16[16,2048]{1,0:T(8,128)(2,1)} %get-tuple-element.21.sorted_ref) | copy-start | bytes 196612
  2.5 27.5 %all-to-all-start = ((f32[16,8,128]{2,1,0:T(8,128)}), f32[16,8,128]{2,1,0:T(8,128)S(1)}, u32[]{:S(2)}, u32[]{:S(2)}) async-start(f32[16,8,128]{2,1,0:T(8,128)} %get-tuple-element.15), calls=%async_computation | async-start | bytes 131072 | tf_op jit(solution)/shard_map/all_to_all | solution.py:390
  18.4 0.7 %copy-start.2 = (s32[2048]{0:T(1024)S(1)}, s32[2048]{0:T(1024)}, u32[]{:S(2)}) copy-start(s32[2048]{0:T(1024)} %param.12) | copy-start | bytes 24580
  19.1 6.7 %copy-start.4 = (bf16[9,2,64,64]{3,2,1,0:T(8,128)(2,1)S(1)}, bf16[9,2,64,64]{3,2,1,0:T(8,128)(2,1)}, u32[]{:S(2)}) copy-start(bf16[9,2,64,64]{3,2,1,0:T(8,128)(2,1)} %transfer_hbm.4) | copy-start | bytes 442372
  19.1 6.7 %copy-start.5 = (bf16[9,2,64,64]{3,2,1,0:T(8,128)(2,1)S(1)}, bf16[9,2,64,64]{3,2,1,0:T(8,128)(2,1)}, u32[]{:S(2)}) copy-start(bf16[9,2,64,64]{3,2,1,0:T(8,128)(2,1)} %coupling_hbm.1) | copy-start | bytes 442372
  19.5 20.9 %collective-permute-start = (bf16[32,128]{1,0:T(8,128)(2,1)S(1)}, bf16[32,128]{1,0:T(8,128)(2,1)S(1)}, u32[]{:S(2)}, u32[]{:S(2)}) collective-permute-start(bf16[32,128]{1,0:T(8,128)(2,1)S(1)} %get-tuple-element.23), channel_id=1, source_target_pairs={{0,1},{1,0},{2,3},{3,2},{4,5},{5,4},{6,7},{7,6},{8,9},{9,8},{10,11... | collective-permute-start | bytes 24584 | tf_op jit(solution)/shard_map/ppermute | solution.py:399
  22.3 18.0 %collective-permute-start.1 = (bf16[32,128]{1,0:T(8,128)(2,1)S(1)}, bf16[32,128]{1,0:T(8,128)(2,1)S(1)}, u32[]{:S(2)}, u32[]{:S(2)}) collective-permute-start(bf16[32,128]{1,0:T(8,128)(2,1)S(1)} %get-tuple-element.24), channel_id=1, source_target_pairs={{1,2},{3,4},{5,6},{7,8},{9,10},{11,12},{13,14},{15,16},{17,18},{19... | collective-permute-start | bytes 24584 | tf_op jit(solution)/shard_map/ppermute | solution.py:401
  25.8 14.6 %copy-start.3 = (bf16[128,64,64]{0,2,1:T(8,128)(2,1)S(1)}, bf16[128,64,64]{0,2,1:T(8,128)(2,1)}, u32[]{:S(2)}) copy-start(bf16[128,64,64]{0,2,1:T(8,128)(2,1)} %param.15) | copy-start | bytes 3145732
  30.0 10.4 %copy-start.9 = (f32[16,16,64]{2,1,0:T(8,128)S(1)}, f32[16,16,64]{2,1,0:T(8,128)}, u32[]{:S(2)}) copy-start(f32[16,16,64]{2,1,0:T(8,128)} %get-tuple-element.20.coef_ref) | copy-start | bytes 196612
  31.0 9.4 %copy-start = (bf16[16,64,128]{2,1,0:T(8,128)(2,1)S(1)}, bf16[16,64,128]{2,1,0:T(8,128)(2,1)}, u32[]{:S(2)}) copy-start(bf16[16,64,128]{2,1,0:T(8,128)(2,1)} %basis_hbm.3) | copy-start | bytes 786436
  31.0 9.4 %copy-start.8 = (s32[2,128]{1,0:T(2,128)S(1)}, s32[2,128]{1,0:T(2,128)}, u32[]{:S(2)}) copy-start(s32[2,128]{1,0:T(2,128)} %far_ref.1) | copy-start | bytes 3076
  31.0 17.0 %all-to-all-start.1 = ((f32[32,8,128]{2,1,0:T(8,128)}), f32[32,8,128]{2,1,0:T(8,128)S(1)}, u32[]{:S(2)}, u32[]{:S(2)}) async-start(f32[32,8,128]{2,1,0:T(8,128)} %get-tuple-element.17), calls=%async_computation.1 | async-start | bytes 262144 | tf_op jit(solution)/shard_map/all_to_all | solution.py:415
  40.4 0.7 %copy-start.7 = (s32[2,48]{1,0:T(2,128)S(1)}, s32[2,48]{1,0:T(2,128)}, u32[]{:S(2)}) copy-start(s32[2,48]{1,0:T(2,128)} %near_ref.1) | copy-start | bytes 1156
  41.1 7.0 %copy-start.1 = (bf16[16,64,64]{2,1,0:T(8,128)(2,1)S(1)}, bf16[16,64,64]{2,1,0:T(8,128)(2,1)}, u32[]{:S(2)}) copy-start(bf16[16,64,64]{2,1,0:T(8,128)(2,1)} %transfer_hbm.5) | copy-start | bytes 393220

commit v4 on v3

--- a/solution.py
+++ b/solution.py
@@ -16,6 +16,9 @@
 PTS = LEAVES * LEAF
 LOW = 4
 HIGHS = 4
+WEIGHTS_FIRST = 4
+LEADER = 10
+MIDDLE = 9
 NLOW = 1 << LOW
 NHIGH = 1 << HIGHS
 LOG2E = 1.4426950408889634
@@ -83,9 +86,20 @@
     return copies
 
 
+def along_z(device):
+    return jnp.bitwise_and(jnp.right_shift(device, 1), NLOW - 1)
+
+
+def weights_first(device):
+    return jnp.logical_and(along_z(device) < WEIGHTS_FIRST, device != 0)
+
+
 def up_kernel(
-    order_hbm, rhs_hbm, basis_hbm, transfer_hbm, sorted_ref, coef_ref, message_ref, order_ref, rhs_ref, basis_ref, transfer_ref, sems
+    order_hbm, rhs_hbm, basis_hbm, transfer_hbm, top_transfer_hbm, top_coupling_hbm,
+    sorted_ref, coef_ref, message_ref, low_hbm, high_hbm,
+    order_ref, rhs_ref, basis_ref, transfer_ref, top_transfer_ref, top_coupling_ref, low_ref, high_ref, sems
 ):
+    device = lax.axis_index("leaf")
     copies = fetch(
         (order_hbm, rhs_hbm, basis_hbm, transfer_hbm),
         (order_ref, rhs_ref, basis_ref, transfer_ref),
@@ -116,8 +130,18 @@
     message = pack_message(root[:COLS] + root[COLS:])
     message_ref[...] = jnp.broadcast_to(message[None], message_ref.shape)
 
-
-def points_kernel(device_ref, coords_hbm, order_hbm, sorted_ref, near_ref, across_ref, points_ref, coords_ref, order_ref, sems):
+    @pl.when(weights_first(device))
+    def _():
+        for copy in fetch(
+            (top_transfer_hbm, top_coupling_hbm), (top_transfer_ref, top_coupling_ref), sems
+        ):
+            copy.wait()
+        form_weights(device, top_transfer_ref, top_coupling_ref, low_ref, high_ref)
+        for copy in fetch((low_ref, high_ref), (low_hbm, high_hbm), sems):
+            copy.wait()
+
+
+def points_kernel(coords_hbm, order_hbm, sorted_ref, near_ref, across_ref, points_ref, coords_ref, order_ref, sems):
     copies = fetch((coords_hbm, order_hbm), (coords_ref, order_ref), sems)
     for copy in copies:
         copy.wait()
@@ -126,7 +150,7 @@
         points_ref[:, start : start + 2 * LEAF] = piece
     head = jnp.concatenate([sorted_ref[:, 0:LEAF], points_ref[:, 0:LEAF]], axis=0)
     tail = jnp.concatenate([sorted_ref[:, PTS - LEAF :], points_ref[:, PTS - LEAF :]], axis=0)
-    even = jnp.bitwise_and(device_ref[0], 1) == 0
+    even = jnp.bitwise_and(lax.axis_index("leaf"), 1) == 0
 
     @pl.when(even)
     def _():
@@ -157,7 +181,7 @@
 
 
 def local_kernel(
-    device_ref, near_ref, far_ref, after_ref, coef_ref, coupling_ref, basis_ref, sorted_ref, points_ref, inner_ref, across_ref, out_ref,
+    near_ref, far_ref, after_ref, coef_ref, coupling_ref, basis_ref, sorted_ref, points_ref, inner_ref, across_ref, out_ref,
     by_pair, spread, far, rhs, source, target, near
 ):
     del after_ref
@@ -177,7 +201,7 @@
     far[...] = jnp.zeros_like(far)
     near[...] = jnp.zeros_like(near)
 
-    even = jnp.bitwise_and(device_ref[0], 1) == 0
+    even = jnp.bitwise_and(lax.axis_index("leaf"), 1) == 0
     inner, across = inner_ref[...].astype(F32), across_ref[...].astype(F32)
     left = jnp.where(even, across, inner).astype(BF)
     right = jnp.where(even, inner, across).astype(BF)
@@ -223,14 +247,18 @@
     return both[: a.shape[0]] + both[a.shape[0] :]
 
 
-def weights_kernel(device_ref, transfer_hbm, coupling_hbm, low_ref, high_ref, transfer_ref, coupling_ref, sems):
-    copies = fetch((transfer_hbm, coupling_hbm), (transfer_ref, coupling_ref), sems)
-    device = device_ref[0]
+def weights_kernel(transfer_ref, coupling_ref, low_ref, high_ref):
+    device = lax.axis_index("leaf")
+
+    @pl.when(jnp.logical_not(weights_first(device)))
+    def _():
+        form_weights(device, transfer_ref, coupling_ref, low_ref, high_ref)
+
+
+def form_weights(device, transfer_ref, coupling_ref, low_ref, high_ref):
     core = jnp.bitwise_and(device, 1)
-    low = jnp.bitwise_and(jnp.right_shift(device, 1), NLOW - 1)
+    low = along_z(device)
     high = jnp.right_shift(device, LOW + 1)
-    for copy in copies:
-        copy.wait()
     mine, other = transfer_ref[0, core], transfer_ref[0, 1 - core]
 
     hi, lo = halves(coupling_ref[0, 1 - core].astype(F32).T)
@@ -286,10 +314,11 @@
     return jnp.concatenate([hi, lo], axis=0)
 
 
-def middle_kernel(device_ref, received_ref, weight_ref, message_ref, field_ref):
-    device = device_ref[0]
+def middle_kernel(received_ref, early_ref, late_ref, message_ref, field_ref):
+    device = lax.axis_index("leaf")
+    weight = jnp.where(weights_first(device), early_ref[...], late_ref[...])
     total = mm(
-        unpacked([received_ref[s] for s in range(NLOW)]), weight_ref[...].reshape(NLOW * RANK, 6 * RANK)
+        unpacked([received_ref[(z - LEADER) % NLOW] for z in range(NLOW)]), weight.reshape(NLOW * RANK, 6 * RANK)
     )
     total = total[:COLS] + total[COLS:]
     node = total[:, :RANK] + total[:, RANK : 2 * RANK]
@@ -297,23 +326,25 @@
     field_ref[...] = fields[:, :RANK]
     message_ref[...] = jnp.broadcast_to(pack_message(node)[None], message_ref.shape)
     high, core = jnp.right_shift(device, LOW + 1), jnp.bitwise_and(device, 1)
-    message_ref[high * 2 + 1 - core] = pack_message(fields[:, RANK:])
+    at = jnp.bitwise_and(high - MIDDLE, NHIGH - 1)
+    message_ref[at * 2 + 1 - core] = pack_message(fields[:, RANK:])
 
 
 def down_kernel(
-    device_ref, received_ref, weight_ref, field_ref, partial_ref, transfer_hbm, basis_hbm, order_hbm, out_ref, transfer_ref, basis_ref, order_ref, sems
+    received_ref, early_ref, late_ref, field_ref, partial_ref, transfer_hbm, basis_hbm, order_hbm, out_ref, transfer_ref, basis_ref, order_ref, sems
 ):
     copies = fetch(
         (transfer_hbm, basis_hbm, order_hbm), (transfer_ref, basis_ref, order_ref), sems
     )
-    device = device_ref[0]
+    device = lax.axis_index("leaf")
     high, core = jnp.right_shift(device, LOW + 1), jnp.bitwise_and(device, 1)
+    places = [(g - MIDDLE) % NHIGH for g in range(NHIGH)]
     total = mm(
-        unpacked([received_ref[2 * g] + received_ref[2 * g + 1] for g in range(NHIGH)]),
-        weight_ref[...].reshape(NHIGH * RANK, 2 * RANK),
+        unpacked([received_ref[2 * g] + received_ref[2 * g + 1] for g in places]),
+        jnp.where(weights_first(device), early_ref[...], late_ref[...]).reshape(NHIGH * RANK, 2 * RANK),
     )
     total = total[:COLS] + total[COLS:]
-    sibling = received_ref[high * 2 + 1 - core]
+    sibling = received_ref[jnp.bitwise_and(high - MIDDLE, NHIGH - 1) * 2 + 1 - core]
     field = field_ref[...] + (total[:, :RANK] + total[:, RANK:])
     field = field + jnp.concatenate([sibling[:, :RANK], sibling[:, RANK:]], axis=0)
     hi, lo = halves(field)
@@ -338,7 +369,7 @@
 
 
 def call(kernel, out, inputs, buffers=(), scratch=(), flops=0, transcendentals=0, vmem=16):
-    shapes = [jax.ShapeDtypeStruct(s, t) for s, t in out]
+    shapes = [jax.ShapeDtypeStruct(o[0], o[1]) for o in out]
     scratches = [pltpu.VMEM(s, t) for s, t in buffers] + [pltpu.VMEM(s, t) for s, t in scratch]
     if buffers:
         scratches.append(pltpu.SemaphoreType.DMA((len(buffers),)))
@@ -346,7 +377,7 @@
         kernel,
         out_shape=shapes,
         in_specs=[space for space, _ in inputs],
-        out_specs=[VMEM] * len(out),
+        out_specs=[o[2] if len(o) > 2 else VMEM for o in out],
         scratch_shapes=scratches,
         compiler_params=pltpu.CompilerParams(vmem_limit_bytes=vmem << 20),
         cost_estimate=pl.CostEstimate(
@@ -368,48 +399,62 @@
     top_coupling,
 ):
     count = lax.axis_size("leaf")
-    device = lax.axis_index("leaf").astype(jnp.int32).reshape(1)
     order = tree_order.reshape(1, PTS)
     basis_like = (leaf_basis.shape, BF)
     transfer_like = (leaf_transfer.shape, BF)
     order_like = (order.shape, jnp.int32)
-    sorted_rhs, coef, message = call(
+    low_like = ((NLOW, RANK, 6 * RANK), BF)
+    high_like = ((NHIGH, RANK, 2 * RANK), BF)
+    top_like = (top_transfer.shape, BF)
+    sorted_rhs, coef, message, early_low, early_high = call(
         up_kernel,
-        [((COLS, PTS), BF), ((LEAVES, COLS, RANK), F32), ((NLOW, 8, 2 * RANK), F32)],
-        [(HBM, order), (HBM, right_sides), (HBM, leaf_basis), (HBM, leaf_transfer)],
-        buffers=[order_like, (right_sides.shape, F32), basis_like, transfer_like],
+        [
+            ((COLS, PTS), BF),
+            ((LEAVES, COLS, RANK), F32),
+            ((NLOW, 8, 2 * RANK), F32),
+            (*low_like, HBM),
+            (*high_like, HBM),
+        ],
+        [
+            (HBM, array)
+            for array in (order, right_sides, leaf_basis, leaf_transfer, top_transfer, top_coupling)
+        ],
+        buffers=[order_like, (right_sides.shape, F32), basis_like, transfer_like]
+        + [top_like, top_like, low_like, high_like],
         vmem=62,
         flops=1 << 28,
     )
     low_groups = [
-        [(g * NLOW + z) * 2 + c for z in range(NLOW)] for g in range(NHIGH) for c in range(2)
+        [(g * NLOW + (LEADER + z) % NLOW) * 2 + c for z in range(NLOW)]
+        for g in range(NHIGH)
+        for c in range(2)
     ]
     high_groups = [
-        [(g * NLOW + z) * 2 + c for g in range(NHIGH) for c in range(2)] for z in range(NLOW)
+        [((MIDDLE + g) % NHIGH * NLOW + z) * 2 + c for g in range(NHIGH) for c in range(2)]
+        for z in range(NLOW)
     ]
     received = lax.all_to_all(message, "leaf", 0, 0, axis_index_groups=low_groups, tiled=True)
 
     inner, across, points = call(
         points_kernel,
         [((2 * COLS, LEAF), BF), ((2 * COLS, LEAF), BF), ((COLS, PTS), BF)],
-        [(SMEM, device), (HBM, coordinates), (HBM, order), (VMEM, sorted_rhs)],
+        [(HBM, coordinates), (HBM, order), (VMEM, sorted_rhs)],
         buffers=[(coordinates.shape, BF), order_like],
         flops=1 << 28,
     )
     inner = lax.ppermute(inner, "leaf", [(i, i ^ 1) for i in range(count)])
     pairs = [(i, i + 1) for i in range(1, count - 1, 2)]
     across = lax.ppermute(across, "leaf", pairs + [(j, i) for i, j in pairs])
-    low_weight, high_weight = call(
+    late_low, late_high = call(
         weights_kernel,
-        [((NLOW, RANK, 6 * RANK), BF), ((NHIGH, RANK, 2 * RANK), BF)],
-        [(SMEM, device), (HBM, top_transfer), (HBM, top_coupling)],
-        buffers=[(top_transfer.shape, BF), (top_coupling.shape, BF)],
+        [low_like, high_like],
+        [(VMEM, top_transfer), (VMEM, top_coupling)],
         flops=1 << 30,
     )
     message, field = call(
         middle_kernel,
         [((2 * NHIGH, 8, 2 * RANK), F32), ((COLS, RANK), F32)],
-        [(SMEM, device), (VMEM, received), (VMEM, low_weight)],
+        [(VMEM, received), (VMEM, early_low), (VMEM, late_low)],
         flops=1 << 27,
     )
     received = lax.all_to_all(message, "leaf", 0, 0, axis_index_groups=high_groups, tiled=True)
@@ -418,7 +463,6 @@
         local_kernel,
         [((COLS, PTS), F32)],
         [
-            (SMEM, device),
             (SMEM, near_pairs),
             (SMEM, far_pairs),
             (ANY, field),
@@ -446,9 +490,9 @@
         down_kernel,
         [((COLS, PTS), F32)],
         [
-            (SMEM, device),
             (VMEM, received),
-            (VMEM, high_weight),
+            (VMEM, early_high),
+            (VMEM, late_high),
             (VMEM, field),
             (VMEM, partial),
             (HBM, leaf_transfer),

time: 50.4 us -> 44.4 us (0.88)
  waiting for transfers between devices: 4.22 us -> 0.01 us
  starting transfers between devices: 31.5 us -> 28.7 us
  Pallas kernels: 12.7 us -> 14.3 us
  local copies, waits for them, and re-layouts: 1.34 us -> 0.7 us
    all_to_all x1, waiting for transfers between devices: 2.66 us -> 0.01 us  [per_device(): lax.all_to_all(message, 'leaf', 0, 0, axis_index_groups=high_groups, tile...]
    all_to_all x1, starting transfers between devices: 15.9 us -> 13.8 us  [per_device(): lax.all_to_all(message, 'leaf', 0, 0, axis_index_groups=low_groups, tiled...]
    pallas_call x6, Pallas kernels: 12.7 us -> 14.3 us  [call(): pl.pallas_call(kernel, out_shape=shapes, in_specs=[space for space, _ in...]
    all_to_all x1, waiting for transfers between devices: 1.55 us -> 0.01 us  [per_device(): lax.all_to_all(message, 'leaf', 0, 0, axis_index_groups=low_groups, tiled...]
    all_to_all x1, starting transfers between devices: 9.32 us -> 8.64 us  [per_device(): lax.all_to_all(message, 'leaf', 0, 0, axis_index_groups=high_groups, tile...]
    unnamed x22 -> x26, local copies, waits for them, and re-layouts: 1.34 us -> 0.7 us
  transfers between devices with their start and end apart: 4 -> 4, of which waited for: 2 -> 0; matrix products, arithmetic and copies ran while one was open for 0% -> 0% of each run, Pallas kernels for 17% -> 13%
where the time goes in v4:
time: 44.4 us; the launch traced here: 44 us
  starting transfers between devices  28.7 us (65%)
  Pallas kernels  14.3 us (32%)
  local copies, waits for them, and re-layouts  0.7 us (2%)
    pallas_call x6, Pallas kernels, call(): pl.pallas_call(kernel, out_shape=shapes, in_specs=[space for space, _ in...  14.3 us
    all_to_all x1, starting transfers between devices, per_device(): lax.all_to_all(message, 'leaf', 0, 0, axis_index_groups=low_groups, tiled...  13.8 us
    all_to_all x1, starting transfers between devices, per_device(): lax.all_to_all(message, 'leaf', 0, 0, axis_index_groups=high_groups, tile...  8.64 us
    ppermute x1, starting transfers between devices, per_device(): inner = lax.ppermute(inner, 'leaf', [(i, i ^ 1) for i in range(count)])  3.13 us
    ppermute x1, starting transfers between devices, per_device(): across = lax.ppermute(across, 'leaf', pairs + [(j, i) for i, j in pairs])  3.13 us
  transfers between devices with their start and end apart: 4, of which 0 were waited for; matrix products, arithmetic and copies ran while one was open for 0% of the time, Pallas kernels for 13%

profile of v4, /device:TPU:1, one launch (start us, length us, event | category | flops | bytes accessed | tf_op | source)
XLA Modules:
  0.0 44.0 jit_solution(15045006120379664471)
XLA Ops:
  0.0 6.8 %shard_map.100 = (bf16[16,2048]{1,0:T(8,128)(2,1)}, f32[16,16,64]{2,1,0:T(8,128)}, f32[16,8,128]{2,1,0:T(8,128)}, bf16[16,64,384]{2,1,0:T(8,128)(2,1)}, bf16[16,64,128]{2,1,0:T(8,128)(2,1)}) custom-call(s32[1,2048]{1,0:T(1,128)} %bitcast.2, f32[16,2048]{1,0:T(8,128)} %rhs_hbm.1, bf16[16,64,128]{2,1,0:T(8,128)(2,1)} %basis_hbm.3, ...), custom_call_target="tpu_custom_call" | custom-call | flops 268435456 | bytes 1048576 | tf_op jit(solution)/shard_map/pallas_call | solution.py:376
  6.8 0.0 copy-start.6
  6.8 0.0 copy-start.9
  6.8 0.0 copy-start.10
  6.8 13.8 %all-to-all-start = ((f32[16,8,128]{2,1,0:T(8,128)}), f32[16,8,128]{2,1,0:T(8,128)S(1)}, u32[]{:S(2)}, u32[]{:S(2)}) async-start(f32[16,8,128]{2,1,0:T(8,128)} %get-tuple-element.17), calls=%async_computation | async-start | bytes 131072 | tf_op jit(solution)/shard_map/all_to_all | solution.py:436
  20.6 0.0 copy-done.6
  20.6 0.0 copy-done.9
  20.6 0.0 copy-done.10
  20.6 0.0 copy-start.3
  20.6 0.0 copy-start.4
  20.7 0.4 shard_map.103
  21.0 3.1 %collective-permute-start = (bf16[32,128]{1,0:T(8,128)(2,1)S(1)}, bf16[32,128]{1,0:T(8,128)(2,1)S(1)}, u32[]{:S(2)}, u32[]{:S(2)}) collective-permute-start(bf16[32,128]{1,0:T(8,128)(2,1)S(1)} %get-tuple-element.27), channel_id=1, source_target_pairs={{0,1},{1,0},{2,3},{3,2},{4,5},{5,4},{6,7},{7,6},{8,9},{9,8},{10,11... | collective-permute-start | bytes 24584 | tf_op jit(solution)/shard_map/ppermute | solution.py:445
  24.2 0.0 copy-start.2
  24.2 3.1 %collective-permute-start.1 = (bf16[32,128]{1,0:T(8,128)(2,1)S(1)}, bf16[32,128]{1,0:T(8,128)(2,1)S(1)}, u32[]{:S(2)}, u32[]{:S(2)}) collective-permute-start(bf16[32,128]{1,0:T(8,128)(2,1)S(1)} %get-tuple-element.28), channel_id=1, source_target_pairs={{1,2},{3,4},{5,6},{7,8},{9,10},{11,12},{13,14},{15,16},{17,18},{19... | collective-permute-start | bytes 24584 | tf_op jit(solution)/shard_map/ppermute | solution.py:447
  27.3 0.0 copy-done.3
  27.4 0.0 copy-start.7
  27.4 0.0 all-to-all-done.received_ref
  27.4 0.0 copy-done.2
  27.4 0.0 copy-start.8
  27.4 1.1 %shard_map.102 = (f32[32,8,128]{2,1,0:T(8,128)}, f32[16,64]{1,0:T(8,128)S(1)}) custom-call(f32[16,8,128]{2,1,0:T(8,128)S(1)} %all-to-all-done.received_ref, bf16[16,64,384]{2,1,0:T(8,128)(2,1)S(1)} %copy-done.2, bf16[16,64,384]{2,1,0:T(8,128)(2,1)S(1)} %get-tuple-element.19.late_ref), custom_call_target="tpu_custom_call" | custom-call | flops 134217728 | bytes 1048576 | tf_op jit(solution)/shard_map/pallas_call | solution.py:376
  28.5 8.6 %all-to-all-start.1 = ((f32[32,8,128]{2,1,0:T(8,128)}), f32[32,8,128]{2,1,0:T(8,128)S(1)}, u32[]{:S(2)}, u32[]{:S(2)}) async-start(f32[32,8,128]{2,1,0:T(8,128)} %get-tuple-element.20), calls=%async_computation.1 | async-start | bytes 262144 | tf_op jit(solution)/shard_map/all_to_all | solution.py:460
  37.1 0.0 collective-permute-done.inner_ref
  37.1 0.0 collective-permute-done.1.across_ref
  37.2 0.0 copy-start.11
  37.2 0.0 copy-done.7
  37.2 0.0 copy-done.8
  37.2 0.0 copy-done
  37.2 0.0 copy-done.12
  37.2 0.6 %copy-done.11 = s32[2,48]{1,0:T(2,128)S(1)} copy-done((s32[2,48]{1,0:T(2,128)S(1)}, s32[2,48]{1,0:T(2,128)}, u32[]{:S(2)}) %copy-start.11) | copy-done | bytes 408
  37.8 4.2 %shard_map.104.partial_ref = f32[16,2048]{1,0:T(8,128)S(1)} custom-call(s32[2,48]{1,0:T(2,128)S(1)} %copy-done.11, s32[2,128]{1,0:T(2,128)S(1)} %copy-done.12, f32[16,64]{1,0:T(8,128)S(1)} %get-tuple-element.23.after_ref.field_ref, f32[16,16,64]{2,1,0:T(8,128)S(1)} %copy-done.8, bf16[64,64,128]{2,1,0:T(8,128)(2,1)S(1)} %bitcast.5, ...), custom_call_target="tpu_custom_call" | custom-call | flops 4294967296 | bytes 1048576 | tf_op jit(solution)/shard_map/pallas_call | solution.py:376
  42.1 0.0 all-to-all-done.1.received_ref
  42.1 1.9 %shard_map.105 = f32[16,2048]{1,0:T(8,128)} custom-call(f32[32,8,128]{2,1,0:T(8,128)S(1)} %all-to-all-done.1.received_ref, bf16[16,64,128]{2,1,0:T(8,128)(2,1)S(1)} %copy-done.5, bf16[16,64,128]{2,1,0:T(8,128)(2,1)S(1)} %get-tuple-element.22.late_ref, f32[16,64]{1,0:T(8,128)S(1)} %get-tuple-element.23.after_ref.field_ref, ...), custom_call_target="tpu_custom_call" | custom-call | flops 268435456 | bytes 1048576 | tf_op jit(solution)/shard_map/pallas_call | solution.py:376
  (8 shorter events, 0.0 us)
Async XLA Ops:
  6.8 13.8 %copy-start.6 = (s32[2048]{0:T(1024)S(1)}, s32[2048]{0:T(1024)}, u32[]{:S(2)}) copy-start(s32[2048]{0:T(1024)} %param.12) | copy-start | bytes 24580
  6.8 13.8 %copy-start.9 = (bf16[16,2048]{1,0:T(8,128)(2,1)S(1)}, bf16[16,2048]{1,0:T(8,128)(2,1)}, u32[]{:S(2)}) copy-start(bf16[16,2048]{1,0:T(8,128)(2,1)} %get-tuple-element.25.sorted_ref) | copy-start | bytes 196612
  6.8 13.8 %copy-start.10 = (bf16[3,2048]{1,0:T(4,128)(2,1)S(1)}, bf16[3,2048]{1,0:T(4,128)(2,1)}, u32[]{:S(2)}) copy-start(bf16[3,2048]{1,0:T(4,128)(2,1)} %coords_hbm.1) | copy-start | bytes 36868
  6.8 20.6 %all-to-all-start = ((f32[16,8,128]{2,1,0:T(8,128)}), f32[16,8,128]{2,1,0:T(8,128)S(1)}, u32[]{:S(2)}, u32[]{:S(2)}) async-start(f32[16,8,128]{2,1,0:T(8,128)} %get-tuple-element.17), calls=%async_computation | async-start | bytes 131072 | tf_op jit(solution)/shard_map/all_to_all | solution.py:436
  20.6 6.7 %copy-start.3 = (bf16[9,2,64,64]{3,2,1,0:T(8,128)(2,1)S(1)}, bf16[9,2,64,64]{3,2,1,0:T(8,128)(2,1)}, u32[]{:S(2)}) copy-start(bf16[9,2,64,64]{3,2,1,0:T(8,128)(2,1)} %transfer_ref.1) | copy-start | bytes 442372
  20.6 6.7 %copy-start.4 = (bf16[9,2,64,64]{3,2,1,0:T(8,128)(2,1)S(1)}, bf16[9,2,64,64]{3,2,1,0:T(8,128)(2,1)}, u32[]{:S(2)}) copy-start(bf16[9,2,64,64]{3,2,1,0:T(8,128)(2,1)} %coupling_ref.1) | copy-start | bytes 442372
  21.0 16.1 %collective-permute-start = (bf16[32,128]{1,0:T(8,128)(2,1)S(1)}, bf16[32,128]{1,0:T(8,128)(2,1)S(1)}, u32[]{:S(2)}, u32[]{:S(2)}) collective-permute-start(bf16[32,128]{1,0:T(8,128)(2,1)S(1)} %get-tuple-element.27), channel_id=1, source_target_pairs={{0,1},{1,0},{2,3},{3,2},{4,5},{5,4},{6,7},{7,6},{8,9},{9,8},{10,11... | collective-permute-start | bytes 24584 | tf_op jit(solution)/shard_map/ppermute | solution.py:445
  24.2 3.2 %copy-start.2 = (bf16[16,64,384]{2,1,0:T(8,128)(2,1)S(1)}, bf16[16,64,384]{2,1,0:T(8,128)(2,1)}, u32[]{:S(2)}) copy-start(bf16[16,64,384]{2,1,0:T(8,128)(2,1)} %get-tuple-element.18.early_ref) | copy-start | bytes 2359300
  24.2 12.9 %collective-permute-start.1 = (bf16[32,128]{1,0:T(8,128)(2,1)S(1)}, bf16[32,128]{1,0:T(8,128)(2,1)S(1)}, u32[]{:S(2)}, u32[]{:S(2)}) collective-permute-start(bf16[32,128]{1,0:T(8,128)(2,1)S(1)} %get-tuple-element.28), channel_id=1, source_target_pairs={{1,2},{3,4},{5,6},{7,8},{9,10},{11,12},{13,14},{15,16},{17,18},{19... | collective-permute-start | bytes 24584 | tf_op jit(solution)/shard_map/ppermute | solution.py:447
  27.4 9.8 %copy-start.7 = (bf16[128,64,64]{0,2,1:T(8,128)(2,1)S(1)}, bf16[128,64,64]{0,2,1:T(8,128)(2,1)}, u32[]{:S(2)}) copy-start(bf16[128,64,64]{0,2,1:T(8,128)(2,1)} %param.15) | copy-start | bytes 3145732
  27.4 9.8 %copy-start.8 = (f32[16,16,64]{2,1,0:T(8,128)S(1)}, f32[16,16,64]{2,1,0:T(8,128)}, u32[]{:S(2)}) copy-start(f32[16,16,64]{2,1,0:T(8,128)} %get-tuple-element.24.coef_ref) | copy-start | bytes 196612
  28.5 8.7 %copy-start = (bf16[16,64,128]{2,1,0:T(8,128)(2,1)S(1)}, bf16[16,64,128]{2,1,0:T(8,128)(2,1)}, u32[]{:S(2)}) copy-start(bf16[16,64,128]{2,1,0:T(8,128)(2,1)} %basis_hbm.3) | copy-start | bytes 786436
  28.5 8.7 %copy-start.12 = (s32[2,128]{1,0:T(2,128)S(1)}, s32[2,128]{1,0:T(2,128)}, u32[]{:S(2)}) copy-start(s32[2,128]{1,0:T(2,128)} %far_ref.1) | copy-start | bytes 3076
  28.5 13.6 %all-to-all-start.1 = ((f32[32,8,128]{2,1,0:T(8,128)}), f32[32,8,128]{2,1,0:T(8,128)S(1)}, u32[]{:S(2)}, u32[]{:S(2)}) async-start(f32[32,8,128]{2,1,0:T(8,128)} %get-tuple-element.20), calls=%async_computation.1 | async-start | bytes 262144 | tf_op jit(solution)/shard_map/all_to_all | solution.py:460
  37.2 0.7 %copy-start.11 = (s32[2,48]{1,0:T(2,128)S(1)}, s32[2,48]{1,0:T(2,128)}, u32[]{:S(2)}) copy-start(s32[2,48]{1,0:T(2,128)} %near_ref.1) | copy-start | bytes 1156
  37.8 4.3 %copy-start.1 = (bf16[16,64,64]{2,1,0:T(8,128)(2,1)S(1)}, bf16[16,64,64]{2,1,0:T(8,128)(2,1)}, u32[]{:S(2)}) copy-start(bf16[16,64,64]{2,1,0:T(8,128)(2,1)} %transfer_hbm.3) | copy-start | bytes 393220
  37.8 4.3 %copy-start.5 = (bf16[16,64,128]{2,1,0:T(8,128)(2,1)S(1)}, bf16[16,64,128]{2,1,0:T(8,128)(2,1)}, u32[]{:S(2)}) copy-start(bf16[16,64,128]{2,1,0:T(8,128)(2,1)} %get-tuple-element.21.early_ref) | copy-start | bytes 786436

commit v5 on v4

--- a/solution.py
+++ b/solution.py
@@ -16,8 +16,8 @@
 PTS = LEAVES * LEAF
 LOW = 4
 HIGHS = 4
-WEIGHTS_FIRST = 4
-LEADER = 10
+WEIGHTS_FIRST = 3
+LEADER = 11
 MIDDLE = 9
 NLOW = 1 << LOW
 NHIGH = 1 << HIGHS

time: 44.4 us -> 43.3 us (0.975)
  starting transfers between devices: 28.7 us -> 27.7 us
    all_to_all x1, starting transfers between devices: 13.8 us -> 12.5 us  [per_device(): lax.all_to_all(message, 'leaf', 0, 0, axis_index_groups=low_groups, tiled...]
where the time goes in v5:
time: 43.3 us; the launch traced here: 43 us
  starting transfers between devices  27.7 us (64%)
  Pallas kernels  14.3 us (33%)
  local copies, waits for them, and re-layouts  0.7 us (2%)
    pallas_call x6, Pallas kernels, call(): pl.pallas_call(kernel, out_shape=shapes, in_specs=[space for space, _ in...  14.3 us
    all_to_all x1, starting transfers between devices, per_device(): lax.all_to_all(message, 'leaf', 0, 0, axis_index_groups=low_groups, tiled...  12.5 us
    all_to_all x1, starting transfers between devices, per_device(): lax.all_to_all(message, 'leaf', 0, 0, axis_index_groups=high_groups, tile...  8.96 us
    ppermute x1, starting transfers between devices, per_device(): inner = lax.ppermute(inner, 'leaf', [(i, i ^ 1) for i in range(count)])  3.16 us
    ppermute x1, starting transfers between devices, per_device(): across = lax.ppermute(across, 'leaf', pairs + [(j, i) for i, j in pairs])  3.11 us
  transfers between devices with their start and end apart: 4, of which 0 were waited for; matrix products, arithmetic and copies ran while one was open for 0% of the time, Pallas kernels for 13%

profile of v5, /device:TPU:1, one launch (start us, length us, event | category | flops | bytes accessed | tf_op | source)
XLA Modules:
  0.0 43.0 jit_solution(17965516852949581658)
XLA Ops:
  0.0 6.8 %shard_map.100 = (bf16[16,2048]{1,0:T(8,128)(2,1)}, f32[16,16,64]{2,1,0:T(8,128)}, f32[16,8,128]{2,1,0:T(8,128)}, bf16[16,64,384]{2,1,0:T(8,128)(2,1)}, bf16[16,64,128]{2,1,0:T(8,128)(2,1)}) custom-call(s32[1,2048]{1,0:T(1,128)} %bitcast.2, f32[16,2048]{1,0:T(8,128)} %rhs_hbm.1, bf16[16,64,128]{2,1,0:T(8,128)(2,1)} %basis_hbm.3, ...), custom_call_target="tpu_custom_call" | custom-call | flops 268435456 | bytes 1048576 | tf_op jit(solution)/shard_map/pallas_call | solution.py:376
  6.8 0.0 copy-start.6
  6.8 0.0 copy-start.9
  6.8 0.0 copy-start.10
  6.8 12.5 %all-to-all-start = ((f32[16,8,128]{2,1,0:T(8,128)}), f32[16,8,128]{2,1,0:T(8,128)S(1)}, u32[]{:S(2)}, u32[]{:S(2)}) async-start(f32[16,8,128]{2,1,0:T(8,128)} %get-tuple-element.17), calls=%async_computation | async-start | bytes 131072 | tf_op jit(solution)/shard_map/all_to_all | solution.py:436
  19.2 0.0 copy-done.6
  19.3 0.0 copy-done.9
  19.3 0.0 copy-done.10
  19.3 0.0 copy-start.3
  19.3 0.0 copy-start.4
  19.3 0.4 shard_map.103
  19.7 3.2 %collective-permute-start = (bf16[32,128]{1,0:T(8,128)(2,1)S(1)}, bf16[32,128]{1,0:T(8,128)(2,1)S(1)}, u32[]{:S(2)}, u32[]{:S(2)}) collective-permute-start(bf16[32,128]{1,0:T(8,128)(2,1)S(1)} %get-tuple-element.27), channel_id=1, source_target_pairs={{0,1},{1,0},{2,3},{3,2},{4,5},{5,4},{6,7},{7,6},{8,9},{9,8},{10,11... | collective-permute-start | bytes 24584 | tf_op jit(solution)/shard_map/ppermute | solution.py:445
  22.8 0.0 copy-start.2
  22.9 3.1 %collective-permute-start.1 = (bf16[32,128]{1,0:T(8,128)(2,1)S(1)}, bf16[32,128]{1,0:T(8,128)(2,1)S(1)}, u32[]{:S(2)}, u32[]{:S(2)}) collective-permute-start(bf16[32,128]{1,0:T(8,128)(2,1)S(1)} %get-tuple-element.28), channel_id=1, source_target_pairs={{1,2},{3,4},{5,6},{7,8},{9,10},{11,12},{13,14},{15,16},{17,18},{19... | collective-permute-start | bytes 24584 | tf_op jit(solution)/shard_map/ppermute | solution.py:447
  26.0 0.0 copy-done.3
  26.0 0.0 copy-start.7
  26.0 0.0 all-to-all-done.received_ref
  26.0 0.0 copy-done.2
  26.1 0.0 copy-start.8
  26.1 1.1 %shard_map.102 = (f32[32,8,128]{2,1,0:T(8,128)}, f32[16,64]{1,0:T(8,128)S(1)}) custom-call(f32[16,8,128]{2,1,0:T(8,128)S(1)} %all-to-all-done.received_ref, bf16[16,64,384]{2,1,0:T(8,128)(2,1)S(1)} %copy-done.2, bf16[16,64,384]{2,1,0:T(8,128)(2,1)S(1)} %get-tuple-element.19.late_ref), custom_call_target="tpu_custom_call" | custom-call | flops 134217728 | bytes 1048576 | tf_op jit(solution)/shard_map/pallas_call | solution.py:376
  27.1 9.0 %all-to-all-start.1 = ((f32[32,8,128]{2,1,0:T(8,128)}), f32[32,8,128]{2,1,0:T(8,128)S(1)}, u32[]{:S(2)}, u32[]{:S(2)}) async-start(f32[32,8,128]{2,1,0:T(8,128)} %get-tuple-element.20), calls=%async_computation.1 | async-start | bytes 262144 | tf_op jit(solution)/shard_map/all_to_all | solution.py:460
  36.1 0.0 collective-permute-done.inner_ref
  36.1 0.0 collective-permute-done.1.across_ref
  36.1 0.0 copy-start.11
  36.1 0.0 copy-done.7
  36.1 0.0 copy-done.8
  36.1 0.0 copy-done
  36.2 0.0 copy-done.12
  36.2 0.6 %copy-done.11 = s32[2,48]{1,0:T(2,128)S(1)} copy-done((s32[2,48]{1,0:T(2,128)S(1)}, s32[2,48]{1,0:T(2,128)}, u32[]{:S(2)}) %copy-start.11) | copy-done | bytes 408
  36.8 4.2 %shard_map.104.partial_ref = f32[16,2048]{1,0:T(8,128)S(1)} custom-call(s32[2,48]{1,0:T(2,128)S(1)} %copy-done.11, s32[2,128]{1,0:T(2,128)S(1)} %copy-done.12, f32[16,64]{1,0:T(8,128)S(1)} %get-tuple-element.23.after_ref.field_ref, f32[16,16,64]{2,1,0:T(8,128)S(1)} %copy-done.8, bf16[64,64,128]{2,1,0:T(8,128)(2,1)S(1)} %bitcast.5, ...), custom_call_target="tpu_custom_call" | custom-call | flops 4294967296 | bytes 1048576 | tf_op jit(solution)/shard_map/pallas_call | solution.py:376
  41.0 0.0 all-to-all-done.1.received_ref
  41.1 1.9 %shard_map.105 = f32[16,2048]{1,0:T(8,128)} custom-call(f32[32,8,128]{2,1,0:T(8,128)S(1)} %all-to-all-done.1.received_ref, bf16[16,64,128]{2,1,0:T(8,128)(2,1)S(1)} %copy-done.5, bf16[16,64,128]{2,1,0:T(8,128)(2,1)S(1)} %get-tuple-element.22.late_ref, f32[16,64]{1,0:T(8,128)S(1)} %get-tuple-element.23.after_ref.field_ref, ...), custom_call_target="tpu_custom_call" | custom-call | flops 268435456 | bytes 1048576 | tf_op jit(solution)/shard_map/pallas_call | solution.py:376
  (8 shorter events, 0.0 us)
Async XLA Ops:
  6.8 12.5 %copy-start.6 = (s32[2048]{0:T(1024)S(1)}, s32[2048]{0:T(1024)}, u32[]{:S(2)}) copy-start(s32[2048]{0:T(1024)} %param.12) | copy-start | bytes 24580
  6.8 12.5 %copy-start.9 = (bf16[16,2048]{1,0:T(8,128)(2,1)S(1)}, bf16[16,2048]{1,0:T(8,128)(2,1)}, u32[]{:S(2)}) copy-start(bf16[16,2048]{1,0:T(8,128)(2,1)} %get-tuple-element.25.sorted_ref) | copy-start | bytes 196612
  6.8 12.5 %copy-start.10 = (bf16[3,2048]{1,0:T(4,128)(2,1)S(1)}, bf16[3,2048]{1,0:T(4,128)(2,1)}, u32[]{:S(2)}) copy-start(bf16[3,2048]{1,0:T(4,128)(2,1)} %coords_hbm.1) | copy-start | bytes 36868
  6.8 19.2 %all-to-all-start = ((f32[16,8,128]{2,1,0:T(8,128)}), f32[16,8,128]{2,1,0:T(8,128)S(1)}, u32[]{:S(2)}, u32[]{:S(2)}) async-start(f32[16,8,128]{2,1,0:T(8,128)} %get-tuple-element.17), calls=%async_computation | async-start | bytes 131072 | tf_op jit(solution)/shard_map/all_to_all | solution.py:436
  19.3 6.7 %copy-start.3 = (bf16[9,2,64,64]{3,2,1,0:T(8,128)(2,1)S(1)}, bf16[9,2,64,64]{3,2,1,0:T(8,128)(2,1)}, u32[]{:S(2)}) copy-start(bf16[9,2,64,64]{3,2,1,0:T(8,128)(2,1)} %transfer_ref.1) | copy-start | bytes 442372
  19.3 6.7 %copy-start.4 = (bf16[9,2,64,64]{3,2,1,0:T(8,128)(2,1)S(1)}, bf16[9,2,64,64]{3,2,1,0:T(8,128)(2,1)}, u32[]{:S(2)}) copy-start(bf16[9,2,64,64]{3,2,1,0:T(8,128)(2,1)} %coupling_ref.1) | copy-start | bytes 442372
  19.7 16.4 %collective-permute-start = (bf16[32,128]{1,0:T(8,128)(2,1)S(1)}, bf16[32,128]{1,0:T(8,128)(2,1)S(1)}, u32[]{:S(2)}, u32[]{:S(2)}) collective-permute-start(bf16[32,128]{1,0:T(8,128)(2,1)S(1)} %get-tuple-element.27), channel_id=1, source_target_pairs={{0,1},{1,0},{2,3},{3,2},{4,5},{5,4},{6,7},{7,6},{8,9},{9,8},{10,11... | collective-permute-start | bytes 24584 | tf_op jit(solution)/shard_map/ppermute | solution.py:445
  22.8 3.2 %copy-start.2 = (bf16[16,64,384]{2,1,0:T(8,128)(2,1)S(1)}, bf16[16,64,384]{2,1,0:T(8,128)(2,1)}, u32[]{:S(2)}) copy-start(bf16[16,64,384]{2,1,0:T(8,128)(2,1)} %get-tuple-element.18.early_ref) | copy-start | bytes 2359300
  22.9 13.3 %collective-permute-start.1 = (bf16[32,128]{1,0:T(8,128)(2,1)S(1)}, bf16[32,128]{1,0:T(8,128)(2,1)S(1)}, u32[]{:S(2)}, u32[]{:S(2)}) collective-permute-start(bf16[32,128]{1,0:T(8,128)(2,1)S(1)} %get-tuple-element.28), channel_id=1, source_target_pairs={{1,2},{3,4},{5,6},{7,8},{9,10},{11,12},{13,14},{15,16},{17,18},{19... | collective-permute-start | bytes 24584 | tf_op jit(solution)/shard_map/ppermute | solution.py:447
  26.0 10.1 %copy-start.7 = (bf16[128,64,64]{0,2,1:T(8,128)(2,1)S(1)}, bf16[128,64,64]{0,2,1:T(8,128)(2,1)}, u32[]{:S(2)}) copy-start(bf16[128,64,64]{0,2,1:T(8,128)(2,1)} %param.15) | copy-start | bytes 3145732
  26.1 10.1 %copy-start.8 = (f32[16,16,64]{2,1,0:T(8,128)S(1)}, f32[16,16,64]{2,1,0:T(8,128)}, u32[]{:S(2)}) copy-start(f32[16,16,64]{2,1,0:T(8,128)} %get-tuple-element.24.coef_ref) | copy-start | bytes 196612
  27.1 9.0 %copy-start = (bf16[16,64,128]{2,1,0:T(8,128)(2,1)S(1)}, bf16[16,64,128]{2,1,0:T(8,128)(2,1)}, u32[]{:S(2)}) copy-start(bf16[16,64,128]{2,1,0:T(8,128)(2,1)} %basis_hbm.3) | copy-start | bytes 786436
  27.1 9.0 %copy-start.12 = (s32[2,128]{1,0:T(2,128)S(1)}, s32[2,128]{1,0:T(2,128)}, u32[]{:S(2)}) copy-start(s32[2,128]{1,0:T(2,128)} %far_ref.1) | copy-start | bytes 3076
  27.1 13.9 %all-to-all-start.1 = ((f32[32,8,128]{2,1,0:T(8,128)}), f32[32,8,128]{2,1,0:T(8,128)S(1)}, u32[]{:S(2)}, u32[]{:S(2)}) async-start(f32[32,8,128]{2,1,0:T(8,128)} %get-tuple-element.20), calls=%async_computation.1 | async-start | bytes 262144 | tf_op jit(solution)/shard_map/all_to_all | solution.py:460
  36.1 0.7 %copy-start.11 = (s32[2,48]{1,0:T(2,128)S(1)}, s32[2,48]{1,0:T(2,128)}, u32[]{:S(2)}) copy-start(s32[2,48]{1,0:T(2,128)} %near_ref.1) | copy-start | bytes 1156
  36.8 4.3 %copy-start.1 = (bf16[16,64,64]{2,1,0:T(8,128)(2,1)S(1)}, bf16[16,64,64]{2,1,0:T(8,128)(2,1)}, u32[]{:S(2)}) copy-start(bf16[16,64,64]{2,1,0:T(8,128)(2,1)} %transfer_hbm.3) | copy-start | bytes 393220
  36.8 4.3 %copy-start.5 = (bf16[16,64,128]{2,1,0:T(8,128)(2,1)S(1)}, bf16[16,64,128]{2,1,0:T(8,128)(2,1)}, u32[]{:S(2)}) copy-start(bf16[16,64,128]{2,1,0:T(8,128)(2,1)} %get-tuple-element.21.early_ref) | copy-start | bytes 786436

commit v6 on v5

--- a/solution.py
+++ b/solution.py
@@ -18,7 +18,7 @@
 HIGHS = 4
 WEIGHTS_FIRST = 3
 LEADER = 11
-MIDDLE = 9
+MIDDLE = 8
 NLOW = 1 << LOW
 NHIGH = 1 << HIGHS
 LOG2E = 1.4426950408889634
@@ -185,12 +185,14 @@
     by_pair, spread, far, rhs, source, target, near
 ):
     del after_ref
-    rows = lax.broadcasted_iota(jnp.int32, (LEAF, LEAF), 0)
-    columns = lax.broadcasted_iota(jnp.int32, (LEAF, LEAF), 1)
-    identity = jnp.where(rows == columns, 1.0, 0.0).astype(BF)
-    for a in range(RANK // 2):
-        two = jnp.concatenate([coupling_ref[a], coupling_ref[a + RANK // 2]], axis=0)
-        by_pair[a * LEAF : (a + 1) * LEAF, :] = mm_nt(identity, two)
+    for first in range(0, RANK // 2, 8):
+        turned = []
+        for a in range(first, first + 8):
+            two = jnp.concatenate([coupling_ref[a], coupling_ref[a + RANK // 2]], axis=0)
+            turned.append(two.astype(F32).T)
+        for j in range(0, LEAF, 8):
+            block = jnp.stack([t[j : j + 8] for t in turned])
+            by_pair[j : j + 8, first : first + 8, :] = jnp.swapaxes(block, 0, 1)
     zero = jnp.zeros((2 * COLS, RANK), BF)
     for n in range(LEAVES):
         hi, lo = halves(coef_ref[n])
@@ -217,7 +219,7 @@
 
     def far_pair(j):
         to, of = far_ref[0, j], far_ref[1, j]
-        rows = by_pair[pl.ds(j, RANK // 2, stride=LEAF), :].astype(BF)
+        rows = by_pair[j].astype(BF)
         far[to] += mm_nt(rows, spread[of])
 
     def near_pair(j):
@@ -314,13 +316,20 @@
     return jnp.concatenate([hi, lo], axis=0)
 
 
-def middle_kernel(received_ref, early_ref, late_ref, message_ref, field_ref):
+def middle_kernel(received_ref, early_ref, late_ref, message_ref, field_ref, result):
     device = lax.axis_index("leaf")
-    weight = jnp.where(weights_first(device), early_ref[...], late_ref[...])
-    total = mm(
-        unpacked([received_ref[(z - LEADER) % NLOW] for z in range(NLOW)]), weight.reshape(NLOW * RANK, 6 * RANK)
-    )
-    total = total[:COLS] + total[COLS:]
+    received = unpacked([received_ref[(z - LEADER) % NLOW] for z in range(NLOW)])
+    first = weights_first(device)
+
+    @pl.when(first)
+    def _():
+        result[...] = mm(received, early_ref[...].reshape(NLOW * RANK, 6 * RANK))
+
+    @pl.when(jnp.logical_not(first))
+    def _():
+        result[...] = mm(received, late_ref[...].reshape(NLOW * RANK, 6 * RANK))
+
+    total = result[:COLS] + result[COLS:]
     node = total[:, :RANK] + total[:, RANK : 2 * RANK]
     fields = total[:, 2 * RANK : 4 * RANK] + total[:, 4 * RANK :]
     field_ref[...] = fields[:, :RANK]
@@ -455,6 +464,7 @@
         middle_kernel,
         [((2 * NHIGH, 8, 2 * RANK), F32), ((COLS, RANK), F32)],
         [(VMEM, received), (VMEM, early_low), (VMEM, late_low)],
+        scratch=[((2 * COLS, 6 * RANK), F32)],
         flops=1 << 27,
     )
     received = lax.all_to_all(message, "leaf", 0, 0, axis_index_groups=high_groups, tiled=True)
@@ -475,7 +485,7 @@
             (VMEM, across),
         ],
         scratch=[
-            ((LEAF * RANK // 2, 2 * RANK), F32),
+            ((LEAF, RANK // 2, 2 * RANK), F32),
             ((LEAVES, 4 * COLS, 2 * RANK), BF),
             ((LEAVES, RANK // 2, 4 * COLS), F32),
             ((LEAVES + 2, COLS, LEAF), BF),

time: 43.3 us -> 43.4 us (level)
  waiting for transfers between devices: 0.01 us -> 0.86 us
  Pallas kernels: 14.3 us -> 13.7 us
    all_to_all x1, waiting for transfers between devices: 0.01 us -> 0.85 us  [per_device(): lax.all_to_all(message, 'leaf', 0, 0, axis_index_groups=high_groups, tile...]
    pallas_call x6, Pallas kernels: 14.3 us -> 13.7 us  [call(): pl.pallas_call(kernel, out_shape=shapes, in_specs=[space for space, _ in...]
  transfers between devices with their start and end apart: 4 -> 4, of which waited for: 0 -> 1; matrix products, arithmetic and copies ran while one was open for 0% -> 0% of each run, Pallas kernels for 13% -> 12%
where the time goes in v6:
time: 43.4 us; the launch traced here: 43 us
  starting transfers between devices  27.6 us (64%)
  Pallas kernels  13.7 us (32%)
  waiting for transfers between devices  0.86 us (2%)
  local copies, waits for them, and re-layouts  0.7 us (2%)
    pallas_call x6, Pallas kernels, call(): pl.pallas_call(kernel, out_shape=shapes, in_specs=[space for space, _ in...  13.7 us
    all_to_all x1, starting transfers between devices, per_device(): lax.all_to_all(message, 'leaf', 0, 0, axis_index_groups=low_groups, tiled...  12.5 us
    all_to_all x1, starting transfers between devices, per_device(): lax.all_to_all(message, 'leaf', 0, 0, axis_index_groups=high_groups, tile...  8.85 us
    ppermute x1, starting transfers between devices, per_device(): inner = lax.ppermute(inner, 'leaf', [(i, i ^ 1) for i in range(count)])  3.16 us
    ppermute x1, starting transfers between devices, per_device(): across = lax.ppermute(across, 'leaf', pairs + [(j, i) for i, j in pairs])  3.11 us
  transfers between devices with their start and end apart: 4, of which 1 were waited for; matrix products, arithmetic and copies ran while one was open for 0% of the time, Pallas kernels for 12%

profile of v6, /device:TPU:1, one launch (start us, length us, event | category | flops | bytes accessed | tf_op | source)
XLA Modules:
  0.0 43.0 jit_solution(8954169090431193834)
XLA Ops:
  0.0 6.8 %shard_map.100 = (bf16[16,2048]{1,0:T(8,128)(2,1)}, f32[16,16,64]{2,1,0:T(8,128)}, f32[16,8,128]{2,1,0:T(8,128)}, bf16[16,64,384]{2,1,0:T(8,128)(2,1)}, bf16[16,64,128]{2,1,0:T(8,128)(2,1)}) custom-call(s32[1,2048]{1,0:T(1,128)} %bitcast.2, f32[16,2048]{1,0:T(8,128)} %rhs_hbm.1, bf16[16,64,128]{2,1,0:T(8,128)(2,1)} %basis_hbm.3, ...), custom_call_target="tpu_custom_call" | custom-call | flops 268435456 | bytes 1048576 | tf_op jit(solution)/shard_map/pallas_call | solution.py:385
  6.8 0.0 copy-start.6
  6.8 0.0 copy-start.9
  6.8 0.0 copy-start.10
  6.8 12.5 %all-to-all-start = ((f32[16,8,128]{2,1,0:T(8,128)}), f32[16,8,128]{2,1,0:T(8,128)S(1)}, u32[]{:S(2)}, u32[]{:S(2)}) async-start(f32[16,8,128]{2,1,0:T(8,128)} %get-tuple-element.17), calls=%async_computation | async-start | bytes 131072 | tf_op jit(solution)/shard_map/all_to_all | solution.py:445
  19.2 0.0 copy-done.6
  19.3 0.0 copy-done.9
  19.3 0.0 copy-done.10
  19.3 0.0 copy-start.3
  19.3 0.0 copy-start.4
  19.3 0.4 shard_map.103
  19.7 3.2 %collective-permute-start = (bf16[32,128]{1,0:T(8,128)(2,1)S(1)}, bf16[32,128]{1,0:T(8,128)(2,1)S(1)}, u32[]{:S(2)}, u32[]{:S(2)}) collective-permute-start(bf16[32,128]{1,0:T(8,128)(2,1)S(1)} %get-tuple-element.27), channel_id=1, source_target_pairs={{0,1},{1,0},{2,3},{3,2},{4,5},{5,4},{6,7},{7,6},{8,9},{9,8},{10,11... | collective-permute-start | bytes 24584 | tf_op jit(solution)/shard_map/ppermute | solution.py:454
  22.8 0.0 copy-start.2
  22.9 3.1 %collective-permute-start.1 = (bf16[32,128]{1,0:T(8,128)(2,1)S(1)}, bf16[32,128]{1,0:T(8,128)(2,1)S(1)}, u32[]{:S(2)}, u32[]{:S(2)}) collective-permute-start(bf16[32,128]{1,0:T(8,128)(2,1)S(1)} %get-tuple-element.28), channel_id=1, source_target_pairs={{1,2},{3,4},{5,6},{7,8},{9,10},{11,12},{13,14},{15,16},{17,18},{19... | collective-permute-start | bytes 24584 | tf_op jit(solution)/shard_map/ppermute | solution.py:456
  26.0 0.0 copy-done.3
  26.0 0.0 copy-done.4
  26.0 0.0 copy-start.7
  26.0 0.0 all-to-all-done.received_ref
  26.0 0.0 copy-done.2
  26.1 0.0 copy-start.8
  26.1 1.1 %shard_map.102 = (f32[32,8,128]{2,1,0:T(8,128)}, f32[16,64]{1,0:T(8,128)S(1)}) custom-call(f32[16,8,128]{2,1,0:T(8,128)S(1)} %all-to-all-done.received_ref, bf16[16,64,384]{2,1,0:T(8,128)(2,1)S(1)} %copy-done.2, bf16[16,64,384]{2,1,0:T(8,128)(2,1)S(1)} %get-tuple-element.19.late_ref), custom_call_target="tpu_custom_call" | custom-call | flops 134217728 | bytes 1048576 | tf_op jit(solution)/shard_map/pallas_call | solution.py:385
  27.2 8.8 %all-to-all-start.1 = ((f32[32,8,128]{2,1,0:T(8,128)}), f32[32,8,128]{2,1,0:T(8,128)S(1)}, u32[]{:S(2)}, u32[]{:S(2)}) async-start(f32[32,8,128]{2,1,0:T(8,128)} %get-tuple-element.20), calls=%async_computation.1 | async-start | bytes 262144 | tf_op jit(solution)/shard_map/all_to_all | solution.py:470
  36.0 0.0 collective-permute-done.inner_ref
  36.0 0.0 collective-permute-done.1.across_ref
  36.1 0.0 copy-start.11
  36.1 0.0 copy-done.7
  36.1 0.0 copy-done.8
  36.1 0.0 copy-done
  36.1 0.6 %copy-done.11 = s32[2,48]{1,0:T(2,128)S(1)} copy-done((s32[2,48]{1,0:T(2,128)S(1)}, s32[2,48]{1,0:T(2,128)}, u32[]{:S(2)}) %copy-start.11) | copy-done | bytes 408
  36.7 3.5 %shard_map.104.partial_ref = f32[16,2048]{1,0:T(8,128)S(1)} custom-call(s32[2,48]{1,0:T(2,128)S(1)} %copy-done.11, s32[2,128]{1,0:T(2,128)S(1)} %copy-done.12, f32[16,64]{1,0:T(8,128)S(1)} %get-tuple-element.23.after_ref.field_ref, f32[16,16,64]{2,1,0:T(8,128)S(1)} %copy-done.8, bf16[64,64,128]{2,1,0:T(8,128)(2,1)S(1)} %bitcast.5, ...), custom_call_target="tpu_custom_call" | custom-call | flops 4294967296 | bytes 1048576 | tf_op jit(solution)/shard_map/pallas_call | solution.py:385
  40.3 0.9 %all-to-all-done.1.received_ref = f32[32,8,128]{2,1,0:T(8,128)S(1)} async-done(((f32[32,8,128]{2,1,0:T(8,128)}), f32[32,8,128]{2,1,0:T(8,128)S(1)}, u32[]{:S(2)}, u32[]{:S(2)}) %all-to-all-start.1) | async-done | bytes 131104 | tf_op jit(solution)/shard_map/all_to_all | solution.py:470
  41.1 1.9 %shard_map.105 = f32[16,2048]{1,0:T(8,128)} custom-call(f32[32,8,128]{2,1,0:T(8,128)S(1)} %all-to-all-done.1.received_ref, bf16[16,64,128]{2,1,0:T(8,128)(2,1)S(1)} %copy-done.5, bf16[16,64,128]{2,1,0:T(8,128)(2,1)S(1)} %get-tuple-element.22.late_ref, f32[16,64]{1,0:T(8,128)S(1)} %get-tuple-element.23.after_ref.field_ref, ...), custom_call_target="tpu_custom_call" | custom-call | flops 268435456 | bytes 1048576 | tf_op jit(solution)/shard_map/pallas_call | solution.py:385
  (8 shorter events, 0.0 us)
Async XLA Ops:
  6.8 12.5 %copy-start.6 = (s32[2048]{0:T(1024)S(1)}, s32[2048]{0:T(1024)}, u32[]{:S(2)}) copy-start(s32[2048]{0:T(1024)} %param.12) | copy-start | bytes 24580
  6.8 12.5 %copy-start.9 = (bf16[16,2048]{1,0:T(8,128)(2,1)S(1)}, bf16[16,2048]{1,0:T(8,128)(2,1)}, u32[]{:S(2)}) copy-start(bf16[16,2048]{1,0:T(8,128)(2,1)} %get-tuple-element.25.sorted_ref) | copy-start | bytes 196612
  6.8 12.5 %copy-start.10 = (bf16[3,2048]{1,0:T(4,128)(2,1)S(1)}, bf16[3,2048]{1,0:T(4,128)(2,1)}, u32[]{:S(2)}) copy-start(bf16[3,2048]{1,0:T(4,128)(2,1)} %coords_hbm.1) | copy-start | bytes 36868
  6.8 19.2 %all-to-all-start = ((f32[16,8,128]{2,1,0:T(8,128)}), f32[16,8,128]{2,1,0:T(8,128)S(1)}, u32[]{:S(2)}, u32[]{:S(2)}) async-start(f32[16,8,128]{2,1,0:T(8,128)} %get-tuple-element.17), calls=%async_computation | async-start | bytes 131072 | tf_op jit(solution)/shard_map/all_to_all | solution.py:445
  19.3 6.7 %copy-start.3 = (bf16[9,2,64,64]{3,2,1,0:T(8,128)(2,1)S(1)}, bf16[9,2,64,64]{3,2,1,0:T(8,128)(2,1)}, u32[]{:S(2)}) copy-start(bf16[9,2,64,64]{3,2,1,0:T(8,128)(2,1)} %transfer_ref.1) | copy-start | bytes 442372
  19.3 6.7 %copy-start.4 = (bf16[9,2,64,64]{3,2,1,0:T(8,128)(2,1)S(1)}, bf16[9,2,64,64]{3,2,1,0:T(8,128)(2,1)}, u32[]{:S(2)}) copy-start(bf16[9,2,64,64]{3,2,1,0:T(8,128)(2,1)} %coupling_ref.1) | copy-start | bytes 442372
  19.7 16.4 %collective-permute-start = (bf16[32,128]{1,0:T(8,128)(2,1)S(1)}, bf16[32,128]{1,0:T(8,128)(2,1)S(1)}, u32[]{:S(2)}, u32[]{:S(2)}) collective-permute-start(bf16[32,128]{1,0:T(8,128)(2,1)S(1)} %get-tuple-element.27), channel_id=1, source_target_pairs={{0,1},{1,0},{2,3},{3,2},{4,5},{5,4},{6,7},{7,6},{8,9},{9,8},{10,11... | collective-permute-start | bytes 24584 | tf_op jit(solution)/shard_map/ppermute | solution.py:454
  22.8 3.2 %copy-start.2 = (bf16[16,64,384]{2,1,0:T(8,128)(2,1)S(1)}, bf16[16,64,384]{2,1,0:T(8,128)(2,1)}, u32[]{:S(2)}) copy-start(bf16[16,64,384]{2,1,0:T(8,128)(2,1)} %get-tuple-element.18.early_ref) | copy-start | bytes 2359300
  22.9 13.2 %collective-permute-start.1 = (bf16[32,128]{1,0:T(8,128)(2,1)S(1)}, bf16[32,128]{1,0:T(8,128)(2,1)S(1)}, u32[]{:S(2)}, u32[]{:S(2)}) collective-permute-start(bf16[32,128]{1,0:T(8,128)(2,1)S(1)} %get-tuple-element.28), channel_id=1, source_target_pairs={{1,2},{3,4},{5,6},{7,8},{9,10},{11,12},{13,14},{15,16},{17,18},{19... | collective-permute-start | bytes 24584 | tf_op jit(solution)/shard_map/ppermute | solution.py:456
  26.0 10.1 %copy-start.7 = (bf16[128,64,64]{0,2,1:T(8,128)(2,1)S(1)}, bf16[128,64,64]{0,2,1:T(8,128)(2,1)}, u32[]{:S(2)}) copy-start(bf16[128,64,64]{0,2,1:T(8,128)(2,1)} %param.15) | copy-start | bytes 3145732
  26.1 10.0 %copy-start.8 = (f32[16,16,64]{2,1,0:T(8,128)S(1)}, f32[16,16,64]{2,1,0:T(8,128)}, u32[]{:S(2)}) copy-start(f32[16,16,64]{2,1,0:T(8,128)} %get-tuple-element.24.coef_ref) | copy-start | bytes 196612
  27.2 8.9 %copy-start = (bf16[16,64,128]{2,1,0:T(8,128)(2,1)S(1)}, bf16[16,64,128]{2,1,0:T(8,128)(2,1)}, u32[]{:S(2)}) copy-start(bf16[16,64,128]{2,1,0:T(8,128)(2,1)} %basis_hbm.3) | copy-start | bytes 786436
  27.2 8.9 %copy-start.12 = (s32[2,128]{1,0:T(2,128)S(1)}, s32[2,128]{1,0:T(2,128)}, u32[]{:S(2)}) copy-start(s32[2,128]{1,0:T(2,128)} %far_ref.1) | copy-start | bytes 3076
  27.2 13.9 %all-to-all-start.1 = ((f32[32,8,128]{2,1,0:T(8,128)}), f32[32,8,128]{2,1,0:T(8,128)S(1)}, u32[]{:S(2)}, u32[]{:S(2)}) async-start(f32[32,8,128]{2,1,0:T(8,128)} %get-tuple-element.20), calls=%async_computation.1 | async-start | bytes 262144 | tf_op jit(solution)/shard_map/all_to_all | solution.py:470
  36.1 0.7 %copy-start.11 = (s32[2,48]{1,0:T(2,128)S(1)}, s32[2,48]{1,0:T(2,128)}, u32[]{:S(2)}) copy-start(s32[2,48]{1,0:T(2,128)} %near_ref.1) | copy-start | bytes 1156
  36.7 4.4 %copy-start.1 = (bf16[16,64,64]{2,1,0:T(8,128)(2,1)S(1)}, bf16[16,64,64]{2,1,0:T(8,128)(2,1)}, u32[]{:S(2)}) copy-start(bf16[16,64,64]{2,1,0:T(8,128)(2,1)} %transfer_hbm.3) | copy-start | bytes 393220
  36.7 4.4 %copy-start.5 = (bf16[16,64,128]{2,1,0:T(8,128)(2,1)S(1)}, bf16[16,64,128]{2,1,0:T(8,128)(2,1)}, u32[]{:S(2)}) copy-start(bf16[16,64,128]{2,1,0:T(8,128)(2,1)} %get-tuple-element.21.early_ref) | copy-start | bytes 786436

commit v7 on v6

--- a/solution.py
+++ b/solution.py
@@ -96,7 +96,7 @@
 
 def up_kernel(
     order_hbm, rhs_hbm, basis_hbm, transfer_hbm, top_transfer_hbm, top_coupling_hbm,
-    sorted_ref, coef_ref, message_ref, low_hbm, high_hbm,
+    sorted_ref, message_ref, low_hbm, high_hbm,
     order_ref, rhs_ref, basis_ref, transfer_ref, top_transfer_ref, top_coupling_ref, low_ref, high_ref, sems
 ):
     device = lax.axis_index("leaf")
@@ -124,7 +124,6 @@
     for n in range(LEAVES):
         coef = mm_nt(total[:, n * LEAF : (n + 1) * LEAF], basis_ref[n])
         coefs.append(coef)
-        coef_ref[n] = coef
     hi, lo = halves(jnp.concatenate(coefs, axis=1))
     root = mm(jnp.concatenate([hi, lo], axis=0), transfer_ref[...].reshape(LEAVES * RANK, RANK))
     message = pack_message(root[:COLS] + root[COLS:])
@@ -181,7 +180,7 @@
 
 
 def local_kernel(
-    near_ref, far_ref, after_ref, coef_ref, coupling_ref, basis_ref, sorted_ref, points_ref, inner_ref, across_ref, out_ref,
+    near_ref, far_ref, after_ref, coupling_ref, basis_ref, sorted_ref, points_ref, inner_ref, across_ref, out_ref,
     by_pair, spread, far, rhs, source, target, near
 ):
     del after_ref
@@ -195,7 +194,7 @@
             by_pair[j : j + 8, first : first + 8, :] = jnp.swapaxes(block, 0, 1)
     zero = jnp.zeros((2 * COLS, RANK), BF)
     for n in range(LEAVES):
-        hi, lo = halves(coef_ref[n])
+        hi, lo = halves(mm_nt(sorted_ref[:, n * LEAF : (n + 1) * LEAF], basis_ref[n]))
         both = jnp.concatenate([hi, lo], axis=0)
         spread[n] = jnp.concatenate(
             [jnp.concatenate([both, zero], axis=1), jnp.concatenate([zero, both], axis=1)], axis=0
@@ -415,11 +414,10 @@
     low_like = ((NLOW, RANK, 6 * RANK), BF)
     high_like = ((NHIGH, RANK, 2 * RANK), BF)
     top_like = (top_transfer.shape, BF)
-    sorted_rhs, coef, message, early_low, early_high = call(
+    sorted_rhs, message, early_low, early_high = call(
         up_kernel,
         [
             ((COLS, PTS), BF),
-            ((LEAVES, COLS, RANK), F32),
             ((NLOW, 8, 2 * RANK), F32),
             (*low_like, HBM),
             (*high_like, HBM),
@@ -476,7 +474,6 @@
             (SMEM, near_pairs),
             (SMEM, far_pairs),
             (ANY, field),
-            (VMEM, coef),
             (VMEM, coupling),
             (VMEM, leaf_basis),
             (VMEM, sorted_rhs),

time: 43.4 us -> 43.3 us (level)
  no operation moved by 1% of the time
where the time goes in v7:
time: 43.3 us; the launch traced here: 42.9 us
  starting transfers between devices  27.6 us (64%)
  Pallas kernels  13.7 us (32%)
  waiting for transfers between devices  0.77 us (2%)
  local copies, waits for them, and re-layouts  0.7 us (2%)
    pallas_call x6, Pallas kernels, call(): pl.pallas_call(kernel, out_shape=shapes, in_specs=[space for space, _ in...  13.7 us
    all_to_all x1, starting transfers between devices, per_device(): lax.all_to_all(message, 'leaf', 0, 0, axis_index_groups=low_groups, tiled...  12.5 us
    all_to_all x1, starting transfers between devices, per_device(): lax.all_to_all(message, 'leaf', 0, 0, axis_index_groups=high_groups, tile...  8.85 us
    ppermute x1, starting transfers between devices, per_device(): inner = lax.ppermute(inner, 'leaf', [(i, i ^ 1) for i in range(count)])  3.15 us
    ppermute x1, starting transfers between devices, per_device(): across = lax.ppermute(across, 'leaf', pairs + [(j, i) for i, j in pairs])  3.12 us
  transfers between devices with their start and end apart: 4, of which 1 were waited for; matrix products, arithmetic and copies ran while one was open for 0% of the time, Pallas kernels for 12%

profile of v7, /device:TPU:1, one launch (start us, length us, event | category | flops | bytes accessed | tf_op | source)
XLA Modules:
  0.0 42.9 jit_solution(17729830393459129558)
XLA Ops:
  0.0 6.7 %shard_map.100 = (bf16[16,2048]{1,0:T(8,128)(2,1)}, f32[16,8,128]{2,1,0:T(8,128)}, bf16[16,64,384]{2,1,0:T(8,128)(2,1)}, bf16[16,64,128]{2,1,0:T(8,128)(2,1)}) custom-call(s32[1,2048]{1,0:T(1,128)} %bitcast.2, f32[16,2048]{1,0:T(8,128)} %rhs_hbm.1, bf16[16,64,128]{2,1,0:T(8,128)(2,1)} %basis_hbm.3, bf16[16,64,64]{2,1,0:T(8,128)(2,1)} %transfer_hbm.3, ...), custom_call_target="tpu_custom_call" | custom-call | flops 268435456 | bytes 1048576 | tf_op jit(solution)/shard_map/pallas_call | solution.py:384
  6.7 0.0 copy-start.6
  6.7 0.0 copy-start.8
  6.7 0.0 copy-start.9
  6.7 12.5 %all-to-all-start = ((f32[16,8,128]{2,1,0:T(8,128)}), f32[16,8,128]{2,1,0:T(8,128)S(1)}, u32[]{:S(2)}, u32[]{:S(2)}) async-start(f32[16,8,128]{2,1,0:T(8,128)} %get-tuple-element.16), calls=%async_computation | async-start | bytes 131072 | tf_op jit(solution)/shard_map/all_to_all | solution.py:443
  19.2 0.0 copy-done.6
  19.2 0.0 copy-done.8
  19.2 0.0 copy-done.9
  19.2 0.0 copy-start.3
  19.2 0.0 copy-start.4
  19.2 0.4 shard_map.103
  19.6 3.2 %collective-permute-start = (bf16[32,128]{1,0:T(8,128)(2,1)S(1)}, bf16[32,128]{1,0:T(8,128)(2,1)S(1)}, u32[]{:S(2)}, u32[]{:S(2)}) collective-permute-start(bf16[32,128]{1,0:T(8,128)(2,1)S(1)} %get-tuple-element.25), channel_id=1, source_target_pairs={{0,1},{1,0},{2,3},{3,2},{4,5},{5,4},{6,7},{7,6},{8,9},{9,8},{10,11... | collective-permute-start | bytes 24584 | tf_op jit(solution)/shard_map/ppermute | solution.py:452
  22.8 0.0 copy-start.2
  22.8 3.1 %collective-permute-start.1 = (bf16[32,128]{1,0:T(8,128)(2,1)S(1)}, bf16[32,128]{1,0:T(8,128)(2,1)S(1)}, u32[]{:S(2)}, u32[]{:S(2)}) collective-permute-start(bf16[32,128]{1,0:T(8,128)(2,1)S(1)} %get-tuple-element.26), channel_id=1, source_target_pairs={{1,2},{3,4},{5,6},{7,8},{9,10},{11,12},{13,14},{15,16},{17,18},{19... | collective-permute-start | bytes 24584 | tf_op jit(solution)/shard_map/ppermute | solution.py:454
  25.9 0.0 copy-done.3
  25.9 0.0 copy-done.4
  26.0 0.0 copy-start.7
  26.0 0.0 all-to-all-done.received_ref
  26.0 0.0 copy-done.2
  26.0 1.1 %shard_map.102 = (f32[32,8,128]{2,1,0:T(8,128)}, f32[16,64]{1,0:T(8,128)S(1)}) custom-call(f32[16,8,128]{2,1,0:T(8,128)S(1)} %all-to-all-done.received_ref, bf16[16,64,384]{2,1,0:T(8,128)(2,1)S(1)} %copy-done.2, bf16[16,64,384]{2,1,0:T(8,128)(2,1)S(1)} %get-tuple-element.18.late_ref), custom_call_target="tpu_custom_call" | custom-call | flops 134217728 | bytes 1048576 | tf_op jit(solution)/shard_map/pallas_call | solution.py:384
  27.1 8.8 %all-to-all-start.1 = ((f32[32,8,128]{2,1,0:T(8,128)}), f32[32,8,128]{2,1,0:T(8,128)S(1)}, u32[]{:S(2)}, u32[]{:S(2)}) async-start(f32[32,8,128]{2,1,0:T(8,128)} %get-tuple-element.19), calls=%async_computation.1 | async-start | bytes 262144 | tf_op jit(solution)/shard_map/all_to_all | solution.py:468
  36.0 0.0 collective-permute-done.inner_ref
  36.0 0.0 collective-permute-done.1.across_ref
  36.0 0.0 copy-start.10
  36.0 0.0 copy-done.7
  36.0 0.0 copy-done
  36.0 0.0 copy-done.11
  36.0 0.6 %copy-done.10 = s32[2,48]{1,0:T(2,128)S(1)} copy-done((s32[2,48]{1,0:T(2,128)S(1)}, s32[2,48]{1,0:T(2,128)}, u32[]{:S(2)}) %copy-start.10) | copy-done | bytes 408
  36.7 3.6 %shard_map.104.partial_ref = f32[16,2048]{1,0:T(8,128)S(1)} custom-call(s32[2,48]{1,0:T(2,128)S(1)} %copy-done.10, s32[2,128]{1,0:T(2,128)S(1)} %copy-done.11, f32[16,64]{1,0:T(8,128)S(1)} %get-tuple-element.22.after_ref.field_ref, bf16[64,64,128]{2,1,0:T(8,128)(2,1)S(1)} %bitcast.5, bf16[16,64,128]{2,1,0:T(8,128)(2,1)S(1)} %copy-done, ...), custom_call_target="tpu_custom_call" | custom-call | flops 4294967296 | bytes 1048576 | tf_op jit(solution)/shard_map/pallas_call | solution.py:384
  40.3 0.8 %all-to-all-done.1.received_ref = f32[32,8,128]{2,1,0:T(8,128)S(1)} async-done(((f32[32,8,128]{2,1,0:T(8,128)}), f32[32,8,128]{2,1,0:T(8,128)S(1)}, u32[]{:S(2)}, u32[]{:S(2)}) %all-to-all-start.1) | async-done | bytes 131104 | tf_op jit(solution)/shard_map/all_to_all | solution.py:468
  41.0 0.0 copy-done.1
  41.0 1.9 %shard_map.105 = f32[16,2048]{1,0:T(8,128)} custom-call(f32[32,8,128]{2,1,0:T(8,128)S(1)} %all-to-all-done.1.received_ref, bf16[16,64,128]{2,1,0:T(8,128)(2,1)S(1)} %copy-done.5, bf16[16,64,128]{2,1,0:T(8,128)(2,1)S(1)} %get-tuple-element.21.late_ref, f32[16,64]{1,0:T(8,128)S(1)} %get-tuple-element.22.after_ref.field_ref, ...), custom_call_target="tpu_custom_call" | custom-call | flops 268435456 | bytes 1048576 | tf_op jit(solution)/shard_map/pallas_call | solution.py:384
  (6 shorter events, 0.0 us)
Async XLA Ops:
  6.7 12.5 %copy-start.6 = (s32[2048]{0:T(1024)S(1)}, s32[2048]{0:T(1024)}, u32[]{:S(2)}) copy-start(s32[2048]{0:T(1024)} %param.12) | copy-start | bytes 24580
  6.7 12.5 %copy-start.8 = (bf16[16,2048]{1,0:T(8,128)(2,1)S(1)}, bf16[16,2048]{1,0:T(8,128)(2,1)}, u32[]{:S(2)}) copy-start(bf16[16,2048]{1,0:T(8,128)(2,1)} %get-tuple-element.23.sorted_ref) | copy-start | bytes 196612
  6.7 12.5 %copy-start.9 = (bf16[3,2048]{1,0:T(4,128)(2,1)S(1)}, bf16[3,2048]{1,0:T(4,128)(2,1)}, u32[]{:S(2)}) copy-start(bf16[3,2048]{1,0:T(4,128)(2,1)} %coords_hbm.1) | copy-start | bytes 36868
  6.7 19.2 %all-to-all-start = ((f32[16,8,128]{2,1,0:T(8,128)}), f32[16,8,128]{2,1,0:T(8,128)S(1)}, u32[]{:S(2)}, u32[]{:S(2)}) async-start(f32[16,8,128]{2,1,0:T(8,128)} %get-tuple-element.16), calls=%async_computation | async-start | bytes 131072 | tf_op jit(solution)/shard_map/all_to_all | solution.py:443
  19.2 6.7 %copy-start.3 = (bf16[9,2,64,64]{3,2,1,0:T(8,128)(2,1)S(1)}, bf16[9,2,64,64]{3,2,1,0:T(8,128)(2,1)}, u32[]{:S(2)}) copy-start(bf16[9,2,64,64]{3,2,1,0:T(8,128)(2,1)} %transfer_ref.1) | copy-start | bytes 442372
  19.2 6.7 %copy-start.4 = (bf16[9,2,64,64]{3,2,1,0:T(8,128)(2,1)S(1)}, bf16[9,2,64,64]{3,2,1,0:T(8,128)(2,1)}, u32[]{:S(2)}) copy-start(bf16[9,2,64,64]{3,2,1,0:T(8,128)(2,1)} %coupling_ref.1) | copy-start | bytes 442372
  19.6 16.4 %collective-permute-start = (bf16[32,128]{1,0:T(8,128)(2,1)S(1)}, bf16[32,128]{1,0:T(8,128)(2,1)S(1)}, u32[]{:S(2)}, u32[]{:S(2)}) collective-permute-start(bf16[32,128]{1,0:T(8,128)(2,1)S(1)} %get-tuple-element.25), channel_id=1, source_target_pairs={{0,1},{1,0},{2,3},{3,2},{4,5},{5,4},{6,7},{7,6},{8,9},{9,8},{10,11... | collective-permute-start | bytes 24584 | tf_op jit(solution)/shard_map/ppermute | solution.py:452
  22.8 3.2 %copy-start.2 = (bf16[16,64,384]{2,1,0:T(8,128)(2,1)S(1)}, bf16[16,64,384]{2,1,0:T(8,128)(2,1)}, u32[]{:S(2)}) copy-start(bf16[16,64,384]{2,1,0:T(8,128)(2,1)} %get-tuple-element.17.early_ref) | copy-start | bytes 2359300
  22.8 13.2 %collective-permute-start.1 = (bf16[32,128]{1,0:T(8,128)(2,1)S(1)}, bf16[32,128]{1,0:T(8,128)(2,1)S(1)}, u32[]{:S(2)}, u32[]{:S(2)}) collective-permute-start(bf16[32,128]{1,0:T(8,128)(2,1)S(1)} %get-tuple-element.26), channel_id=1, source_target_pairs={{1,2},{3,4},{5,6},{7,8},{9,10},{11,12},{13,14},{15,16},{17,18},{19... | collective-permute-start | bytes 24584 | tf_op jit(solution)/shard_map/ppermute | solution.py:454
  26.0 10.0 %copy-start.7 = (bf16[128,64,64]{0,2,1:T(8,128)(2,1)S(1)}, bf16[128,64,64]{0,2,1:T(8,128)(2,1)}, u32[]{:S(2)}) copy-start(bf16[128,64,64]{0,2,1:T(8,128)(2,1)} %param.15) | copy-start | bytes 3145732
  27.1 8.9 %copy-start = (bf16[16,64,128]{2,1,0:T(8,128)(2,1)S(1)}, bf16[16,64,128]{2,1,0:T(8,128)(2,1)}, u32[]{:S(2)}) copy-start(bf16[16,64,128]{2,1,0:T(8,128)(2,1)} %basis_hbm.3) | copy-start | bytes 786436
  27.1 8.9 %copy-start.11 = (s32[2,128]{1,0:T(2,128)S(1)}, s32[2,128]{1,0:T(2,128)}, u32[]{:S(2)}) copy-start(s32[2,128]{1,0:T(2,128)} %far_ref.1) | copy-start | bytes 3076
  27.1 13.9 %all-to-all-start.1 = ((f32[32,8,128]{2,1,0:T(8,128)}), f32[32,8,128]{2,1,0:T(8,128)S(1)}, u32[]{:S(2)}, u32[]{:S(2)}) async-start(f32[32,8,128]{2,1,0:T(8,128)} %get-tuple-element.19), calls=%async_computation.1 | async-start | bytes 262144 | tf_op jit(solution)/shard_map/all_to_all | solution.py:468
  36.0 0.7 %copy-start.10 = (s32[2,48]{1,0:T(2,128)S(1)}, s32[2,48]{1,0:T(2,128)}, u32[]{:S(2)}) copy-start(s32[2,48]{1,0:T(2,128)} %near_ref.1) | copy-start | bytes 1156
  36.7 4.4 %copy-start.1 = (bf16[16,64,64]{2,1,0:T(8,128)(2,1)S(1)}, bf16[16,64,64]{2,1,0:T(8,128)(2,1)}, u32[]{:S(2)}) copy-start(bf16[16,64,64]{2,1,0:T(8,128)(2,1)} %transfer_hbm.3) | copy-start | bytes 393220
  36.7 4.4 %copy-start.5 = (bf16[16,64,128]{2,1,0:T(8,128)(2,1)S(1)}, bf16[16,64,128]{2,1,0:T(8,128)(2,1)}, u32[]{:S(2)}) copy-start(bf16[16,64,128]{2,1,0:T(8,128)(2,1)} %get-tuple-element.20.early_ref) | copy-start | bytes 786436

commit v8 on v7

--- a/solution.py
+++ b/solution.py
@@ -106,11 +106,11 @@
         sems,
     )
     copies[0].wait()
-    copies[1].wait()
-    x = rhs_ref[...].astype(BF)
     order = order_ref[...]
     block = jnp.right_shift(order, 8)
     places = low_onehot(order)
+    copies[1].wait()
+    x = rhs_ref[...].astype(BF)
     copies[2].wait()
     copies[3].wait()
     stacked = jnp.concatenate([x[:, h * WIDE : (h + 1) * WIDE] for h in range(BLOCKS)], axis=0)

time: 43.3 us -> 43.3 us (level)
  no operation moved by 1% of the time
where the time goes in v8:
time: 43.3 us; the launch traced here: 42.9 us
  starting transfers between devices  27.6 us (64%)
  Pallas kernels  13.7 us (32%)
  waiting for transfers between devices  0.77 us (2%)
  local copies, waits for them, and re-layouts  0.7 us (2%)
    pallas_call x6, Pallas kernels, call(): pl.pallas_call(kernel, out_shape=shapes, in_specs=[space for space, _ in...  13.7 us
    all_to_all x1, starting transfers between devices, per_device(): lax.all_to_all(message, 'leaf', 0, 0, axis_index_groups=low_groups, tiled...  12.5 us
    all_to_all x1, starting transfers between devices, per_device(): lax.all_to_all(message, 'leaf', 0, 0, axis_index_groups=high_groups, tile...  8.85 us
    ppermute x1, starting transfers between devices, per_device(): inner = lax.ppermute(inner, 'leaf', [(i, i ^ 1) for i in range(count)])  3.15 us
    ppermute x1, starting transfers between devices, per_device(): across = lax.ppermute(across, 'leaf', pairs + [(j, i) for i, j in pairs])  3.12 us
  transfers between devices with their start and end apart: 4, of which 1 were waited for; matrix products, arithmetic and copies ran while one was open for 0% of the time, Pallas kernels for 12%

profile of v8, /device:TPU:1, one launch (start us, length us, event | category | flops | bytes accessed | tf_op | source)
XLA Modules:
  0.0 42.9 jit_solution(9562503422622548151)
XLA Ops:
  0.0 6.7 %shard_map.100 = (bf16[16,2048]{1,0:T(8,128)(2,1)}, f32[16,8,128]{2,1,0:T(8,128)}, bf16[16,64,384]{2,1,0:T(8,128)(2,1)}, bf16[16,64,128]{2,1,0:T(8,128)(2,1)}) custom-call(s32[1,2048]{1,0:T(1,128)} %bitcast.2, f32[16,2048]{1,0:T(8,128)} %rhs_hbm.1, bf16[16,64,128]{2,1,0:T(8,128)(2,1)} %basis_hbm.3, bf16[16,64,64]{2,1,0:T(8,128)(2,1)} %transfer_hbm.3, ...), custom_call_target="tpu_custom_call" | custom-call | flops 268435456 | bytes 1048576 | tf_op jit(solution)/shard_map/pallas_call | solution.py:384
  6.7 0.0 copy-start.6
  6.7 0.0 copy-start.8
  6.7 0.0 copy-start.9
  6.7 12.5 %all-to-all-start = ((f32[16,8,128]{2,1,0:T(8,128)}), f32[16,8,128]{2,1,0:T(8,128)S(1)}, u32[]{:S(2)}, u32[]{:S(2)}) async-start(f32[16,8,128]{2,1,0:T(8,128)} %get-tuple-element.16), calls=%async_computation | async-start | bytes 131072 | tf_op jit(solution)/shard_map/all_to_all | solution.py:443
  19.2 0.0 copy-done.6
  19.2 0.0 copy-done.8
  19.2 0.0 copy-done.9
  19.2 0.0 copy-start.3
  19.2 0.0 copy-start.4
  19.2 0.4 shard_map.103
  19.6 3.2 %collective-permute-start = (bf16[32,128]{1,0:T(8,128)(2,1)S(1)}, bf16[32,128]{1,0:T(8,128)(2,1)S(1)}, u32[]{:S(2)}, u32[]{:S(2)}) collective-permute-start(bf16[32,128]{1,0:T(8,128)(2,1)S(1)} %get-tuple-element.25), channel_id=1, source_target_pairs={{0,1},{1,0},{2,3},{3,2},{4,5},{5,4},{6,7},{7,6},{8,9},{9,8},{10,11... | collective-permute-start | bytes 24584 | tf_op jit(solution)/shard_map/ppermute | solution.py:452
  22.8 0.0 copy-start.2
  22.8 3.1 %collective-permute-start.1 = (bf16[32,128]{1,0:T(8,128)(2,1)S(1)}, bf16[32,128]{1,0:T(8,128)(2,1)S(1)}, u32[]{:S(2)}, u32[]{:S(2)}) collective-permute-start(bf16[32,128]{1,0:T(8,128)(2,1)S(1)} %get-tuple-element.26), channel_id=1, source_target_pairs={{1,2},{3,4},{5,6},{7,8},{9,10},{11,12},{13,14},{15,16},{17,18},{19... | collective-permute-start | bytes 24584 | tf_op jit(solution)/shard_map/ppermute | solution.py:454
  25.9 0.0 copy-done.3
  25.9 0.0 copy-done.4
  26.0 0.0 copy-start.7
  26.0 0.0 all-to-all-done.received_ref
  26.0 0.0 copy-done.2
  26.0 1.1 %shard_map.102 = (f32[32,8,128]{2,1,0:T(8,128)}, f32[16,64]{1,0:T(8,128)S(1)}) custom-call(f32[16,8,128]{2,1,0:T(8,128)S(1)} %all-to-all-done.received_ref, bf16[16,64,384]{2,1,0:T(8,128)(2,1)S(1)} %copy-done.2, bf16[16,64,384]{2,1,0:T(8,128)(2,1)S(1)} %get-tuple-element.18.late_ref), custom_call_target="tpu_custom_call" | custom-call | flops 134217728 | bytes 1048576 | tf_op jit(solution)/shard_map/pallas_call | solution.py:384
  27.1 8.8 %all-to-all-start.1 = ((f32[32,8,128]{2,1,0:T(8,128)}), f32[32,8,128]{2,1,0:T(8,128)S(1)}, u32[]{:S(2)}, u32[]{:S(2)}) async-start(f32[32,8,128]{2,1,0:T(8,128)} %get-tuple-element.19), calls=%async_computation.1 | async-start | bytes 262144 | tf_op jit(solution)/shard_map/all_to_all | solution.py:468
  36.0 0.0 collective-permute-done.inner_ref
  36.0 0.0 collective-permute-done.1.across_ref
  36.0 0.0 copy-start.10
  36.0 0.0 copy-done.7
  36.0 0.0 copy-done
  36.0 0.0 copy-done.11
  36.0 0.6 %copy-done.10 = s32[2,48]{1,0:T(2,128)S(1)} copy-done((s32[2,48]{1,0:T(2,128)S(1)}, s32[2,48]{1,0:T(2,128)}, u32[]{:S(2)}) %copy-start.10) | copy-done | bytes 408
  36.7 3.6 %shard_map.104.partial_ref = f32[16,2048]{1,0:T(8,128)S(1)} custom-call(s32[2,48]{1,0:T(2,128)S(1)} %copy-done.10, s32[2,128]{1,0:T(2,128)S(1)} %copy-done.11, f32[16,64]{1,0:T(8,128)S(1)} %get-tuple-element.22.after_ref.field_ref, bf16[64,64,128]{2,1,0:T(8,128)(2,1)S(1)} %bitcast.5, bf16[16,64,128]{2,1,0:T(8,128)(2,1)S(1)} %copy-done, ...), custom_call_target="tpu_custom_call" | custom-call | flops 4294967296 | bytes 1048576 | tf_op jit(solution)/shard_map/pallas_call | solution.py:384
  40.3 0.8 %all-to-all-done.1.received_ref = f32[32,8,128]{2,1,0:T(8,128)S(1)} async-done(((f32[32,8,128]{2,1,0:T(8,128)}), f32[32,8,128]{2,1,0:T(8,128)S(1)}, u32[]{:S(2)}, u32[]{:S(2)}) %all-to-all-start.1) | async-done | bytes 131104 | tf_op jit(solution)/shard_map/all_to_all | solution.py:468
  41.0 0.0 copy-done.1
  41.0 1.9 %shard_map.105 = f32[16,2048]{1,0:T(8,128)} custom-call(f32[32,8,128]{2,1,0:T(8,128)S(1)} %all-to-all-done.1.received_ref, bf16[16,64,128]{2,1,0:T(8,128)(2,1)S(1)} %copy-done.5, bf16[16,64,128]{2,1,0:T(8,128)(2,1)S(1)} %get-tuple-element.21.late_ref, f32[16,64]{1,0:T(8,128)S(1)} %get-tuple-element.22.after_ref.field_ref, ...), custom_call_target="tpu_custom_call" | custom-call | flops 268435456 | bytes 1048576 | tf_op jit(solution)/shard_map/pallas_call | solution.py:384
  (6 shorter events, 0.0 us)
Async XLA Ops:
  6.7 12.5 %copy-start.6 = (s32[2048]{0:T(1024)S(1)}, s32[2048]{0:T(1024)}, u32[]{:S(2)}) copy-start(s32[2048]{0:T(1024)} %param.12) | copy-start | bytes 24580
  6.7 12.5 %copy-start.8 = (bf16[16,2048]{1,0:T(8,128)(2,1)S(1)}, bf16[16,2048]{1,0:T(8,128)(2,1)}, u32[]{:S(2)}) copy-start(bf16[16,2048]{1,0:T(8,128)(2,1)} %get-tuple-element.23.sorted_ref) | copy-start | bytes 196612
  6.7 12.5 %copy-start.9 = (bf16[3,2048]{1,0:T(4,128)(2,1)S(1)}, bf16[3,2048]{1,0:T(4,128)(2,1)}, u32[]{:S(2)}) copy-start(bf16[3,2048]{1,0:T(4,128)(2,1)} %coords_hbm.1) | copy-start | bytes 36868
  6.7 19.2 %all-to-all-start = ((f32[16,8,128]{2,1,0:T(8,128)}), f32[16,8,128]{2,1,0:T(8,128)S(1)}, u32[]{:S(2)}, u32[]{:S(2)}) async-start(f32[16,8,128]{2,1,0:T(8,128)} %get-tuple-element.16), calls=%async_computation | async-start | bytes 131072 | tf_op jit(solution)/shard_map/all_to_all | solution.py:443
  19.2 6.7 %copy-start.3 = (bf16[9,2,64,64]{3,2,1,0:T(8,128)(2,1)S(1)}, bf16[9,2,64,64]{3,2,1,0:T(8,128)(2,1)}, u32[]{:S(2)}) copy-start(bf16[9,2,64,64]{3,2,1,0:T(8,128)(2,1)} %transfer_ref.1) | copy-start | bytes 442372
  19.2 6.7 %copy-start.4 = (bf16[9,2,64,64]{3,2,1,0:T(8,128)(2,1)S(1)}, bf16[9,2,64,64]{3,2,1,0:T(8,128)(2,1)}, u32[]{:S(2)}) copy-start(bf16[9,2,64,64]{3,2,1,0:T(8,128)(2,1)} %coupling_ref.1) | copy-start | bytes 442372
  19.6 16.4 %collective-permute-start = (bf16[32,128]{1,0:T(8,128)(2,1)S(1)}, bf16[32,128]{1,0:T(8,128)(2,1)S(1)}, u32[]{:S(2)}, u32[]{:S(2)}) collective-permute-start(bf16[32,128]{1,0:T(8,128)(2,1)S(1)} %get-tuple-element.25), channel_id=1, source_target_pairs={{0,1},{1,0},{2,3},{3,2},{4,5},{5,4},{6,7},{7,6},{8,9},{9,8},{10,11... | collective-permute-start | bytes 24584 | tf_op jit(solution)/shard_map/ppermute | solution.py:452
  22.8 3.2 %copy-start.2 = (bf16[16,64,384]{2,1,0:T(8,128)(2,1)S(1)}, bf16[16,64,384]{2,1,0:T(8,128)(2,1)}, u32[]{:S(2)}) copy-start(bf16[16,64,384]{2,1,0:T(8,128)(2,1)} %get-tuple-element.17.early_ref) | copy-start | bytes 2359300
  22.8 13.2 %collective-permute-start.1 = (bf16[32,128]{1,0:T(8,128)(2,1)S(1)}, bf16[32,128]{1,0:T(8,128)(2,1)S(1)}, u32[]{:S(2)}, u32[]{:S(2)}) collective-permute-start(bf16[32,128]{1,0:T(8,128)(2,1)S(1)} %get-tuple-element.26), channel_id=1, source_target_pairs={{1,2},{3,4},{5,6},{7,8},{9,10},{11,12},{13,14},{15,16},{17,18},{19... | collective-permute-start | bytes 24584 | tf_op jit(solution)/shard_map/ppermute | solution.py:454
  26.0 10.0 %copy-start.7 = (bf16[128,64,64]{0,2,1:T(8,128)(2,1)S(1)}, bf16[128,64,64]{0,2,1:T(8,128)(2,1)}, u32[]{:S(2)}) copy-start(bf16[128,64,64]{0,2,1:T(8,128)(2,1)} %param.15) | copy-start | bytes 3145732
  27.1 8.9 %copy-start = (bf16[16,64,128]{2,1,0:T(8,128)(2,1)S(1)}, bf16[16,64,128]{2,1,0:T(8,128)(2,1)}, u32[]{:S(2)}) copy-start(bf16[16,64,128]{2,1,0:T(8,128)(2,1)} %basis_hbm.3) | copy-start | bytes 786436
  27.1 8.9 %copy-start.11 = (s32[2,128]{1,0:T(2,128)S(1)}, s32[2,128]{1,0:T(2,128)}, u32[]{:S(2)}) copy-start(s32[2,128]{1,0:T(2,128)} %far_ref.1) | copy-start | bytes 3076
  27.1 13.9 %all-to-all-start.1 = ((f32[32,8,128]{2,1,0:T(8,128)}), f32[32,8,128]{2,1,0:T(8,128)S(1)}, u32[]{:S(2)}, u32[]{:S(2)}) async-start(f32[32,8,128]{2,1,0:T(8,128)} %get-tuple-element.19), calls=%async_computation.1 | async-start | bytes 262144 | tf_op jit(solution)/shard_map/all_to_all | solution.py:468
  36.0 0.7 %copy-start.10 = (s32[2,48]{1,0:T(2,128)S(1)}, s32[2,48]{1,0:T(2,128)}, u32[]{:S(2)}) copy-start(s32[2,48]{1,0:T(2,128)} %near_ref.1) | copy-start | bytes 1156
  36.7 4.4 %copy-start.1 = (bf16[16,64,64]{2,1,0:T(8,128)(2,1)S(1)}, bf16[16,64,64]{2,1,0:T(8,128)(2,1)}, u32[]{:S(2)}) copy-start(bf16[16,64,64]{2,1,0:T(8,128)(2,1)} %transfer_hbm.3) | copy-start | bytes 393220
  36.7 4.4 %copy-start.5 = (bf16[16,64,128]{2,1,0:T(8,128)(2,1)S(1)}, bf16[16,64,128]{2,1,0:T(8,128)(2,1)}, u32[]{:S(2)}) copy-start(bf16[16,64,128]{2,1,0:T(8,128)(2,1)} %get-tuple-element.20.early_ref) | copy-start | bytes 786436
